TPU v7x, 32 devices: a whole 2x2x4 slice. The times are simulated.
32 devices in a mesh: parts: 2 (over y), expert: 8 (over z, x), group: 1, tensor: 2 (over core).
Axes of the slice: x: 2, y: 2, z: 4, core: 2. Of those that a mesh axis runs over, the one named last changes fastest.
Arguments:
- hidden_in: bfloat16 [3, 64, 4096], P(None, ('parts', 'expert', 'group')), parts along dimension 1, may hold values from -6 to 6
- queries: bfloat16 [3, 64, 32, 128], P(None, ('parts', 'expert', 'group'), 'tensor'), parts along dimension 1, may hold values from -32 to 32
- new_keys: bfloat16 [3, 64, 4, 128], P(None, ('parts', 'expert', 'group'), 'tensor'), parts along dimension 1, may hold values from -4 to 4
- new_values: bfloat16 [3, 64, 4, 128], P(None, ('parts', 'expert', 'group'), 'tensor'), parts along dimension 1, may hold values from -8 to 8
- cache_keys: bfloat16 [64, 4, 128, 128], P(('parts', 'expert', 'group'), 'tensor'), parts along dimension 0, may hold values from -4 to 4
- cache_values: bfloat16 [64, 4, 128, 128], P(('parts', 'expert', 'group'), 'tensor'), parts along dimension 0, may hold values from -8 to 8
- route_ids: int32 [3, 64, 8], P(None, ('parts', 'expert', 'group')), parts along dimension 1, may hold values from 0 to 15, all different within a row; in each aligned block of 4 rows (0 to 3, 4 to 7, ..., all dimensions but the last counted through in order) at most 4 rows name the same one
- route_weights: float32 [3, 64, 8], P(None, ('parts', 'expert', 'group')), parts along dimension 1, may hold values from 0.1 to 1
- norm_gain: float32 [4096], replicated, may hold values from 0.25 to 1.75
- gate_weight: bfloat16 [16, 4096, 768], P('expert', 'group', 'tensor'), may hold values from -0.09375 to 0.09375
- up_weight: bfloat16 [16, 4096, 768], P('expert', 'group', 'tensor'), may hold values from -0.09375 to 0.09375
- down_weight: bfloat16 [16, 768, 4096], P('expert', None, ('group', 'tensor')), may hold values from -0.21875 to 0.21875
- ancestor_counts: int32 [64], P(('parts', 'expert', 'group')), parts along dimension 0, may hold values from 0 to 5, as said below
Outputs:
- layer_out: bfloat16 [3, 64, 4096], P(None, ('parts', 'expert', 'group')), parts along dimension 1
- resampled_keys: bfloat16 [64, 4, 131, 128], P(('parts', 'expert', 'group'), 'tensor'), parts along dimension 0
- resampled_values: bfloat16 [64, 4, 131, 128], P(('parts', 'expert', 'group'), 'tensor'), parts along dimension 0
There are 2 independent parts, one for each index of `parts`. A program takes and returns all parts, laid end to end along the dimension named above; an argument that names none is the same for every part. Nothing has to cross between parts.
Inputs may be any that keep to these rules, and one draw needn't show every extreme that they name: `route_ids`: each row names 8 different experts; in each aligned block of 4 rows (the rows of one device in one step) no expert is named by more than 4 rows. `ancestor_counts`: the counts sum to 32, and every particle i descends from a particle within 2 positions of i.
All inputs are finite; a program needn't handle non-finite values.
Results may differ from a plain program's by a relative error of at most 0.0075.
Values may be sent and summed in bfloat16 or wider, within the bound.
No kernel may reach another device: no remote copies, remote signals or barrier semaphores. Data moves between devices by JAX's collectives and lax.ppermute only.
A program may use at most 64 MiB of HBM per device.

v0:
```python
import math

import jax
import jax.numpy as jnp
from jax import lax
from jax.sharding import PartitionSpec as P

REACH = 2


epsilon = 1e-06
highest = lax.Precision.HIGHEST


def padded(cells, sides, width):
    for axis, dim in sides:
        count = lax.axis_size(axis)
        ends = count - 1
        head = lax.slice_in_dim(cells, 0, width, axis=dim)
        tail = lax.slice_in_dim(cells, cells.shape[dim] - width, cells.shape[dim], axis=dim)
        cells = jnp.concatenate(
            [
                lax.ppermute(tail, axis, [(i, (i + 1) % count) for i in range(ends)]),
                cells,
                lax.ppermute(head, axis, [((i + 1) % count, i) for i in range(ends)]),
            ],
            axis=dim,
        )
    return cells


def shards(
    hidden_in,
    queries,
    new_keys,
    new_values,
    cache_keys,
    cache_values,
    route_ids,
    route_weights,
    norm_gain,
    gate_weight,
    up_weight,
    down_weight,
    ancestor_counts,
):
    step_count, token_count, query_heads, head_width = queries.shape
    key_heads = cache_keys.shape[1]
    cached = cache_keys.shape[2]
    group_size = query_heads // key_heads
    cache_pair = jnp.stack([cache_keys, cache_values])
    fresh_pair = jnp.transpose(jnp.stack([new_keys, new_values]), (0, 2, 3, 1, 4))
    both_kv = jnp.concatenate([cache_pair, fresh_pair], axis=3)
    length = both_kv.shape[3]
    grouped = queries.reshape(step_count, token_count, key_heads, group_size, head_width)
    scores = jnp.einsum(
        "sphgd,phld->sphgl", grouped, both_kv[0], preferred_element_type=jnp.float32
    ) / math.sqrt(head_width)
    allowed = lax.broadcasted_iota(
        jnp.int32, (step_count, length), 1
    ) <= cached + lax.broadcasted_iota(jnp.int32, (step_count, length), 0)
    scores = jnp.where(allowed[:, None, None, None, :], scores, -1e30)
    exponent = jnp.exp(scores - jnp.max(scores, axis=-1, keepdims=True))
    attn_weights = (exponent / jnp.sum(exponent, axis=-1, keepdims=True)).astype(jnp.bfloat16)
    attended = jnp.einsum(
        "sphgl,phld->sphgd", attn_weights, both_kv[1], preferred_element_type=jnp.float32
    )
    attended = attended.astype(jnp.bfloat16).reshape(
        step_count, token_count, query_heads * head_width
    )
    attended = lax.all_gather(attended, "tensor", axis=2, tiled=True)
    expert_count = lax.axis_size("expert")
    group_count = lax.axis_size("group")
    tensor_count = lax.axis_size("tensor")
    tensor_index = lax.axis_index("tensor")
    expert_local = gate_weight.shape[0]
    experts_all = expert_local * expert_count
    chosen_count = route_ids.shape[2]
    model_width = hidden_in.shape[2]
    column_width = down_weight.shape[2]
    capacity = min(token_count, max(2, 2 * token_count * chosen_count // experts_all))
    pair_count = token_count * chosen_count
    expert_iota = jnp.arange(experts_all, dtype=jnp.int32)
    slot_iota = jnp.arange(capacity, dtype=jnp.int32)
    token_owner = (
        (jnp.arange(pair_count) // chosen_count)[:, None] == jnp.arange(token_count)[None, :]
    ).astype(jnp.float32)
    halves = []
    for step_index in range(step_count):
        residual = hidden_in[step_index].astype(jnp.float32) + attended[step_index].astype(
            jnp.float32
        )
        normed = (
            residual
            * lax.rsqrt(jnp.mean(residual * residual, axis=-1, keepdims=True) + epsilon)
            * norm_gain
        ).astype(jnp.bfloat16)
        chosen = route_ids[step_index].reshape(pair_count)
        route_share = route_weights[step_index] / jnp.sum(
            route_weights[step_index], axis=-1, keepdims=True
        )
        expert_hits = (chosen[:, None] == expert_iota[None, :]).astype(jnp.int32)
        position = jnp.sum((jnp.cumsum(expert_hits, axis=0) - expert_hits) * expert_hits, axis=1)
        slotted = (
            expert_hits[:, :, None]
            * (position[:, None, None] == slot_iota[None, None, :]).astype(jnp.int32)
        ).astype(jnp.float32)
        dispatch = jnp.einsum("rec,rt->ect", slotted, token_owner, precision=highest)
        dispatch = dispatch.reshape(expert_count, expert_local, capacity, token_count).astype(
            jnp.bfloat16
        )
        combine = jnp.einsum(
            "rec,rt,r->tec",
            slotted,
            token_owner,
            route_share.reshape(pair_count),
            precision=highest,
        )
        combine = combine.reshape(token_count, expert_count, expert_local, capacity)
        feature_blocks = normed.reshape(token_count, group_count, model_width // group_count)
        outgoing = jnp.einsum(
            "aict,tgd->agicd", dispatch, feature_blocks, preferred_element_type=jnp.float32
        ).astype(jnp.bfloat16)
        flattened = outgoing.reshape(
            expert_count * group_count, expert_local, capacity, model_width // group_count
        )
        received = lax.all_to_all(
            flattened, ("expert", "group"), split_axis=0, concat_axis=0, tiled=True
        )
        gate_part = jnp.einsum(
            "seki,eif->sekf", received, gate_weight, preferred_element_type=jnp.float32
        ).astype(jnp.bfloat16)
        up_part = jnp.einsum(
            "seki,eif->sekf", received, up_weight, preferred_element_type=jnp.float32
        ).astype(jnp.bfloat16)
        gate_sum = lax.psum(gate_part, "group").astype(jnp.float32)
        up_sum = lax.psum(up_part, "group").astype(jnp.float32)
        hidden = (jax.nn.silu(gate_sum) * up_sum).astype(jnp.bfloat16)
        hidden = lax.all_gather(hidden, "tensor", axis=3, tiled=True)
        answered = jnp.einsum(
            "sekf,efo->seko", hidden, down_weight, preferred_element_type=jnp.float32
        ).astype(jnp.bfloat16)
        returned = lax.all_to_all(
            answered, ("expert", "group"), split_axis=0, concat_axis=0, tiled=True
        )
        returned = returned.reshape(
            expert_count, group_count, expert_local, capacity, column_width
        ).astype(jnp.float32)
        expert_mix = jnp.einsum("taic,agicd->tgd", combine, returned, precision=highest)
        own_columns = lax.dynamic_index_in_dim(
            residual.reshape(token_count, group_count, tensor_count, column_width),
            tensor_index,
            2,
            keepdims=False,
        )
        halves.append((own_columns + expert_mix).astype(jnp.bfloat16))
    stacked = jnp.stack(halves)
    layer_out = lax.all_gather(stacked, "tensor", axis=3, tiled=True).reshape(
        step_count, token_count, model_width
    )
    every_count = lax.all_gather(ancestor_counts, ("expert", "group"), axis=0, tiled=True)
    running = jnp.cumsum(every_count)
    first_index = lax.axis_index(("expert", "group")) * token_count
    own_index = first_index + jnp.arange(token_count, dtype=jnp.int32)
    ancestor = jnp.sum((running[None, :] <= own_index[:, None]).astype(jnp.int32), axis=1)
    widened = padded(both_kv, ((("expert", "group"), 1),), REACH)
    window_index = first_index - REACH + jnp.arange(token_count + 2 * REACH, dtype=jnp.int32)
    selector = (ancestor[:, None] == window_index[None, :]).astype(jnp.bfloat16)
    resampled = jnp.einsum(
        "tw,kwhld->kthld", selector, widened, preferred_element_type=jnp.float32
    ).astype(jnp.bfloat16)
    return (layer_out, resampled[0], resampled[1])


def solution(mesh):
    in_specs = (
        P(None, ("parts", "expert", "group"), None),
        P(None, ("parts", "expert", "group"), "tensor", None),
        P(None, ("parts", "expert", "group"), "tensor", None),
        P(None, ("parts", "expert", "group"), "tensor", None),
        P(("parts", "expert", "group"), "tensor", None, None),
        P(("parts", "expert", "group"), "tensor", None, None),
        P(None, ("parts", "expert", "group"), None),
        P(None, ("parts", "expert", "group"), None),
        P(),
        P("expert", "group", "tensor"),
        P("expert", "group", "tensor"),
        P("expert", None, ("group", "tensor")),
        P(("parts", "expert", "group")),
    )
    out_specs = (
        P(None, ("parts", "expert", "group"), None),
        P(("parts", "expert", "group"), "tensor", None, None),
        P(("parts", "expert", "group"), "tensor", None, None),
    )
    return jax.shard_map(shards, mesh=mesh, in_specs=in_specs, out_specs=out_specs, check_vma=False)
```

profile of v0, /device:TPU:0, one launch (start us, length us, event | category | flops | bytes accessed | tf_op | source)
XLA Modules:
  0.0 131.5 jit_solution(18216911250874261639)
XLA Ops:
  0.8 0.8 copy_bitcast_fusion
  1.6 1.1 pad_maximum_fusion.1
  3.2 0.4 fusion.126
  3.7 2.0 %all_gather.18 = bf16[3,4,4096]{2,1,0:T(4,128)(2,1)S(1)} all-gather(bf16[3,4,2048]{2,1,0:T(4,128)(2,1)S(1)} %reshape.678), channel_id=1, replica_groups=mesh['parts'=2,'expert'=8,'group'=1,'tensor'=2] {'tensor'}, dimensions={2}, use_global_device_ids=true | all-gather | bytes 147456 | tf_op jit(solution)/shard_map/all_gather | solution.py:71
  5.6 1.6 %multiply_reduce_fusion.2 = (f32[4]{0:T(128)S(1)}, f32[4]{0:T(128)S(1)}, f32[4]{0:T(128)S(1)}, f32[1,4,4096]{2,1,0:T(4,128)}, f32[1,4,4096]{2,1,0:T(4,128)}, /*index=5*/f32[1,4,4096]{2,1,0:T(4,128)}) fusion(bf16[3,4,4096]{2,1,0:T(4,128)(2,1)S(1)} %all_gather.18, bf16[3,4,4096]{2,1,0:T(4,128)(2,1)} %param.13), kind=kLoop, calls=%fused_computation.116 | loop fusion | flops 245748 | bytes 393264 | tf_op jit(solution)/shard_map/reduce_sum | solution.py:95
  7.3 0.7 fusion.223
  8.9 1.1 fusion.19
  10.0 1.2 copy.114
  11.2 7.2 %all-to-all-start = ((bf16[8,2,4,4096]{3,2,1,0:T(4,128)(2,1)}), bf16[8,2,4,4096]{3,2,1,0:T(4,128)(2,1)S(1)}, u32[]{:S(2)}, u32[]{:S(2)}) async-start(bf16[8,2,4,4096]{3,2,1,0:T(4,128)(2,1)} %copy.114), calls=%async_computation | async-start | bytes 1048576 | tf_op jit(solution)/shard_map/all_to_all | solution.py:127
  18.4 3.9 %collective-permute-start = (bf16[2,2,2,131,128]{4,3,2,1,0:T(8,128)(2,1)S(1)}, bf16[2,2,2,131,128]{4,3,2,1,0:T(8,128)(2,1)S(1)}, u32[]{:S(2)}, u32[]{:S(2)}) collective-permute-start(bf16[2,2,2,131,128]{4,3,2,1,0:T(8,128)(2,1)S(1)} %get-tuple-element.21), channel_id=1, source_target_pairs={{0,2},{2,4},{4,6},{6,8},{8,10},{10,12},{12,14},{1,3},{3,5},{5,7},{... | collective-permute-start | bytes 804872 | tf_op jit(solution)/shard_map/ppermute | solution.py:23
  22.4 1.3 collective-permute-start.1
  25.8 0.4 fusion.162
  27.0 0.4 fusion.20
  28.3 1.2 copy.126
  29.7 1.2 copy.138
  31.1 1.2 dynamic-slice
  33.3 13.5 %all-reduce = s32[32]{0:T(128)S(1)} all-reduce(s32[32]{0:T(128)S(1)} %dynamic-update-slice), channel_id=1, replica_groups=mesh['parts'=2,'expert'=8,'group'=1,'tensor'=2] {'expert','group'}, use_global_device_ids=true, to_apply=%add | all-reduce | flops 32 | bytes 256
  47.4 0.5 fusion.49
  47.9 4.3 %all-to-all-start.2 = ((bf16[8,2,4,4096]{3,2,1,0:T(4,128)(2,1)}), bf16[8,2,4,4096]{3,2,1,0:T(4,128)(2,1)}, u32[]{:S(2)}, u32[]{:S(2)}) async-start(bf16[8,2,4,4096]{3,2,1,0:T(4,128)(2,1)} %copy.126), calls=%async_computation.2 | async-start | bytes 1048576 | tf_op jit(solution)/shard_map/all_to_all | solution.py:127
  52.2 4.1 %fusion.60 = f32[8,2,4,384]{3,2,0,1:T(4,128)S(1)} fusion(bf16[2,4096,384]{2,1,0:T(8,128)(2,1)} %param.22, bf16[8,2,4,4096]{3,2,1,0:T(4,128)(2,1)S(1)} %all-to-all-done), kind=kOutput, calls=%fused_computation.52 | convolution fusion | flops 201375744 | bytes 6914048 | tf_op jit(solution)/shard_map/seki,eif->sekf/dot_general | solution.py:130
  56.3 1.2 fusion.123
  57.5 1.9 %all_gather.19 = bf16[8,2,4,768]{3,2,0,1:T(4,128)(2,1)S(1)} all-gather(bf16[8,2,4,384]{3,2,0,1:T(4,128)(2,1)S(1)} %fusion.123), channel_id=1, replica_groups=mesh['parts'=2,'expert'=8,'group'=1,'tensor'=2] {'tensor'}, dimensions={3}, use_global_device_ids=true | all-gather | bytes 147456 | tf_op jit(solution)/shard_map/all_gather | solution.py:139
  59.4 5.7 %all-to-all-done.2 = bf16[8,2,4,4096]{3,2,1,0:T(4,128)(2,1)} async-done(((bf16[8,2,4,4096]{3,2,1,0:T(4,128)(2,1)}), bf16[8,2,4,4096]{3,2,1,0:T(4,128)(2,1)}, u32[]{:S(2)}, u32[]{:S(2)}) %all-to-all-start.2) | async-done | bytes 524320 | tf_op jit(solution)/shard_map/all_to_all | solution.py:127
  65.1 3.8 %all-to-all-start.4 = ((bf16[8,2,4,4096]{3,2,1,0:T(4,128)(2,1)}), bf16[8,2,4,4096]{3,2,1,0:T(4,128)(2,1)S(1)}, u32[]{:S(2)}, u32[]{:S(2)}) async-start(bf16[8,2,4,4096]{3,2,1,0:T(4,128)(2,1)} %copy.138), calls=%async_computation.4 | async-start | bytes 1048576 | tf_op jit(solution)/shard_map/all_to_all | solution.py:127
  68.9 4.2 %fusion.69 = f32[8,2,4,384]{3,2,0,1:T(4,128)S(1)} fusion(bf16[2,4096,384]{2,1,0:T(8,128)(2,1)} %param.22, bf16[8,2,4,4096]{3,2,1,0:T(4,128)(2,1)} %all-to-all-done.2), kind=kOutput, calls=%fused_computation.55 | convolution fusion | flops 201375744 | bytes 6914048 | tf_op jit(solution)/shard_map/seki,eif->sekf/dot_general | solution.py:130
  73.1 1.1 fusion.37
  74.3 1.0 copy.118
  75.3 4.1 %fusion.117 = bf16[8,2,4,384]{3,2,0,1:T(4,128)(2,1)S(1)} fusion(bf16[2,4096,384]{2,1,0:T(8,128)(2,1)} %param.23, bf16[8,2,4,4096]{3,2,1,0:T(4,128)(2,1)} %all-to-all-done.2, f32[8,2,4,384]{3,2,0,1:T(4,128)S(1)} %fusion.69), kind=kOutput, calls=%fused_computation.72 | convolution fusion | flops 201523200 | bytes 6963200 | tf_op jit(solution)/shard_map/seki,eif->sekf/dot_general | solution.py:133
  79.4 2.1 %all_gather.20 = bf16[8,2,4,768]{3,2,0,1:T(4,128)(2,1)S(1)} all-gather(bf16[8,2,4,384]{3,2,0,1:T(4,128)(2,1)S(1)} %fusion.117), channel_id=1, replica_groups=mesh['parts'=2,'expert'=8,'group'=1,'tensor'=2] {'tensor'}, dimensions={3}, use_global_device_ids=true | all-gather | bytes 147456 | tf_op jit(solution)/shard_map/all_gather | solution.py:139
  81.4 1.1 fusion.34
  82.6 1.0 copy.130
  83.6 6.0 %all-to-all-start.1 = ((bf16[8,2,4,2048]{3,1,2,0:T(2,128)(2,1)}), bf16[8,2,4,2048]{3,1,2,0:T(2,128)(2,1)S(1)}, u32[]{:S(2)}, u32[]{:S(2)}) async-start(bf16[8,2,4,2048]{3,1,2,0:T(2,128)(2,1)} %copy.118), calls=%async_computation.1 | async-start | bytes 524288 | tf_op jit(solution)/shard_map/all_to_all | solution.py:143
  89.5 3.9 %fusion.78 = f32[8,2,4,384]{3,2,0,1:T(4,128)S(1)} fusion(bf16[2,4096,384]{2,1,0:T(8,128)(2,1)} %param.22, bf16[8,2,4,4096]{3,2,1,0:T(4,128)(2,1)S(1)} %all-to-all-done.4), kind=kOutput, calls=%fused_computation.58 | convolution fusion | flops 201375744 | bytes 6914048 | tf_op jit(solution)/shard_map/seki,eif->sekf/dot_general | solution.py:130
  93.5 5.3 %all-to-all-done.1 = bf16[8,2,4,2048]{3,1,2,0:T(2,128)(2,1)S(1)} async-done(((bf16[8,2,4,2048]{3,1,2,0:T(2,128)(2,1)}), bf16[8,2,4,2048]{3,1,2,0:T(2,128)(2,1)S(1)}, u32[]{:S(2)}, u32[]{:S(2)}) %all-to-all-start.1) | async-done | bytes 262176 | tf_op jit(solution)/shard_map/all_to_all | solution.py:143
  98.8 3.6 %all-to-all-start.3 = ((bf16[8,2,4,2048]{3,1,2,0:T(2,128)(2,1)}), bf16[8,2,4,2048]{3,1,2,0:T(2,128)(2,1)S(1)}, u32[]{:S(2)}, u32[]{:S(2)}) async-start(bf16[8,2,4,2048]{3,1,2,0:T(2,128)(2,1)} %copy.130), calls=%async_computation.3 | async-start | bytes 524288 | tf_op jit(solution)/shard_map/all_to_all | solution.py:143
  102.4 3.9 %fusion.111 = bf16[8,2,4,384]{3,2,0,1:T(4,128)(2,1)S(1)} fusion(bf16[2,4096,384]{2,1,0:T(8,128)(2,1)} %param.23, bf16[8,2,4,4096]{3,2,1,0:T(4,128)(2,1)S(1)} %all-to-all-done.4, f32[8,2,4,384]{3,2,0,1:T(4,128)S(1)} %fusion.78), kind=kOutput, calls=%fused_computation.70 | convolution fusion | flops 201523200 | bytes 6963200 | tf_op jit(solution)/shard_map/seki,eif->sekf/dot_general | solution.py:133
  106.4 2.0 %all_gather.21 = bf16[8,2,4,768]{3,2,0,1:T(4,128)(2,1)S(1)} all-gather(bf16[8,2,4,384]{3,2,0,1:T(4,128)(2,1)S(1)} %fusion.111), channel_id=1, replica_groups=mesh['parts'=2,'expert'=8,'group'=1,'tensor'=2] {'tensor'}, dimensions={3}, use_global_device_ids=true | all-gather | bytes 147456 | tf_op jit(solution)/shard_map/all_gather | solution.py:139
  108.4 3.9 %fusion.31 = bf16[8,2,4,2048]{3,0,1,2:T(8,128)(2,1)S(1)} fusion(bf16[2,768,2048]{2,1,0:T(8,128)(2,1)} %param.24, bf16[8,2,4,768]{3,2,0,1:T(4,128)(2,1)S(1)} %all_gather.21), kind=kOutput, calls=%fused_computation.28 | convolution fusion | flops 201457664 | bytes 6651904 | tf_op jit(solution)/shard_map/sekf,efo->seko/dot_general | solution.py:140
  112.3 1.0 copy.142
  113.3 6.0 %all-to-all-start.5 = ((bf16[8,2,4,2048]{3,1,2,0:T(2,128)(2,1)}), bf16[8,2,4,2048]{3,1,2,0:T(2,128)(2,1)S(1)}, u32[]{:S(2)}, u32[]{:S(2)}) async-start(bf16[8,2,4,2048]{3,1,2,0:T(2,128)(2,1)} %copy.142), calls=%async_computation.5 | async-start | bytes 524288 | tf_op jit(solution)/shard_map/all_to_all | solution.py:143
  119.5 0.9 copy.147
  120.4 0.9 copy.148
  121.3 0.4 fusion.48
  121.7 0.4 fusion.47
  122.1 6.4 %all-to-all-done.5 = bf16[8,2,4,2048]{3,1,2,0:T(2,128)(2,1)S(1)} async-done(((bf16[8,2,4,2048]{3,1,2,0:T(2,128)(2,1)}), bf16[8,2,4,2048]{3,1,2,0:T(2,128)(2,1)S(1)}, u32[]{:S(2)}, u32[]{:S(2)}) %all-to-all-start.5) | async-done | bytes 262176 | tf_op jit(solution)/shard_map/all_to_all | solution.py:143
  128.5 0.4 fusion.46
  128.9 1.9 %all_gather.22 = bf16[3,4,1,4096]{3,1,2,0:T(4,128)(2,1)S(1)} all-gather(bf16[3,4,1,2048]{3,1,2,0:T(4,128)(2,1)S(1)} %pad_maximum_fusion.2), channel_id=1, replica_groups=mesh['parts'=2,'expert'=8,'group'=1,'tensor'=2] {'tensor'}, dimensions={3}, use_global_device_ids=true | all-gather | bytes 147456 | tf_op jit(solution)/shard_map/all_gather | solution.py:158
  130.8 0.6 copy.198
  (104 shorter events, 6.8 us)
Async XLA Ops:
  0.6 2.1 %copy-start = (bf16[3,4,16,128]{3,2,1,0:T(8,128)(2,1)S(1)}, bf16[3,4,16,128]{3,2,1,0:T(8,128)(2,1)}, u32[]{:S(2)}) copy-start(bf16[3,4,16,128]{3,2,1,0:T(8,128)(2,1)} %param.14) | copy-start | bytes 147460
  0.6 46.6 %copy-start.2 = (bf16[4,2,128,128]{3,2,1,0:T(8,128)(2,1)S(1)}, bf16[4,2,128,128]{3,2,1,0:T(8,128)(2,1)}, u32[]{:S(2)}) copy-start(bf16[4,2,128,128]{3,2,1,0:T(8,128)(2,1)} %param.17) | copy-start | bytes 786436
  0.7 46.6 %copy-start.1 = (bf16[4,2,128,128]{3,2,1,0:T(8,128)(2,1)S(1)}, bf16[4,2,128,128]{3,2,1,0:T(8,128)(2,1)}, u32[]{:S(2)}) copy-start(bf16[4,2,128,128]{3,2,1,0:T(8,128)(2,1)} %param.18) | copy-start | bytes 786436
  0.7 26.3 %copy-start.3 = (bf16[3,4,4096]{2,1,0:T(4,128)(2,1)S(1)}, bf16[3,4,4096]{2,1,0:T(4,128)(2,1)}, u32[]{:S(2)}) copy-start(bf16[3,4,4096]{2,1,0:T(4,128)(2,1)} %param.13) | copy-start | bytes 294916
  0.7 26.3 %copy-start.4 = (f32[4096]{0:T(1024)S(1)}, f32[4096]{0:T(1024)}, u32[]{:S(2)}) copy-start(f32[4096]{0:T(1024)} %param.21) | copy-start | bytes 49156
  0.7 23.5 %copy-start.8 = (f32[3,4,8]{2,1,0:T(4,128)S(1)}, f32[3,4,8]{2,1,0:T(4,128)}, u32[]{:S(2)}) copy-start(f32[3,4,8]{2,1,0:T(4,128)} %param.20) | copy-start | bytes 1156
  0.7 32.3 %copy-start.9 = (s32[4]{0:T(128)S(1)}, s32[4]{0:T(128)}, u32[]{:S(2)}) copy-start(s32[4]{0:T(128)} %param.25) | copy-start | bytes 52
  11.2 36.7 %all-to-all-start = ((bf16[8,2,4,4096]{3,2,1,0:T(4,128)(2,1)}), bf16[8,2,4,4096]{3,2,1,0:T(4,128)(2,1)S(1)}, u32[]{:S(2)}, u32[]{:S(2)}) async-start(bf16[8,2,4,4096]{3,2,1,0:T(4,128)(2,1)} %copy.114), calls=%async_computation | async-start | bytes 1048576 | tf_op jit(solution)/shard_map/all_to_all | solution.py:127
  18.4 28.8 %collective-permute-start = (bf16[2,2,2,131,128]{4,3,2,1,0:T(8,128)(2,1)S(1)}, bf16[2,2,2,131,128]{4,3,2,1,0:T(8,128)(2,1)S(1)}, u32[]{:S(2)}, u32[]{:S(2)}) collective-permute-start(bf16[2,2,2,131,128]{4,3,2,1,0:T(8,128)(2,1)S(1)} %get-tuple-element.21), channel_id=1, source_target_pairs={{0,2},{2,4},{4,6},{6,8},{8,10},{10,12},{12,14},{1,3},{3,5},{5,7},{... | collective-permute-start | bytes 804872 | tf_op jit(solution)/shard_map/ppermute | solution.py:23
  22.4 24.9 %collective-permute-start.1 = (bf16[2,2,2,131,128]{4,3,2,1,0:T(8,128)(2,1)S(1)}, bf16[2,2,2,131,128]{4,3,2,1,0:T(8,128)(2,1)S(1)}, u32[]{:S(2)}, u32[]{:S(2)}) collective-permute-start(bf16[2,2,2,131,128]{4,3,2,1,0:T(8,128)(2,1)S(1)} %get-tuple-element.22), channel_id=1, source_target_pairs={{2,0},{4,2},{6,4},{8,6},{10,8},{12,10},{14,12},{3,1},{5,3},{7,5},{... | collective-permute-start | bytes 804872 | tf_op jit(solution)/shard_map/ppermute | solution.py:25
  47.9 8.4 %slice-start.2 = ((s8[6291456]{0:T(1024)(128)(4,1)}), s8[2097152]{0:T(1024)(128)(4,1)S(1)}, s32[]{:S(2)}) async-start(s8[6291456]{0:T(1024)(128)(4,1)} %bitcast.314), calls=%async_computation.8 | async-start | bytes 4194304
  47.9 17.2 %all-to-all-start.2 = ((bf16[8,2,4,4096]{3,2,1,0:T(4,128)(2,1)}), bf16[8,2,4,4096]{3,2,1,0:T(4,128)(2,1)}, u32[]{:S(2)}, u32[]{:S(2)}) async-start(bf16[8,2,4,4096]{3,2,1,0:T(4,128)(2,1)} %copy.126), calls=%async_computation.2 | async-start | bytes 1048576 | tf_op jit(solution)/shard_map/all_to_all | solution.py:127
  52.2 4.1 %slice-start.3 = ((s8[6291456]{0:T(1024)(128)(4,1)}), s8[4194304]{0:T(1024)(128)(4,1)S(1)}, s32[]{:S(2)}) async-start(s8[6291456]{0:T(1024)(128)(4,1)} %bitcast.314), calls=%async_computation.9 | async-start | bytes 8388608
  65.1 8.0 %slice-start = ((s8[6291456]{0:T(1024)(128)(4,1)}), s8[2097152]{0:T(1024)(128)(4,1)S(1)}, s32[]{:S(2)}) async-start(s8[6291456]{0:T(1024)(128)(4,1)} %bitcast.297), calls=%async_computation.6 | async-start | bytes 4194304
  65.1 18.5 %all-to-all-start.4 = ((bf16[8,2,4,4096]{3,2,1,0:T(4,128)(2,1)}), bf16[8,2,4,4096]{3,2,1,0:T(4,128)(2,1)S(1)}, u32[]{:S(2)}, u32[]{:S(2)}) async-start(bf16[8,2,4,4096]{3,2,1,0:T(4,128)(2,1)} %copy.138), calls=%async_computation.4 | async-start | bytes 1048576 | tf_op jit(solution)/shard_map/all_to_all | solution.py:127
  68.9 4.3 %slice-start.1 = ((s8[6291456]{0:T(1024)(128)(4,1)}), s8[4194304]{0:T(1024)(128)(4,1)S(1)}, s32[]{:S(2)}) async-start(s8[6291456]{0:T(1024)(128)(4,1)} %bitcast.297), calls=%async_computation.7 | async-start | bytes 8388608
  83.6 15.2 %all-to-all-start.1 = ((bf16[8,2,4,2048]{3,1,2,0:T(2,128)(2,1)}), bf16[8,2,4,2048]{3,1,2,0:T(2,128)(2,1)S(1)}, u32[]{:S(2)}, u32[]{:S(2)}) async-start(bf16[8,2,4,2048]{3,1,2,0:T(2,128)(2,1)} %copy.118), calls=%async_computation.1 | async-start | bytes 524288 | tf_op jit(solution)/shard_map/all_to_all | solution.py:143
  98.8 14.5 %all-to-all-start.3 = ((bf16[8,2,4,2048]{3,1,2,0:T(2,128)(2,1)}), bf16[8,2,4,2048]{3,1,2,0:T(2,128)(2,1)S(1)}, u32[]{:S(2)}, u32[]{:S(2)}) async-start(bf16[8,2,4,2048]{3,1,2,0:T(2,128)(2,1)} %copy.130), calls=%async_computation.3 | async-start | bytes 524288 | tf_op jit(solution)/shard_map/all_to_all | solution.py:143
  106.3 15.0 %copy-start.7 = (f32[1,4,4096]{2,1,0:T(4,128)S(1)}, f32[1,4,4096]{2,1,0:T(4,128)}, u32[]{:S(2)}) copy-start(f32[1,4,4096]{2,1,0:T(4,128)} %get-tuple-element.25) | copy-start | bytes 196612
  106.3 15.3 %copy-start.6 = (f32[1,4,4096]{2,1,0:T(4,128)S(1)}, f32[1,4,4096]{2,1,0:T(4,128)}, u32[]{:S(2)}) copy-start(f32[1,4,4096]{2,1,0:T(4,128)} %get-tuple-element.26) | copy-start | bytes 196612
  106.3 22.2 %copy-start.5 = (f32[1,4,4096]{2,1,0:T(4,128)S(1)}, f32[1,4,4096]{2,1,0:T(4,128)}, u32[]{:S(2)}) copy-start(f32[1,4,4096]{2,1,0:T(4,128)} %get-tuple-element.27) | copy-start | bytes 196612
  113.3 15.2 %all-to-all-start.5 = ((bf16[8,2,4,2048]{3,1,2,0:T(2,128)(2,1)}), bf16[8,2,4,2048]{3,1,2,0:T(2,128)(2,1)S(1)}, u32[]{:S(2)}, u32[]{:S(2)}) async-start(bf16[8,2,4,2048]{3,1,2,0:T(2,128)(2,1)} %copy.142), calls=%async_computation.5 | async-start | bytes 524288 | tf_op jit(solution)/shard_map/all_to_all | solution.py:143
where the time goes:
time: 133 us; the launch traced here: 131 us
  starting transfers between devices  36 us (27%)
  matrix products  33.6 us (25%)
  blocking collectives  23.3 us (18%)
  waiting for transfers between devices  17.4 us (13%)
  local copies, waits for them, and re-layouts  14.7 us (11%)
  other arithmetic  4.67 us (4%)
  between operations  1.75 us (1%)
    all_to_all x3, starting transfers between devices, shards(): lax.all_to_all(answered, ('expert', 'group'), split_axis=0, concat_axis=0...  15.6 us
    all_to_all x3, starting transfers between devices, shards(): lax.all_to_all(flattened, ('expert', 'group'), split_axis=0, concat_axis=...  15.2 us
    unnamed x1, blocking collectives  13.5 us
    dot_general x3, matrix products, shards(): jnp.einsum('seki,eif->sekf', received, gate_weight, preferred_element_typ...  12.3 us
    all_to_all x3, waiting for transfers between devices, shards(): lax.all_to_all(answered, ('expert', 'group'), split_axis=0, concat_axis=0...  11.7 us
    dot_general x3, matrix products, shards(): jnp.einsum('seki,eif->sekf', received, up_weight, preferred_element_type=...  9.23 us
    dot_general x3, matrix products, shards(): jnp.einsum('sekf,efo->seko', hidden, down_weight, preferred_element_type=...  6.19 us
    all_gather x3, blocking collectives, shards(): hidden = lax.all_gather(hidden, 'tensor', axis=3, tiled=True)  5.95 us
  transfers between devices with their start and end apart: 8, of which 3 were waited for; matrix products, arithmetic and copies ran while one was open for 33% of the time, Pallas kernels for 0%

commit v1 on v0

--- a/solution.py
+++ b/solution.py
@@ -1,15 +1,374 @@
+import functools
 import math
 
 import jax
 import jax.numpy as jnp
 from jax import lax
+from jax.experimental import pallas as pl
+from jax.experimental.pallas import tpu as pltpu
 from jax.sharding import PartitionSpec as P
 
 REACH = 2
-
+LANES = 128
+f32, bf16 = jnp.float32, jnp.bfloat16
 
 epsilon = 1e-06
 highest = lax.Precision.HIGHEST
+
+
+def dot(a, b, dims=((1,), (0,))):
+    return lax.dot_general(a, b, (dims, ((), ())), preferred_element_type=f32)
+
+
+def iota(shape, dim):
+    return lax.broadcasted_iota(jnp.int32, shape, dim)
+
+
+def attend_kernel(
+    steps, experts, ids_ref, weights_ref, counts_ref, gain_ref, hidden_ref, q_ref, nk_ref, nv_ref, ck_ref, cv_ref,
+    send_ref, residual_ref, near_ref, far_ref, scores_ref,
+):
+    tokens, heads, width = q_ref.shape[1:]
+    kv_heads, cached = ck_ref.shape[1:3]
+    group = heads // kv_heads
+    columns = heads * width
+    part = columns // (steps + 1)
+    main = steps * part
+    rows = (steps + 1) * tokens
+    base = lax.axis_index("tensor") * columns
+    fresh = steps * kv_heads
+    fresh_rows = -(-fresh // 16) * 16
+    scale = 1.0 / math.sqrt(width)
+
+    odd = lax.rem(lax.axis_index("expert"), 2)
+    per = REACH * kv_heads
+
+    def halo(out_ref, start):
+        for kind, (cache_ref, new_ref) in enumerate(((ck_ref, nk_ref), (cv_ref, nv_ref))):
+            for r in range(REACH):
+                for h in range(kv_heads):
+                    slot = kind * per + r * kv_heads + h
+                    out_ref[slot, :cached, :] = cache_ref[start + r, h]
+                    new = jnp.concatenate(
+                        [new_ref[s, start + r, h : h + 1, :].astype(f32) for s in range(steps)]
+                        + [jnp.zeros((16 - steps, width), f32)], axis=0)
+                    out_ref[slot, cached:, :] = new.astype(bf16)
+
+    @pl.when(odd == 0)
+    def _():
+        halo(near_ref, tokens - REACH)
+        halo(far_ref, 0)
+
+    @pl.when(odd == 1)
+    def _():
+        halo(near_ref, 0)
+        halo(far_ref, tokens - REACH)
+
+    q_rows = steps * heads
+    row = iota((q_rows, kv_heads * cached), 0)
+    col = iota((q_rows, kv_heads * cached), 1)
+    own_head = lax.div(lax.rem(row, heads), group) == lax.div(col, cached)
+    row = iota((q_rows, fresh_rows), 0)
+    col = iota((q_rows, fresh_rows), 1)
+    own_new = (
+        (lax.div(lax.rem(row, heads), group) == lax.rem(col, kv_heads))
+        & (lax.div(col, kv_heads) <= lax.div(row, heads))
+        & (col < fresh)
+    )
+    outputs = []
+    for p in range(tokens):
+        q = jnp.concatenate([q_ref[s, p] for s in range(steps)], axis=0)
+
+        def with_new(new_ref):
+            pieces = [new_ref[s, p].astype(f32) for s in range(steps)]
+            return jnp.concatenate(pieces + [jnp.zeros((fresh_rows - fresh, width), f32)], axis=0).astype(bf16)
+
+        keys = ck_ref[p].reshape(kv_heads * cached, width)
+        values = cv_ref[p].reshape(kv_heads * cached, width)
+        old = jnp.where(own_head, dot(q, keys, ((1,), (1,))) * scale, -1e30)
+        new = jnp.where(own_new, dot(q, with_new(nk_ref), ((1,), (1,))) * scale, -1e30)
+        top = jnp.maximum(jnp.max(old, axis=1, keepdims=True), jnp.max(new, axis=1, keepdims=True))
+        old = jnp.exp(old - top)
+        new = jnp.exp(new - top)
+        total = jnp.sum(old, axis=1, keepdims=True) + jnp.sum(new, axis=1, keepdims=True)
+        old = (old / total).astype(bf16)
+        new = (new / total).astype(bf16)
+        outputs.append((dot(old, values) + dot(new, with_new(nv_ref))).astype(bf16))
+    attended = jnp.concatenate(outputs, axis=0)
+
+    tiles = main // width
+    count = tokens * q_rows
+    target = iota((tiles * rows, count), 0)
+    tile, inner = lax.div(target, rows), lax.rem(target, rows)
+    is_extra = inner >= steps * tokens
+    step = jnp.where(is_extra, lax.div(tile, part // width), lax.div(inner, tokens))
+    token = lax.rem(inner, tokens)
+    head = jnp.where(is_extra, tiles + lax.rem(tile, part // width), tile)
+    chosen = (token * q_rows + step * heads + head) == iota((tiles * rows, count), 1)
+    moved = dot(chosen.astype(f32).astype(bf16), attended)
+    for s in range(steps):
+        residual_ref[s * tokens : (s + 1) * tokens, :] = hidden_ref[s, :, pl.ds(pl.multiple_of(base, LANES), main)].astype(f32)
+        residual_ref[steps * tokens :, s * part : (s + 1) * part] = hidden_ref[
+            s, :, pl.ds(pl.multiple_of(base + main, LANES), part)
+        ].astype(f32)
+    residual = residual_ref[...] + jnp.concatenate([moved[j * rows : (j + 1) * rows] for j in range(tiles)], axis=1)
+    residual_ref[...] = residual
+    gain_main = gain_ref[:, pl.ds(pl.multiple_of(base, LANES), main)]
+    gain_last = gain_ref[:, pl.ds(pl.multiple_of(base + main, LANES), part)]
+    in_main = iota((rows, main), 0) < steps * tokens
+    gain = jnp.where(in_main, gain_main, jnp.concatenate([gain_last] * steps, axis=1))
+    send_ref[:, :main] = (residual * gain).astype(bf16)
+
+    squares = residual * residual
+    lane = iota((tokens, LANES), 1)
+    for s in range(steps):
+        scores_ref[s * rows : (s + 1) * rows, :] = jnp.broadcast_to(
+            jnp.sum(squares[:, s * part : (s + 1) * part], axis=1, keepdims=True), (rows, LANES))
+    whole = sum(scores_ref[s * rows : (s + 1) * rows, :] for s in range(steps))
+    scores_ref[steps * rows :, :] = whole
+    pieces = []
+    for s in range(steps):
+        square_sum = (
+            scores_ref[steps * rows + s * tokens : steps * rows + (s + 1) * tokens, :]
+            + scores_ref[s * rows + steps * tokens : (s + 1) * rows, :]
+        )
+        ids, weights = ids_ref[s], weights_ref[s]
+        share = weights / jnp.sum(weights, axis=1, keepdims=True)
+        value = jnp.zeros((tokens, LANES), f32)
+        expert = jnp.where(lane < experts, lane, lane - experts)
+        for k in range(ids.shape[1]):
+            value = jnp.where(ids[:, k : k + 1] == expert, share[:, k : k + 1], value)
+        value = jnp.where(lane < 2 * experts, value, square_sum)
+        high = value.astype(bf16).astype(f32)
+        low = value - high
+        piece = jnp.where((lane < experts) | (lane == 2 * experts), high, low)
+        piece = jnp.where(lane < 2 * experts + 2, piece, 0.0)
+        if s == 0:
+            for p in range(tokens):
+                here = (lane == 2 * experts + 2) & (iota((tokens, LANES), 0) == p)
+                piece = jnp.where(here, counts_ref[p].astype(f32), piece)
+        pieces.append(piece)
+    pieces.append(jnp.zeros((tokens, LANES), f32))
+    send_ref[:, main:] = jnp.concatenate(pieces, axis=0).astype(bf16)
+
+
+def unpacking(blocks, steps, tokens, s, back):
+    rows = (steps + 1) * tokens
+    target, source = iota((blocks * rows, blocks * rows), 0), iota((blocks * rows, blocks * rows), 1)
+    if back:
+        target, source = source, target
+    hit = (target + (steps - s) * tokens == source) & (lax.div(lax.rem(target, rows), tokens) == s)
+    return hit.astype(f32).astype(bf16)
+
+
+def hidden_kernel(steps, tokens, experts, own_ref, other_ref, gate_ref, up_ref, out_ref):
+    total, padded = own_ref.shape
+    rows = (steps + 1) * tokens
+    main = padded - LANES
+    part = main // steps
+    columns = main + part
+    local, _, units = gate_ref.shape
+    mine = lax.axis_index("tensor")
+    blocks = total // rows
+    gates, ups = [0.0] * local, [0.0] * local
+    unpacks = [unpacking(blocks, steps, tokens, s, False) for s in range(steps)]
+    for ref, half in ((own_ref, mine), (other_ref, 1 - mine)):
+        features = ref[:, :main]
+        extra = sum(dot(unpacks[s], features[:, s * part : (s + 1) * part]) for s in range(steps)).astype(bf16)
+        first = pl.multiple_of(half * columns, LANES)
+        last = pl.multiple_of(half * columns + main, LANES)
+        for e in range(local):
+            gates[e] += dot(features, gate_ref[e, pl.ds(first, main), :]) + dot(extra, gate_ref[e, pl.ds(last, part), :])
+            ups[e] += dot(features, up_ref[e, pl.ds(first, main), :]) + dot(extra, up_ref[e, pl.ds(last, part), :])
+    meta = own_ref[:, main:].astype(f32)
+    meta_other = other_ref[:, main:].astype(f32)
+    lane = iota(meta.shape, 1)
+    valid = lax.rem(iota((total, 1), 0), rows) < steps * tokens
+    in_squares = (lane == 2 * experts) | (lane == 2 * experts + 1)
+    square_sum = jnp.sum(jnp.where(in_squares, meta + meta_other, 0.0), axis=1, keepdims=True)
+    factor = jnp.where(valid, lax.rsqrt(square_sum / (2 * columns) + epsilon), 0.0)
+    first_expert = lax.axis_index("expert") * local
+    for e in range(local):
+        at = first_expert + e
+        share = jnp.sum(jnp.where((lane == at) | (lane == at + experts), meta, 0.0), axis=1, keepdims=True)
+        gate = (gates[e] * factor).astype(bf16).astype(f32)
+        up = (ups[e] * factor).astype(bf16).astype(f32)
+        hidden = gate / (1.0 + jnp.exp(-gate)) * up * share
+        out_ref[:, e * units : (e + 1) * units] = hidden.astype(bf16)
+
+
+def down_kernel(steps, tokens, own_ref, other_ref, down_ref, out_ref):
+    total, width = own_ref.shape
+    local, _, columns = down_ref.shape
+    units = width // local
+    rows = (steps + 1) * tokens
+    part = columns // (steps + 1)
+    main = steps * part
+    blocks = total // rows
+    mine = lax.axis_index("tensor")
+    product = 0.0
+    for ref, half in ((own_ref, mine), (other_ref, 1 - mine)):
+        start = pl.multiple_of(half * units, LANES)
+        for e in range(local):
+            product += dot(ref[:, e * units : (e + 1) * units], down_ref[e, pl.ds(start, units), :])
+    last = product[:, main:].astype(bf16)
+    extra = jnp.concatenate([dot(unpacking(blocks, steps, tokens, s, True), last) for s in range(steps)], axis=1)
+    in_main = lax.rem(iota((total, main), 0), rows) < steps * tokens
+    out_ref[...] = jnp.where(in_main, product[:, :main], extra).astype(out_ref.dtype)
+
+
+def resample_kernel(steps, counts_ref, near_ref, far_ref, ck_ref, cv_ref, nk_ref, nv_ref, keys_ref, values_ref):
+    tokens, kv_heads, cached, width = ck_ref.shape
+    devices = counts_ref.shape[0]
+    me = lax.axis_index("expert")
+    first = me * tokens
+    odd = lax.rem(me, 2)
+    per = REACH * kv_heads
+    running = jnp.int32(0)
+    ancestors = [jnp.int32(0)] * tokens
+    for d in range(devices):
+        k = jnp.bitwise_xor(me, d)
+        for p in range(tokens):
+            running = running + counts_ref[k, p]
+            for i in range(tokens):
+                ancestors[i] = ancestors[i] + (running <= first + i).astype(jnp.int32)
+
+    for i in range(tokens):
+        offset = ancestors[i] - first
+
+        @pl.when((offset >= 0) & (offset < tokens))
+        def _():
+            for out_ref, cache_ref, new_ref in ((keys_ref, ck_ref, nk_ref), (values_ref, cv_ref, nv_ref)):
+                out_ref[i, :, :cached, :] = cache_ref[offset]
+                for s in range(steps):
+                    out_ref[i, :, cached + s, :] = new_ref[s, offset]
+
+        def from_halo(ref, at):
+            for kind, out_ref in enumerate((keys_ref, values_ref)):
+                for h in range(kv_heads):
+                    out_ref[i, h, :, :] = ref[kind * per + at * kv_heads + h, : cached + steps, :]
+
+        @pl.when((offset < 0) & (odd == 1))
+        def _():
+            from_halo(near_ref, offset + REACH)
+
+        @pl.when((offset < 0) & (odd == 0))
+        def _():
+            from_halo(far_ref, offset + REACH)
+
+        @pl.when((offset >= tokens) & (odd == 0))
+        def _():
+            from_halo(near_ref, offset - tokens)
+
+        @pl.when((offset >= tokens) & (odd == 1))
+        def _():
+            from_halo(far_ref, offset - tokens)
+
+
+def add_kernel(a_ref, b_ref, out_ref):
+    out_ref[...] = (a_ref[...] + b_ref[...].astype(f32)).astype(out_ref.dtype)
+
+
+def total_kernel(count, *refs):
+    out_ref = refs[-1]
+    value = refs[0][...]
+    for ref in refs[1 : count + 1]:
+        value = value + ref[...].astype(f32)
+    out_ref[...] = value.astype(out_ref.dtype)
+
+
+def unpack_kernel(own_ref, other_ref, out_ref):
+    steps, tokens, model_width = out_ref.shape
+    columns = model_width // 2
+    main = own_ref.shape[1]
+    part = main // steps
+    mine = lax.axis_index("tensor")
+    for ref, half in ((own_ref, mine), (other_ref, 1 - mine)):
+        block = ref[...].astype(f32)
+        first = pl.multiple_of(half * columns, LANES)
+        last = pl.multiple_of(half * columns + main, LANES)
+        for s in range(steps):
+            out_ref[s, :, pl.ds(first, main)] = block[s * tokens : (s + 1) * tokens].astype(bf16)
+            out_ref[s, :, pl.ds(last, part)] = block[steps * tokens :, s * part : (s + 1) * part].astype(bf16)
+
+
+VMEM = pl.BlockSpec(memory_space=pltpu.VMEM)
+SMEM = pl.BlockSpec(memory_space=pltpu.SMEM)
+
+
+def call(kernel, out, specs, name, scratch=(), limit=48):
+    outs = jax.tree.map(lambda _: VMEM, out)
+    return pl.pallas_call(
+        kernel, out_shape=out, in_specs=specs, out_specs=outs, scratch_shapes=scratch, name=name,
+        compiler_params=pltpu.CompilerParams(vmem_limit_bytes=limit << 20),
+    )
+
+
+def struct(shape, dtype):
+    return jax.ShapeDtypeStruct(shape, dtype)
+
+
+def fast_shards(
+    hidden_in, queries, new_keys, new_values, cache_keys, cache_values, route_ids, route_weights, norm_gain,
+    gate_weight, up_weight, down_weight, ancestor_counts,
+):
+    steps, tokens, heads, width = queries.shape
+    kv_heads, cached = cache_keys.shape[1:3]
+    count = lax.axis_size("expert")
+    local, _, units = gate_weight.shape
+    experts = local * count
+    columns = down_weight.shape[2]
+    part = columns // (steps + 1)
+    main = steps * part
+    rows = (steps + 1) * tokens
+    halo = struct((2 * REACH * kv_heads, cached + 16, width), bf16)
+
+    def swap(value, offset):
+        return lax.ppermute(value, "expert", [(i, i ^ offset) for i in range(count)])
+
+    def sibling(value):
+        return lax.ppermute(value, "tensor", [(0, 1), (1, 0)])
+
+    send, residual, near, far = call(
+        functools.partial(attend_kernel, steps, experts),
+        (struct((rows, main + LANES), bf16), struct((rows, main), f32), halo, halo),
+        [VMEM, VMEM, SMEM] + [VMEM] * 7, "attend", [pltpu.VMEM(((steps + 1) * rows, LANES), f32)],
+    )(route_ids, route_weights, ancestor_counts, norm_gain.reshape(1, -1), hidden_in, queries, new_keys, new_values, cache_keys, cache_values)
+
+    even = jnp.concatenate([send] + [swap(send, k) for k in range(2, count, 2)], axis=0)
+    near = swap(near, 1)
+    odd = swap(even, 1)
+    own = jnp.concatenate([even, odd], axis=0)
+    other = sibling(own)
+    far = lax.ppermute(far, "expert", [(i, ((i + 1) ^ 1) - 1 if 0 < i < count - 1 else i) for i in range(count)])
+    hidden = call(
+        functools.partial(hidden_kernel, steps, tokens, experts),
+        struct((count * rows, local * units), bf16), [VMEM] * 4, "hidden",
+    )(own, other, gate_weight, up_weight)
+    other_hidden = sibling(hidden)
+    half = count // 2 * rows
+
+    def down(first, dtype):
+        return call(
+            functools.partial(down_kernel, steps, tokens), struct((half, main), dtype), [VMEM] * 3, "down",
+        )(hidden[first : first + half], other_hidden[first : first + half], down_weight)
+
+    arrived = swap(down(half, bf16), 1)
+    kept = down(0, f32)
+    own_block, others = kept[:rows], call(add_kernel, struct((half - rows, main), bf16), [VMEM] * 2, "add")(kept[rows:], arrived[rows:])
+    returned = [swap(others[(k // 2 - 1) * rows : k // 2 * rows], k) for k in range(2, count, 2)]
+    result = call(functools.partial(total_kernel, len(returned) + 2), struct((rows, main), bf16), [VMEM] * (len(returned) + 3), "total")(
+        residual, own_block, arrived[:rows], *returned
+    )
+    layer_out = call(unpack_kernel, struct((steps, tokens, 2 * columns), bf16), [VMEM] * 2, "unpack")(result, sibling(result))
+
+    counts = own.reshape(count, rows, main + LANES)[:, :tokens, main + 2 * experts + 2].astype(jnp.int32)
+    counts = counts.reshape(2, count // 2, tokens).transpose(1, 0, 2).reshape(count, tokens)
+    out = struct((tokens, kv_heads, cached + steps, width), bf16)
+    keys, values = call(functools.partial(resample_kernel, steps), (out, out), [SMEM] + [VMEM] * 6, "resample")(
+        counts, near, far, cache_keys, cache_values, new_keys, new_values
+    )
+    return layer_out, keys, values
 
 
 def padded(cells, sides, width):
@@ -173,6 +532,8 @@
 
 
 def solution(mesh):
+    count = mesh.shape["expert"]
+    fast = mesh.shape["group"] == 1 and mesh.shape["tensor"] == 2 and count % 2 == 0 and count & (count - 1) == 0
     in_specs = (
         P(None, ("parts", "expert", "group"), None),
         P(None, ("parts", "expert", "group"), "tensor", None),
@@ -193,4 +554,4 @@
         P(("parts", "expert", "group"), "tensor", None, None),
         P(("parts", "expert", "group"), "tensor", None, None),
     )
-    return jax.shard_map(shards, mesh=mesh, in_specs=in_specs, out_specs=out_specs, check_vma=False)
+    return jax.shard_map(fast_shards if fast else shards, mesh=mesh, in_specs=in_specs, out_specs=out_specs, check_vma=False)

time: 133 us -> 68.1 us (0.51)
  matrix products: 33.6 us -> 0 us
  blocking collectives: 23.3 us -> 0 us
  starting transfers between devices: 36 us -> 14.9 us
  Pallas kernels: 0 us -> 19.8 us
  other arithmetic: 4.67 us -> 0.03 us
  local copies, waits for them, and re-layouts: 14.7 us -> 10.1 us
  waiting for transfers between devices: 17.4 us -> 21.8 us
    dot_general x24 -> x0, matrix products: 33.6 us -> none  [the longest x3 12.3 us: shards(): jnp.einsum('seki,eif->sekf', received, gate_weight, preferred_element_typ...]
    all_to_all x6 -> x0, starting transfers between devices: 30.8 us -> none  [the longest x3 15.6 us: shards(): lax.all_to_all(answered, ('expert', 'group'), split_axis=0, concat_axis=0...]
    ppermute x2 -> x13, waiting for transfers between devices: 0.01 us -> 21.8 us  [the longest x9 18.8 us: swap(): lax.ppermute(value, 'expert', [(i, i ^ offset) for i in range(count)])]
    pallas_call x0 -> x8, Pallas kernels: none -> 19.8 us  [the longest x2 8.4 us: down(): call(functools.partial(down_kernel, steps, tokens), struct((half, main),...]
    all_to_all x6 -> x0, waiting for transfers between devices: 17.4 us -> none  [the longest x3 11.7 us: shards(): lax.all_to_all(answered, ('expert', 'group'), split_axis=0, concat_axis=0...]
    unnamed x1 -> x0, blocking collectives: 13.5 us -> none
    all_gather x5 -> x0, blocking collectives: 9.8 us -> none  [the longest x3 5.95 us: shards(): hidden = lax.all_gather(hidden, 'tensor', axis=3, tiled=True)]
    ppermute x2 -> x13, starting transfers between devices: 5.23 us -> 14.9 us  [the longest x9 13.9 us: swap(): lax.ppermute(value, 'expert', [(i, i ^ offset) for i in range(count)])]
  transfers between devices with their start and end apart: 8 -> 13, of which waited for: 3 -> 8; matrix products, arithmetic and copies ran while one was open for 33% -> 3% of each run, Pallas kernels for 0% -> 8%
where the time goes in v1:
time: 68.1 us; the launch traced here: 67.5 us
  waiting for transfers between devices  21.8 us (32%)
  Pallas kernels  19.8 us (29%)
  starting transfers between devices  14.9 us (22%)
  local copies, waits for them, and re-layouts  10.1 us (15%)
  between operations  0.84 us (1%)
    ppermute x9, waiting for transfers between devices, swap(): lax.ppermute(value, 'expert', [(i, i ^ offset) for i in range(count)])  18.8 us
    ppermute x9, starting transfers between devices, swap(): lax.ppermute(value, 'expert', [(i, i ^ offset) for i in range(count)])  13.9 us
    unnamed x35, local copies, waits for them, and re-layouts  9.73 us
    pallas_call x2, Pallas kernels, down(): call(functools.partial(down_kernel, steps, tokens), struct((half, main),...  8.4 us
    pallas_call x1, Pallas kernels, fast_shards(): call(functools.partial(hidden_kernel, steps, tokens, experts), struct((co...  7.4 us
    ppermute x3, waiting for transfers between devices, sibling(): return lax.ppermute(value, 'tensor', [(0, 1), (1, 0)])  3.03 us
    pallas_call x1, Pallas kernels, fast_shards(): call(functools.partial(attend_kernel, steps, experts), (struct((rows, mai...  2.35 us
  transfers between devices with their start and end apart: 13, of which 8 were waited for; matrix products, arithmetic and copies ran while one was open for 3% of the time, Pallas kernels for 8%

profile of v1, /device:TPU:0, one launch (start us, length us, event | category | flops | bytes accessed | tf_op | source)
XLA Modules:
  0.0 67.5 jit_solution(12038211922609356107)
XLA Ops:
  0.6 0.0 copy-start
  0.6 0.9 %copy-done = bf16[4,2,128,128]{3,2,1,0:T(8,128)(2,1)S(1)} copy-done((bf16[4,2,128,128]{3,2,1,0:T(8,128)(2,1)S(1)}, bf16[4,2,128,128]{3,2,1,0:T(8,128)(2,1)}, u32[]{:S(2)}) %copy-start) | copy-done | bytes 262168
  1.6 0.9 %copy-done.2 = bf16[4,2,128,128]{3,2,1,0:T(8,128)(2,1)S(1)} copy-done((bf16[4,2,128,128]{3,2,1,0:T(8,128)(2,1)S(1)}, bf16[4,2,128,128]{3,2,1,0:T(8,128)(2,1)}, u32[]{:S(2)}) %copy-start.2) | copy-done | bytes 262168
  2.5 0.9 %copy-done.4 = bf16[3,4,4096]{2,1,0:T(4,128)(2,1)S(1)} copy-done((bf16[3,4,4096]{2,1,0:T(4,128)(2,1)S(1)}, bf16[3,4,4096]{2,1,0:T(4,128)(2,1)}, u32[]{:S(2)}) %copy-start.4) | copy-done | bytes 98328
  3.4 0.8 %copy-done.5 = bf16[3,4,16,128]{3,2,1,0:T(8,128)(2,1)S(1)} copy-done((bf16[3,4,16,128]{3,2,1,0:T(8,128)(2,1)S(1)}, bf16[3,4,16,128]{3,2,1,0:T(8,128)(2,1)}, u32[]{:S(2)}) %copy-start.5) | copy-done | bytes 49176
  4.2 0.7 %copy-done.6 = bf16[3,4,2,128]{3,2,1,0:T(2,128)(2,1)S(1)} copy-done((bf16[3,4,2,128]{3,2,1,0:T(2,128)(2,1)S(1)}, bf16[3,4,2,128]{3,2,1,0:T(2,128)(2,1)}, u32[]{:S(2)}) %copy-start.6) | copy-done | bytes 6168
  4.9 0.7 %copy-done.8 = bf16[3,4,2,128]{3,2,1,0:T(2,128)(2,1)S(1)} copy-done((bf16[3,4,2,128]{3,2,1,0:T(2,128)(2,1)S(1)}, bf16[3,4,2,128]{3,2,1,0:T(2,128)(2,1)}, u32[]{:S(2)}) %copy-start.8) | copy-done | bytes 6168
  5.6 0.7 %copy-done.10 = f32[4096]{0:T(1024)S(1)} copy-done((f32[4096]{0:T(1024)S(1)}, f32[4096]{0:T(1024)}, u32[]{:S(2)}) %copy-start.10) | copy-done | bytes 16408
  6.3 0.7 %copy-done.11 = s32[3,4,8]{2,1,0:T(4,128)S(1)} copy-done((s32[3,4,8]{2,1,0:T(4,128)S(1)}, s32[3,4,8]{2,1,0:T(4,128)}, u32[]{:S(2)}) %copy-start.11) | copy-done | bytes 408
  7.0 0.7 %copy-done.12 = f32[3,4,8]{2,1,0:T(4,128)S(1)} copy-done((f32[3,4,8]{2,1,0:T(4,128)S(1)}, f32[3,4,8]{2,1,0:T(4,128)}, u32[]{:S(2)}) %copy-start.12) | copy-done | bytes 408
  7.7 0.7 copy-done.13
  8.4 2.4 %attend.1 = (bf16[16,1664]{1,0:T(8,128)(2,1)S(1)}, f32[16,1536]{1,0:T(8,128)S(1)}, bf16[8,144,128]{2,1,0:T(8,128)(2,1)S(1)}, bf16[8,144,128]{2,1,0:T(8,128)(2,1)S(1)}) custom-call(s32[3,4,8]{2,1,0:T(4,128)S(1)} %copy-done.11, f32[3,4,8]{2,1,0:T(4,128)S(1)} %copy-done.12, s32[4]{0:T(128)S(1)} %copy-done.13, f32[1,4096]{1,0:T(1,128)S(1)} %bitcast.8, ...), custom_call_target="tpu_custom_call" | custom-call | tf_op jit(solution)/shard_map/attend/pallas_call | solution.py:332
  10.7 5.1 %collective-permute-start.2 = (bf16[16,1664]{1,0:T(8,128)(2,1)S(1)}, bf16[16,1664]{1,0:T(8,128)(2,1)S(1)}, u32[]{:S(2)}, u32[]{:S(2)}) collective-permute-start(bf16[16,1664]{1,0:T(8,128)(2,1)S(1)} %get-tuple-element.10), channel_id=1, source_target_pairs={{0,12},{2,14},{4,8},{6,10},{8,4},{10,6},{12,0},{14,2},{1,13},{3,15... | collective-permute-start | bytes 159752 | tf_op jit(solution)/shard_map/ppermute | solution.py:327
  15.8 0.0 collective-permute-start.1
  15.8 0.6 collective-permute-start
  16.5 1.7 %collective-permute-done.2 = bf16[16,1664]{1,0:T(8,128)(2,1)S(1)} collective-permute-done((bf16[16,1664]{1,0:T(8,128)(2,1)S(1)}, bf16[16,1664]{1,0:T(8,128)(2,1)S(1)}, u32[]{:S(2)}, u32[]{:S(2)}) %collective-permute-start.2) | collective-permute-done | bytes 53280 | tf_op jit(solution)/shard_map/ppermute | solution.py:327
  18.2 2.7 %collective-permute-done.1 = bf16[16,1664]{1,0:T(8,128)(2,1)S(1)} collective-permute-done((bf16[16,1664]{1,0:T(8,128)(2,1)S(1)}, bf16[16,1664]{1,0:T(8,128)(2,1)S(1)}, u32[]{:S(2)}, u32[]{:S(2)}) %collective-permute-start.1) | collective-permute-done | bytes 53280 | tf_op jit(solution)/shard_map/ppermute | solution.py:327
  20.9 1.6 %collective-permute-start.3 = (bf16[64,1664]{1,0:T(8,128)(2,1)S(1)}, bf16[64,1664]{1,0:T(8,128)(2,1)S(1)}, u32[]{:S(2)}, u32[]{:S(2)}) collective-permute-start(bf16[64,1664]{1,0:T(8,128)(2,1)S(1)} %pad_maximum_fusion), channel_id=1, source_target_pairs={{0,2},{2,0},{4,6},{6,4},{8,10},{10,8},{12,14},{14,12},{1,3},{3,1},... | collective-permute-start | bytes 638984 | tf_op jit(solution)/shard_map/ppermute | solution.py:327
  22.5 4.6 %collective-permute-done.3 = bf16[64,1664]{1,0:T(8,128)(2,1)S(1)} collective-permute-done((bf16[64,1664]{1,0:T(8,128)(2,1)S(1)}, bf16[64,1664]{1,0:T(8,128)(2,1)S(1)}, u32[]{:S(2)}, u32[]{:S(2)}) %collective-permute-start.3) | collective-permute-done | bytes 213024 | tf_op jit(solution)/shard_map/ppermute | solution.py:327
  27.1 0.1 collective-permute-start.4
  27.2 1.8 %collective-permute-done.4.other_ref = bf16[128,1664]{1,0:T(8,128)(2,1)S(1)} collective-permute-done((bf16[128,1664]{1,0:T(8,128)(2,1)S(1)}, bf16[128,1664]{1,0:T(8,128)(2,1)S(1)}, u32[]{:S(2)}, u32[]{:S(2)}) %collective-permute-start.4) | collective-permute-done | bytes 426016 | tf_op jit(solution)/shard_map/ppermute | solution.py:330
  29.0 7.4 %hidden.1 = bf16[128,768]{1,0:T(8,128)(2,1)S(1)} custom-call(bf16[128,1664]{1,0:T(8,128)(2,1)S(1)} %constant_dynamic-update-slice_fusion.own_ref, bf16[128,1664]{1,0:T(8,128)(2,1)S(1)} %collective-permute-done.4.other_ref, bf16[2,4096,384]{2,1,0:T(8,128)(2,1)} %gate_ref.1, bf16[2,4096,384]{2,1,0:T(8,128)(2,1)} %up_ref.1), custom_call_target="tpu_custom_call" | custom-call | tf_op jit(solution)/shard_map/hidden/pallas_call | solution.py:344
  36.4 0.2 collective-permute-start.5
  36.6 1.3 %collective-permute-done.5 = bf16[128,768]{1,0:T(8,128)(2,1)S(1)} collective-permute-done((bf16[128,768]{1,0:T(8,128)(2,1)S(1)}, bf16[128,768]{1,0:T(8,128)(2,1)S(1)}, u32[]{:S(2)}, u32[]{:S(2)}) %collective-permute-start.5) | collective-permute-done | bytes 196640 | tf_op jit(solution)/shard_map/ppermute | solution.py:330
  37.9 4.2 %down.3 = bf16[64,1536]{1,0:T(8,128)(2,1)S(1)} custom-call(bf16[64,768]{1,0:T(8,128)(2,1)S(1)} %get-tuple-element.20.own_ref, bf16[64,768]{1,0:T(8,128)(2,1)S(1)} %get-tuple-element.18.other_ref, bf16[2,768,2048]{2,1,0:T(8,128)(2,1)} %down_ref.3), custom_call_target="tpu_custom_call" | custom-call | tf_op jit(solution)/shard_map/down/pallas_call | solution.py:352
  42.1 0.0 copy-start.1
  42.1 0.0 copy-start.3
  42.1 0.0 copy-start.7
  42.2 0.0 copy-start.9
  42.2 1.6 %collective-permute-start.6 = (bf16[64,1536]{1,0:T(8,128)(2,1)S(1)}, bf16[64,1536]{1,0:T(8,128)(2,1)S(1)}, u32[]{:S(2)}, u32[]{:S(2)}) collective-permute-start(bf16[64,1536]{1,0:T(8,128)(2,1)S(1)} %down.3), channel_id=1, source_target_pairs={{0,2},{2,0},{4,6},{6,4},{8,10},{10,8},{12,14},{14,12},{1,3},{3,1},... | collective-permute-start | bytes 589832 | tf_op jit(solution)/shard_map/ppermute | solution.py:327
  43.7 0.5 collective-permute-start.11
  44.3 0.7 collective-permute-start.12
  44.9 4.2 %down.2 = f32[64,1536]{1,0:T(8,128)S(1)} custom-call(bf16[64,768]{1,0:T(8,128)(2,1)S(1)} %get-tuple-element.21.own_ref, bf16[64,768]{1,0:T(8,128)(2,1)S(1)} %get-tuple-element.19.other_ref, bf16[2,768,2048]{2,1,0:T(8,128)(2,1)} %down_ref.3), custom_call_target="tpu_custom_call" | custom-call | tf_op jit(solution)/shard_map/down/pallas_call | solution.py:352
  49.2 6.0 %collective-permute-done.6 = bf16[64,1536]{1,0:T(8,128)(2,1)S(1)} collective-permute-done((bf16[64,1536]{1,0:T(8,128)(2,1)S(1)}, bf16[64,1536]{1,0:T(8,128)(2,1)S(1)}, u32[]{:S(2)}, u32[]{:S(2)}) %collective-permute-start.6) | collective-permute-done | bytes 196640 | tf_op jit(solution)/shard_map/ppermute | solution.py:327
  55.2 3.3 %collective-permute-start.9 = (bf16[16,1536]{1,0:T(8,128)(2,1)S(1)}, bf16[16,1536]{1,0:T(8,128)(2,1)S(1)}, u32[]{:S(2)}, u32[]{:S(2)}) collective-permute-start(bf16[16,1536]{1,0:T(8,128)(2,1)S(1)} %get-tuple-element.22), channel_id=1, source_target_pairs={{0,12},{2,14},{4,8},{6,10},{8,4},{10,6},{12,0},{14,2},{1,13},{3,15... | collective-permute-start | bytes 147464 | tf_op jit(solution)/shard_map/ppermute | solution.py:327
  58.5 0.1 collective-permute-start.8
  58.6 1.1 %collective-permute-start.7 = (bf16[16,1536]{1,0:T(8,128)(2,1)S(1)}, bf16[16,1536]{1,0:T(8,128)(2,1)S(1)}, u32[]{:S(2)}, u32[]{:S(2)}) collective-permute-start(bf16[16,1536]{1,0:T(8,128)(2,1)S(1)} %get-tuple-element.24), channel_id=1, source_target_pairs={{0,4},{2,6},{4,0},{6,2},{8,12},{10,14},{12,8},{14,10},{1,5},{3,7},... | collective-permute-start | bytes 147464 | tf_op jit(solution)/shard_map/ppermute | solution.py:327
  59.7 1.5 %collective-permute-done.9.refs_5_ = bf16[16,1536]{1,0:T(8,128)(2,1)S(1)} collective-permute-done((bf16[16,1536]{1,0:T(8,128)(2,1)S(1)}, bf16[16,1536]{1,0:T(8,128)(2,1)S(1)}, u32[]{:S(2)}, u32[]{:S(2)}) %collective-permute-start.9) | collective-permute-done | bytes 49184 | tf_op jit(solution)/shard_map/ppermute | solution.py:327
  61.2 2.3 %collective-permute-done.8.refs_4_ = bf16[16,1536]{1,0:T(8,128)(2,1)S(1)} collective-permute-done((bf16[16,1536]{1,0:T(8,128)(2,1)S(1)}, bf16[16,1536]{1,0:T(8,128)(2,1)S(1)}, u32[]{:S(2)}, u32[]{:S(2)}) %collective-permute-start.8) | collective-permute-done | bytes 49184 | tf_op jit(solution)/shard_map/ppermute | solution.py:327
  63.5 0.1 collective-permute-start.10
  63.6 0.1 slice.59
  63.7 0.1 copy.20
  63.8 0.1 reshape.29
  63.9 0.1 copy.17
  64.0 1.0 %resample.1 = (bf16[4,2,131,128]{3,2,1,0:T(8,128)(2,1)S(1)}, bf16[4,2,131,128]{3,2,1,0:T(8,128)(2,1)S(1)}) custom-call(s32[8,4]{1,0:T(8,128)S(1)} %bitcast.7, bf16[8,144,128]{2,1,0:T(8,128)(2,1)S(1)} %collective-permute-done.11.near_ref, bf16[8,144,128]{2,1,0:T(8,128)(2,1)S(1)} %collective-permute-done.12.far_ref, bf16[4,2,128,128]{3,2,1,0:T(8,128)(2,1)S(1)} %copy-done.1, ...), custom_call_target="tpu_custom_call" | custom-call | tf_op jit(solution)/shard_map/resample/pallas_call | solution.py:368
  65.0 0.9 %copy.18 = bf16[4,2,131,128]{3,1,2,0:T(2,128)(2,1)} copy(bf16[4,2,131,128]{3,2,1,0:T(8,128)(2,1)S(1)} %get-tuple-element.16) | data formatting | bytes 536576
  65.9 0.9 %copy.19 = bf16[4,2,131,128]{3,1,2,0:T(2,128)(2,1)} copy(bf16[4,2,131,128]{3,2,1,0:T(8,128)(2,1)S(1)} %get-tuple-element.17) | data formatting | bytes 536576
  66.8 0.7 unpack.1
  (34 shorter events, 0.3 us)
Async XLA Ops:
  0.6 1.0 %copy-start = (bf16[4,2,128,128]{3,2,1,0:T(8,128)(2,1)S(1)}, bf16[4,2,128,128]{3,2,1,0:T(8,128)(2,1)}, u32[]{:S(2)}) copy-start(bf16[4,2,128,128]{3,2,1,0:T(8,128)(2,1)} %ck_ref.3) | copy-start | bytes 786436
  1.6 0.9 %copy-start.2 = (bf16[4,2,128,128]{3,2,1,0:T(8,128)(2,1)S(1)}, bf16[4,2,128,128]{3,2,1,0:T(8,128)(2,1)}, u32[]{:S(2)}) copy-start(bf16[4,2,128,128]{3,2,1,0:T(8,128)(2,1)} %cv_ref.3) | copy-start | bytes 786436
  2.5 0.9 %copy-start.4 = (bf16[3,4,4096]{2,1,0:T(4,128)(2,1)S(1)}, bf16[3,4,4096]{2,1,0:T(4,128)(2,1)}, u32[]{:S(2)}) copy-start(bf16[3,4,4096]{2,1,0:T(4,128)(2,1)} %hidden_ref.1) | copy-start | bytes 294916
  3.4 0.8 %copy-start.5 = (bf16[3,4,16,128]{3,2,1,0:T(8,128)(2,1)S(1)}, bf16[3,4,16,128]{3,2,1,0:T(8,128)(2,1)}, u32[]{:S(2)}) copy-start(bf16[3,4,16,128]{3,2,1,0:T(8,128)(2,1)} %q_ref.1) | copy-start | bytes 147460
  4.2 0.7 %copy-start.6 = (bf16[3,4,2,128]{3,2,1,0:T(2,128)(2,1)S(1)}, bf16[3,4,2,128]{3,2,1,0:T(2,128)(2,1)}, u32[]{:S(2)}) copy-start(bf16[3,4,2,128]{3,2,1,0:T(2,128)(2,1)} %nk_ref.3) | copy-start | bytes 18436
  4.9 0.7 %copy-start.8 = (bf16[3,4,2,128]{3,2,1,0:T(2,128)(2,1)S(1)}, bf16[3,4,2,128]{3,2,1,0:T(2,128)(2,1)}, u32[]{:S(2)}) copy-start(bf16[3,4,2,128]{3,2,1,0:T(2,128)(2,1)} %nv_ref.3) | copy-start | bytes 18436
  5.6 0.7 %copy-start.10 = (f32[4096]{0:T(1024)S(1)}, f32[4096]{0:T(1024)}, u32[]{:S(2)}) copy-start(f32[4096]{0:T(1024)} %param.21) | copy-start | bytes 49156
  6.3 0.7 %copy-start.11 = (s32[3,4,8]{2,1,0:T(4,128)S(1)}, s32[3,4,8]{2,1,0:T(4,128)}, u32[]{:S(2)}) copy-start(s32[3,4,8]{2,1,0:T(4,128)} %ids_ref.1) | copy-start | bytes 1156
  7.0 0.7 %copy-start.12 = (f32[3,4,8]{2,1,0:T(4,128)S(1)}, f32[3,4,8]{2,1,0:T(4,128)}, u32[]{:S(2)}) copy-start(f32[3,4,8]{2,1,0:T(4,128)} %weights_ref.1) | copy-start | bytes 1156
  7.7 0.7 copy-start.13
  10.7 7.4 %collective-permute-start.2 = (bf16[16,1664]{1,0:T(8,128)(2,1)S(1)}, bf16[16,1664]{1,0:T(8,128)(2,1)S(1)}, u32[]{:S(2)}, u32[]{:S(2)}) collective-permute-start(bf16[16,1664]{1,0:T(8,128)(2,1)S(1)} %get-tuple-element.10), channel_id=1, source_target_pairs={{0,12},{2,14},{4,8},{6,10},{8,4},{10,6},{12,0},{14,2},{1,13},{3,15... | collective-permute-start | bytes 159752 | tf_op jit(solution)/shard_map/ppermute | solution.py:327
  15.8 5.0 %collective-permute-start.1 = (bf16[16,1664]{1,0:T(8,128)(2,1)S(1)}, bf16[16,1664]{1,0:T(8,128)(2,1)S(1)}, u32[]{:S(2)}, u32[]{:S(2)}) collective-permute-start(bf16[16,1664]{1,0:T(8,128)(2,1)S(1)} %get-tuple-element.10), channel_id=1, source_target_pairs={{0,8},{2,10},{4,12},{6,14},{8,0},{10,2},{12,4},{14,6},{1,9},{3,11}... | collective-permute-start | bytes 159752 | tf_op jit(solution)/shard_map/ppermute | solution.py:327
  15.8 5.0 %collective-permute-start = (bf16[16,1664]{1,0:T(8,128)(2,1)S(1)}, bf16[16,1664]{1,0:T(8,128)(2,1)S(1)}, u32[]{:S(2)}, u32[]{:S(2)}) collective-permute-start(bf16[16,1664]{1,0:T(8,128)(2,1)S(1)} %get-tuple-element.10), channel_id=1, source_target_pairs={{0,4},{2,6},{4,0},{6,2},{8,12},{10,14},{12,8},{14,10},{1,5},{3,7},... | collective-permute-start | bytes 159752 | tf_op jit(solution)/shard_map/ppermute | solution.py:327
  20.9 6.2 %collective-permute-start.3 = (bf16[64,1664]{1,0:T(8,128)(2,1)S(1)}, bf16[64,1664]{1,0:T(8,128)(2,1)S(1)}, u32[]{:S(2)}, u32[]{:S(2)}) collective-permute-start(bf16[64,1664]{1,0:T(8,128)(2,1)S(1)} %pad_maximum_fusion), channel_id=1, source_target_pairs={{0,2},{2,0},{4,6},{6,4},{8,10},{10,8},{12,14},{14,12},{1,3},{3,1},... | collective-permute-start | bytes 638984 | tf_op jit(solution)/shard_map/ppermute | solution.py:327
  27.1 1.8 %collective-permute-start.4 = (bf16[128,1664]{1,0:T(8,128)(2,1)S(1)}, bf16[128,1664]{1,0:T(8,128)(2,1)S(1)}, u32[]{:S(2)}, u32[]{:S(2)}) collective-permute-start(bf16[128,1664]{1,0:T(8,128)(2,1)S(1)} %constant_dynamic-update-slice_fusion.own_ref), channel_id=1, source_target_pairs={{0,1},{1,0},{2,3},{3,2},{4,5},{5,4},{6,7},{7,6},{8,9},{9,8},{10,11... | collective-permute-start | bytes 1277960 | tf_op jit(solution)/shard_map/ppermute | solution.py:330
  36.4 1.5 %collective-permute-start.5 = (bf16[128,768]{1,0:T(8,128)(2,1)S(1)}, bf16[128,768]{1,0:T(8,128)(2,1)S(1)}, u32[]{:S(2)}, u32[]{:S(2)}) collective-permute-start(bf16[128,768]{1,0:T(8,128)(2,1)S(1)} %hidden.1), channel_id=1, source_target_pairs={{0,1},{1,0},{2,3},{3,2},{4,5},{5,4},{6,7},{7,6},{8,9},{9,8},{10,11... | collective-permute-start | bytes 589832 | tf_op jit(solution)/shard_map/ppermute | solution.py:330
  42.1 21.9 %copy-start.1 = (bf16[4,2,128,128]{3,2,1,0:T(8,128)(2,1)S(1)}, bf16[4,2,128,128]{3,2,1,0:T(8,128)(2,1)}, u32[]{:S(2)}) copy-start(bf16[4,2,128,128]{3,2,1,0:T(8,128)(2,1)} %ck_ref.3) | copy-start | bytes 786436
  42.1 21.9 %copy-start.3 = (bf16[4,2,128,128]{3,2,1,0:T(8,128)(2,1)S(1)}, bf16[4,2,128,128]{3,2,1,0:T(8,128)(2,1)}, u32[]{:S(2)}) copy-start(bf16[4,2,128,128]{3,2,1,0:T(8,128)(2,1)} %cv_ref.3) | copy-start | bytes 786436
  42.1 21.9 %copy-start.7 = (bf16[3,4,2,128]{3,2,1,0:T(2,128)(2,1)S(1)}, bf16[3,4,2,128]{3,2,1,0:T(2,128)(2,1)}, u32[]{:S(2)}) copy-start(bf16[3,4,2,128]{3,2,1,0:T(2,128)(2,1)} %nk_ref.3) | copy-start | bytes 18436
  42.2 21.9 %copy-start.9 = (bf16[3,4,2,128]{3,2,1,0:T(2,128)(2,1)S(1)}, bf16[3,4,2,128]{3,2,1,0:T(2,128)(2,1)}, u32[]{:S(2)}) copy-start(bf16[3,4,2,128]{3,2,1,0:T(2,128)(2,1)} %nv_ref.3) | copy-start | bytes 18436
  42.2 13.0 %collective-permute-start.6 = (bf16[64,1536]{1,0:T(8,128)(2,1)S(1)}, bf16[64,1536]{1,0:T(8,128)(2,1)S(1)}, u32[]{:S(2)}, u32[]{:S(2)}) collective-permute-start(bf16[64,1536]{1,0:T(8,128)(2,1)S(1)} %down.3), channel_id=1, source_target_pairs={{0,2},{2,0},{4,6},{6,4},{8,10},{10,8},{12,14},{14,12},{1,3},{3,1},... | collective-permute-start | bytes 589832 | tf_op jit(solution)/shard_map/ppermute | solution.py:327
  43.7 20.3 %collective-permute-start.11 = (bf16[8,144,128]{2,1,0:T(8,128)(2,1)S(1)}, bf16[8,144,128]{2,1,0:T(8,128)(2,1)S(1)}, u32[]{:S(2)}, u32[]{:S(2)}) collective-permute-start(bf16[8,144,128]{2,1,0:T(8,128)(2,1)S(1)} %get-tuple-element.11), channel_id=1, source_target_pairs={{0,2},{2,0},{4,6},{6,4},{8,10},{10,8},{12,14},{14,12},{1,3},{3,1},... | collective-permute-start | bytes 884744 | tf_op jit(solution)/shard_map/ppermute | solution.py:327
  44.3 19.8 %collective-permute-start.12 = (bf16[8,144,128]{2,1,0:T(8,128)(2,1)S(1)}, bf16[8,144,128]{2,1,0:T(8,128)(2,1)S(1)}, u32[]{:S(2)}, u32[]{:S(2)}) collective-permute-start(bf16[8,144,128]{2,1,0:T(8,128)(2,1)S(1)} %get-tuple-element.12), channel_id=1, source_target_pairs={{0,0},{2,4},{4,2},{6,8},{8,6},{10,12},{12,10},{14,14},{1,1},{3,5},... | collective-permute-start | bytes 884744 | tf_op jit(solution)/shard_map/ppermute | solution.py:343
  55.2 6.0 %collective-permute-start.9 = (bf16[16,1536]{1,0:T(8,128)(2,1)S(1)}, bf16[16,1536]{1,0:T(8,128)(2,1)S(1)}, u32[]{:S(2)}, u32[]{:S(2)}) collective-permute-start(bf16[16,1536]{1,0:T(8,128)(2,1)S(1)} %get-tuple-element.22), channel_id=1, source_target_pairs={{0,12},{2,14},{4,8},{6,10},{8,4},{10,6},{12,0},{14,2},{1,13},{3,15... | collective-permute-start | bytes 147464 | tf_op jit(solution)/shard_map/ppermute | solution.py:327
  58.5 5.0 %collective-permute-start.8 = (bf16[16,1536]{1,0:T(8,128)(2,1)S(1)}, bf16[16,1536]{1,0:T(8,128)(2,1)S(1)}, u32[]{:S(2)}, u32[]{:S(2)}) collective-permute-start(bf16[16,1536]{1,0:T(8,128)(2,1)S(1)} %get-tuple-element.23), channel_id=1, source_target_pairs={{0,8},{2,10},{4,12},{6,14},{8,0},{10,2},{12,4},{14,6},{1,9},{3,11}... | collective-permute-start | bytes 147464 | tf_op jit(solution)/shard_map/ppermute | solution.py:327
  58.6 4.9 %collective-permute-start.7 = (bf16[16,1536]{1,0:T(8,128)(2,1)S(1)}, bf16[16,1536]{1,0:T(8,128)(2,1)S(1)}, u32[]{:S(2)}, u32[]{:S(2)}) collective-permute-start(bf16[16,1536]{1,0:T(8,128)(2,1)S(1)} %get-tuple-element.24), channel_id=1, source_target_pairs={{0,4},{2,6},{4,0},{6,2},{8,12},{10,14},{12,8},{14,10},{1,5},{3,7},... | collective-permute-start | bytes 147464 | tf_op jit(solution)/shard_map/ppermute | solution.py:327
  63.5 3.3 %collective-permute-start.10 = (bf16[16,1536]{1,0:T(8,128)(2,1)S(1)}, bf16[16,1536]{1,0:T(8,128)(2,1)S(1)}, u32[]{:S(2)}, u32[]{:S(2)}) collective-permute-start(bf16[16,1536]{1,0:T(8,128)(2,1)S(1)} %total.1.own_ref), channel_id=1, source_target_pairs={{0,1},{1,0},{2,3},{3,2},{4,5},{5,4},{6,7},{7,6},{8,9},{9,8},{10,11... | collective-permute-start | bytes 147464 | tf_op jit(solution)/shard_map/ppermute | solution.py:330

commit v2 on v1

--- a/solution.py
+++ b/solution.py
@@ -10,6 +10,7 @@
 
 REACH = 2
 LANES = 128
+PAD = 8
 f32, bf16 = jnp.float32, jnp.bfloat16
 
 epsilon = 1e-06
@@ -24,9 +25,69 @@
     return lax.broadcasted_iota(jnp.int32, shape, dim)
 
 
+def load_kernel(
+    steps, ids_in, weights_in, counts_in, gain_in, hidden_in, q_in, nk_in, nv_in, ck_in, cv_in,
+    ids_ref, weights_ref, counts_ref, gain_ref, hidden_ref, q_ref, nk_ref, nv_ref, ck_ref, cv_ref, near_ref, far_ref, sems,
+):
+    pairs = (
+        (ck_in, ck_ref), (cv_in, cv_ref), (nk_in, nk_ref), (nv_in, nv_ref), (q_in, q_ref), (hidden_in, hidden_ref),
+        (gain_in, gain_ref), (ids_in, ids_ref), (weights_in, weights_ref), (counts_in, counts_ref),
+    )
+    copies = [pltpu.make_async_copy(source, target, sems.at[n]) for n, (source, target) in enumerate(pairs)]
+    for copy in copies:
+        copy.start()
+    for copy in copies:
+        copy.wait()
+    tokens, kv_heads, cached, width = ck_ref.shape
+
+    odd = lax.rem(lax.axis_index("expert"), 2)
+    per = REACH * kv_heads
+
+    early = near_ref.shape[0]
+
+    def halo(start, kinds, slot):
+        for cache_ref, new_ref in kinds:
+            for r in range(REACH):
+                for h in range(kv_heads):
+                    out_ref, at = (near_ref, slot) if slot < early else (far_ref, slot - early)
+                    out_ref[at, :cached, :] = cache_ref[start + r, h]
+                    new = jnp.concatenate(
+                        [new_ref[s, start + r, h : h + 1, :].astype(f32) for s in range(steps)]
+                        + [jnp.zeros((PAD - steps, width), f32)], axis=0)
+                    out_ref[at, cached:, :] = new.astype(bf16)
+                    slot += 1
+
+    keys, values = (ck_ref, nk_ref), (cv_ref, nv_ref)
+    tail = tokens - REACH
+
+    @pl.when(odd == 0)
+    def _():
+        halo(tail, (keys, values), 0)
+        halo(0, (keys, values), 2 * per)
+
+    @pl.when(odd == 1)
+    def _():
+        halo(0, (keys, values), 0)
+        halo(tail, (keys, values), 2 * per)
+
+
+def weight_kernel(after_ref, source, target, token_ref, sems):
+    copies = []
+    part = source.shape[1] // 2
+    for e in range(source.shape[0]):
+        for k in range(2):
+            at = pl.ds(k * part, part)
+            copies.append(pltpu.make_async_copy(source.at[e, at], target.at[e, at], sems.at[len(copies)]))
+    for copy in copies:
+        copy.start()
+    for copy in copies:
+        copy.wait()
+    token_ref[...] = jnp.zeros_like(token_ref)
+
+
 def attend_kernel(
     steps, experts, ids_ref, weights_ref, counts_ref, gain_ref, hidden_ref, q_ref, nk_ref, nv_ref, ck_ref, cv_ref,
-    send_ref, residual_ref, near_ref, far_ref, scores_ref,
+    send_ref, residual_ref, scores_ref,
 ):
     tokens, heads, width = q_ref.shape[1:]
     kv_heads, cached = ck_ref.shape[1:3]
@@ -39,30 +100,6 @@
     fresh = steps * kv_heads
     fresh_rows = -(-fresh // 16) * 16
     scale = 1.0 / math.sqrt(width)
-
-    odd = lax.rem(lax.axis_index("expert"), 2)
-    per = REACH * kv_heads
-
-    def halo(out_ref, start):
-        for kind, (cache_ref, new_ref) in enumerate(((ck_ref, nk_ref), (cv_ref, nv_ref))):
-            for r in range(REACH):
-                for h in range(kv_heads):
-                    slot = kind * per + r * kv_heads + h
-                    out_ref[slot, :cached, :] = cache_ref[start + r, h]
-                    new = jnp.concatenate(
-                        [new_ref[s, start + r, h : h + 1, :].astype(f32) for s in range(steps)]
-                        + [jnp.zeros((16 - steps, width), f32)], axis=0)
-                    out_ref[slot, cached:, :] = new.astype(bf16)
-
-    @pl.when(odd == 0)
-    def _():
-        halo(near_ref, tokens - REACH)
-        halo(far_ref, 0)
-
-    @pl.when(odd == 1)
-    def _():
-        halo(near_ref, 0)
-        halo(far_ref, tokens - REACH)
 
     q_rows = steps * heads
     row = iota((q_rows, kv_heads * cached), 0)
@@ -161,27 +198,44 @@
     return hit.astype(f32).astype(bf16)
 
 
-def hidden_kernel(steps, tokens, experts, own_ref, other_ref, gate_ref, up_ref, out_ref):
-    total, padded = own_ref.shape
+def halves(even_ref, odd_ref, at):
+    return jnp.concatenate([even_ref[:, at], odd_ref[:, at]], axis=0)
+
+
+def expert_products(steps, tokens, features, gate_ref, up_ref, half):
+    total, main = features.shape
     rows = (steps + 1) * tokens
-    main = padded - LANES
     part = main // steps
     columns = main + part
+    local = gate_ref.shape[0]
+    blocks = total // rows
+    extra = sum(
+        dot(unpacking(blocks, steps, tokens, s, False), features[:, s * part : (s + 1) * part]) for s in range(steps)
+    ).astype(bf16)
+    first = pl.ds(pl.multiple_of(half * columns, LANES), main)
+    last = pl.ds(pl.multiple_of(half * columns + main, LANES), part)
+    return [
+        dot(features, ref[e, first, :]) + dot(extra, ref[e, last, :]) for ref in (gate_ref, up_ref) for e in range(local)
+    ]
+
+
+def partial_kernel(steps, tokens, after_ref, also_after_ref, even_ref, odd_ref, gate_ref, up_ref, out_ref):
+    main = even_ref.shape[1] - LANES
+    products = expert_products(steps, tokens, halves(even_ref, odd_ref, slice(0, main)), gate_ref, up_ref, lax.axis_index("tensor"))
+    for n, product in enumerate(products):
+        out_ref[n] = product
+
+
+def hidden_kernel(steps, tokens, experts, partial_ref, even_ref, odd_ref, even_other_ref, odd_other_ref, gate_ref, up_ref, out_ref):
+    main = even_ref.shape[1] - LANES
+    total = 2 * even_ref.shape[0]
+    rows = (steps + 1) * tokens
+    columns = main + main // steps
     local, _, units = gate_ref.shape
-    mine = lax.axis_index("tensor")
-    blocks = total // rows
-    gates, ups = [0.0] * local, [0.0] * local
-    unpacks = [unpacking(blocks, steps, tokens, s, False) for s in range(steps)]
-    for ref, half in ((own_ref, mine), (other_ref, 1 - mine)):
-        features = ref[:, :main]
-        extra = sum(dot(unpacks[s], features[:, s * part : (s + 1) * part]) for s in range(steps)).astype(bf16)
-        first = pl.multiple_of(half * columns, LANES)
-        last = pl.multiple_of(half * columns + main, LANES)
-        for e in range(local):
-            gates[e] += dot(features, gate_ref[e, pl.ds(first, main), :]) + dot(extra, gate_ref[e, pl.ds(last, part), :])
-            ups[e] += dot(features, up_ref[e, pl.ds(first, main), :]) + dot(extra, up_ref[e, pl.ds(last, part), :])
-    meta = own_ref[:, main:].astype(f32)
-    meta_other = other_ref[:, main:].astype(f32)
+    features = halves(even_other_ref, odd_other_ref, slice(0, main))
+    products = expert_products(steps, tokens, features, gate_ref, up_ref, 1 - lax.axis_index("tensor"))
+    meta = halves(even_ref, odd_ref, slice(main, None)).astype(f32)
+    meta_other = halves(even_other_ref, odd_other_ref, slice(main, None)).astype(f32)
     lane = iota(meta.shape, 1)
     valid = lax.rem(iota((total, 1), 0), rows) < steps * tokens
     in_squares = (lane == 2 * experts) | (lane == 2 * experts + 1)
@@ -191,14 +245,14 @@
     for e in range(local):
         at = first_expert + e
         share = jnp.sum(jnp.where((lane == at) | (lane == at + experts), meta, 0.0), axis=1, keepdims=True)
-        gate = (gates[e] * factor).astype(bf16).astype(f32)
-        up = (ups[e] * factor).astype(bf16).astype(f32)
+        gate = ((partial_ref[e] + products[e]) * factor).astype(bf16).astype(f32)
+        up = ((partial_ref[local + e] + products[local + e]) * factor).astype(bf16).astype(f32)
         hidden = gate / (1.0 + jnp.exp(-gate)) * up * share
         out_ref[:, e * units : (e + 1) * units] = hidden.astype(bf16)
 
 
-def down_kernel(steps, tokens, own_ref, other_ref, down_ref, out_ref):
-    total, width = own_ref.shape
+def down_kernel(steps, tokens, begin, own_ref, other_ref, down_ref, out_ref):
+    total, width = out_ref.shape[0], own_ref.shape[1]
     local, _, columns = down_ref.shape
     units = width // local
     rows = (steps + 1) * tokens
@@ -210,14 +264,14 @@
     for ref, half in ((own_ref, mine), (other_ref, 1 - mine)):
         start = pl.multiple_of(half * units, LANES)
         for e in range(local):
-            product += dot(ref[:, e * units : (e + 1) * units], down_ref[e, pl.ds(start, units), :])
+            product += dot(ref[begin : begin + total, e * units : (e + 1) * units], down_ref[e, pl.ds(start, units), :])
     last = product[:, main:].astype(bf16)
     extra = jnp.concatenate([dot(unpacking(blocks, steps, tokens, s, True), last) for s in range(steps)], axis=1)
     in_main = lax.rem(iota((total, main), 0), rows) < steps * tokens
     out_ref[...] = jnp.where(in_main, product[:, :main], extra).astype(out_ref.dtype)
 
 
-def resample_kernel(steps, counts_ref, near_ref, far_ref, ck_ref, cv_ref, nk_ref, nv_ref, keys_ref, values_ref):
+def resample_kernel(steps, early, counts_ref, near_ref, relay_ref, ck_ref, cv_ref, nk_ref, nv_ref, keys_ref, values_ref):
     tokens, kv_heads, cached, width = ck_ref.shape
     devices = counts_ref.shape[0]
     me = lax.axis_index("expert")
@@ -239,30 +293,27 @@
         @pl.when((offset >= 0) & (offset < tokens))
         def _():
             for out_ref, cache_ref, new_ref in ((keys_ref, ck_ref, nk_ref), (values_ref, cv_ref, nv_ref)):
-                out_ref[i, :, :cached, :] = cache_ref[offset]
+                out_ref[i, :cached] = jnp.swapaxes(cache_ref[offset], 0, 1)
                 for s in range(steps):
-                    out_ref[i, :, cached + s, :] = new_ref[s, offset]
+                    out_ref[i, cached + s] = new_ref[s, offset]
 
         def from_halo(ref, at):
             for kind, out_ref in enumerate((keys_ref, values_ref)):
-                for h in range(kv_heads):
-                    out_ref[i, h, :, :] = ref[kind * per + at * kv_heads + h, : cached + steps, :]
-
-        @pl.when((offset < 0) & (odd == 1))
+                slots = ref[pl.ds(kind * per + at * kv_heads, kv_heads)]
+                out_ref[i] = jnp.swapaxes(slots[:, : cached + steps], 0, 1)
+
+        left = offset < 0
+        near = (left & (odd == 1)) | ((offset >= tokens) & (odd == 0))
+        far = (left & (odd == 0)) | ((offset >= tokens) & (odd == 1))
+        at = jnp.where(left, offset + REACH, offset - tokens)
+
+        @pl.when(near)
         def _():
-            from_halo(near_ref, offset + REACH)
-
-        @pl.when((offset < 0) & (odd == 0))
+            from_halo(near_ref, at)
+
+        @pl.when(far)
         def _():
-            from_halo(far_ref, offset + REACH)
-
-        @pl.when((offset >= tokens) & (odd == 0))
-        def _():
-            from_halo(near_ref, offset - tokens)
-
-        @pl.when((offset >= tokens) & (odd == 1))
-        def _():
-            from_halo(far_ref, offset - tokens)
+            from_halo(relay_ref, at)
 
 
 def add_kernel(a_ref, b_ref, out_ref):
@@ -294,18 +345,24 @@
 
 VMEM = pl.BlockSpec(memory_space=pltpu.VMEM)
 SMEM = pl.BlockSpec(memory_space=pltpu.SMEM)
-
-
-def call(kernel, out, specs, name, scratch=(), limit=48):
+HBM = pl.BlockSpec(memory_space=pltpu.HBM)
+
+
+def call(kernel, out, specs, name, microseconds, scratch=(), limit=20):
     outs = jax.tree.map(lambda _: VMEM, out)
     return pl.pallas_call(
         kernel, out_shape=out, in_specs=specs, out_specs=outs, scratch_shapes=scratch, name=name,
+        cost_estimate=pl.CostEstimate(flops=0, bytes_accessed=int(microseconds * 3.5e6), transcendentals=0),
         compiler_params=pltpu.CompilerParams(vmem_limit_bytes=limit << 20),
     )
 
 
 def struct(shape, dtype):
     return jax.ShapeDtypeStruct(shape, dtype)
+
+
+def in_hbm(value):
+    return pltpu.with_memory_space_constraint(value, pltpu.HBM)
 
 
 def fast_shards(
@@ -321,7 +378,9 @@
     part = columns // (steps + 1)
     main = steps * part
     rows = (steps + 1) * tokens
-    halo = struct((2 * REACH * kv_heads, cached + 16, width), bf16)
+    per = REACH * kv_heads
+    early = 2 * per + per // 2
+    halos = [pltpu.VMEM((slots, cached + PAD, width), bf16) for slots in (early, 4 * per - early)]
 
     def swap(value, offset):
         return lax.ppermute(value, "expert", [(i, i ^ offset) for i in range(count)])
@@ -329,46 +388,76 @@
     def sibling(value):
         return lax.ppermute(value, "tensor", [(0, 1), (1, 0)])
 
-    send, residual, near, far = call(
+    inputs = (route_ids, route_weights, ancestor_counts, norm_gain.reshape(1, -1), hidden_in, queries, new_keys, new_values, cache_keys, cache_values)
+    spaces = [pltpu.SMEM if value is ancestor_counts else pltpu.VMEM for value in inputs]
+    loaded = pl.pallas_call(
+        functools.partial(load_kernel, steps),
+        out_shape=[space(value.shape, value.dtype) for space, value in zip(spaces, inputs)] + halos,
+        in_specs=[HBM] * len(inputs), out_specs=[pl.BlockSpec(memory_space=space) for space in spaces] + [VMEM] * 2,
+        scratch_shapes=[pltpu.SemaphoreType.DMA((len(inputs),))], name="load",
+        compiler_params=pltpu.CompilerParams(vmem_limit_bytes=20 << 20),
+    )(*(in_hbm(value) for value in inputs))
+    *loaded, near, far = loaded
+    near = swap(near, 1)
+    new_keys, new_values, cache_keys, cache_values = loaded[6:]
+    send, residual = call(
         functools.partial(attend_kernel, steps, experts),
-        (struct((rows, main + LANES), bf16), struct((rows, main), f32), halo, halo),
-        [VMEM, VMEM, SMEM] + [VMEM] * 7, "attend", [pltpu.VMEM(((steps + 1) * rows, LANES), f32)],
-    )(route_ids, route_weights, ancestor_counts, norm_gain.reshape(1, -1), hidden_in, queries, new_keys, new_values, cache_keys, cache_values)
-
+        (struct((rows, main + LANES), bf16), struct((rows, main), f32)),
+        [VMEM, VMEM, SMEM] + [VMEM] * 7, "attend", 2.3, [pltpu.VMEM(((steps + 1) * rows, LANES), f32)],
+    )(*loaded)
+
+    def fetch(after, weight, name):
+        return pl.pallas_call(
+            weight_kernel, out_shape=[pltpu.VMEM(weight.shape, weight.dtype), pltpu.VMEM((8, LANES), f32)],
+            in_specs=[VMEM, HBM], out_specs=[VMEM] * 2, scratch_shapes=[pltpu.SemaphoreType.DMA((2 * local,))], name=name,
+            cost_estimate=pl.CostEstimate(flops=0, bytes_accessed=7_000_000, transcendentals=0),
+            compiler_params=pltpu.CompilerParams(vmem_limit_bytes=16 << 20),
+        )(after, in_hbm(weight))
+
+    gate, token = fetch(residual, gate_weight, "gate")
     even = jnp.concatenate([send] + [swap(send, k) for k in range(2, count, 2)], axis=0)
-    near = swap(near, 1)
+    even, near, token = lax.optimization_barrier((even, near, token))
     odd = swap(even, 1)
-    own = jnp.concatenate([even, odd], axis=0)
-    other = sibling(own)
-    far = lax.ppermute(far, "expert", [(i, ((i + 1) ^ 1) - 1 if 0 < i < count - 1 else i) for i in range(count)])
+    even_other = sibling(even)
+    up, token_up = fetch(even, up_weight, "up")
+    odd, token_up, far = lax.optimization_barrier((odd, token_up, far))
+    relayed = swap(far, 1)
+    odd_other = sibling(odd)
+    partial = call(
+        functools.partial(partial_kernel, steps, tokens), struct((2 * local, count * rows, units), f32), [VMEM] * 6, "partial", 0.01,
+    )(token, token_up, even, odd, gate, up)
     hidden = call(
         functools.partial(hidden_kernel, steps, tokens, experts),
-        struct((count * rows, local * units), bf16), [VMEM] * 4, "hidden",
-    )(own, other, gate_weight, up_weight)
+        struct((count * rows, local * units), bf16), [VMEM] * 7, "hidden", 0.01,
+    )(partial, even, odd, even_other, odd_other, gate, up)
     other_hidden = sibling(hidden)
     half = count // 2 * rows
 
     def down(first, dtype):
         return call(
-            functools.partial(down_kernel, steps, tokens), struct((half, main), dtype), [VMEM] * 3, "down",
-        )(hidden[first : first + half], other_hidden[first : first + half], down_weight)
-
-    arrived = swap(down(half, bf16), 1)
+            functools.partial(down_kernel, steps, tokens, first), struct((half, main), dtype), [VMEM] * 3, "down", 0.01,
+        )(hidden, other_hidden, down_weight)
+
+    leaving, relayed = lax.optimization_barrier((down(half, bf16), relayed))
+    arrived = swap(leaving, 1)
+    ring = [(i, min(i + 2, count - 1) if i % 2 == 0 else max(i - 2, 0)) for i in range(count)]
+    far = lax.ppermute(jnp.concatenate([near[2 * per :], relayed], axis=0), "expert", ring)
     kept = down(0, f32)
-    own_block, others = kept[:rows], call(add_kernel, struct((half - rows, main), bf16), [VMEM] * 2, "add")(kept[rows:], arrived[rows:])
+    own_block, others = kept[:rows], call(add_kernel, struct((half - rows, main), bf16), [VMEM] * 2, "add", 0.1)(kept[rows:], arrived[rows:])
+
+    counts = jnp.stack([even, odd], 0).reshape(2, count // 2, rows, main + LANES)[:, :, :tokens, main + 2 * experts + 2].astype(jnp.int32)
+    counts = counts.transpose(1, 0, 2).reshape(count, tokens)
+    out = struct((tokens, cached + steps, kv_heads, width), bf16)
+    keys, values = call(functools.partial(resample_kernel, steps, early), (out, out), [SMEM] + [VMEM] * 6, "resample", 2.2)(
+        counts, near, far, cache_keys, cache_values, new_keys, new_values
+    )
     returned = [swap(others[(k // 2 - 1) * rows : k // 2 * rows], k) for k in range(2, count, 2)]
-    result = call(functools.partial(total_kernel, len(returned) + 2), struct((rows, main), bf16), [VMEM] * (len(returned) + 3), "total")(
+    keys, values, *returned = lax.optimization_barrier((keys, values, *returned))
+    result = call(functools.partial(total_kernel, len(returned) + 2), struct((rows, main), bf16), [VMEM] * (len(returned) + 3), "total", 0.1)(
         residual, own_block, arrived[:rows], *returned
     )
-    layer_out = call(unpack_kernel, struct((steps, tokens, 2 * columns), bf16), [VMEM] * 2, "unpack")(result, sibling(result))
-
-    counts = own.reshape(count, rows, main + LANES)[:, :tokens, main + 2 * experts + 2].astype(jnp.int32)
-    counts = counts.reshape(2, count // 2, tokens).transpose(1, 0, 2).reshape(count, tokens)
-    out = struct((tokens, kv_heads, cached + steps, width), bf16)
-    keys, values = call(functools.partial(resample_kernel, steps), (out, out), [SMEM] + [VMEM] * 6, "resample")(
-        counts, near, far, cache_keys, cache_values, new_keys, new_values
-    )
-    return layer_out, keys, values
+    layer_out = call(unpack_kernel, struct((steps, tokens, 2 * columns), bf16), [VMEM] * 2, "unpack", 0.5)(result, sibling(result))
+    return layer_out, keys.transpose(0, 2, 1, 3), values.transpose(0, 2, 1, 3)
 
 
 def padded(cells, sides, width):

time: 68.1 us -> 47.4 us (0.70)
  local copies, waits for them, and re-layouts: 10.1 us -> 0.09 us
  waiting for transfers between devices: 21.8 us -> 14.7 us
  Pallas kernels: 19.8 us -> 17.3 us
  starting transfers between devices: 14.9 us -> 14 us
    unnamed x35 -> x8, local copies, waits for them, and re-layouts: 9.73 us -> 0.02 us
    ppermute x9 -> x10, waiting for transfers between devices: 18.8 us -> 12.3 us  [swap(): lax.ppermute(value, 'expert', [(i, i ^ offset) for i in range(count)])]
    pallas_call x1, Pallas kernels: 7.4 us -> 1.51 us  [fast_shards(): call(functools.partial(hidden_kernel, steps, tokens, experts), struct((co...]
    pallas_call x4 -> x8, Pallas kernels: 9.39 us -> 13.3 us  [the longest x2 5.73 us: fetch(): pl.pallas_call(weight_kernel, out_shape=[pltpu.VMEM(weight.shape, weight....]
    ppermute x3 -> x4, waiting for transfers between devices: 3.03 us -> 2.44 us  [sibling(): return lax.ppermute(value, 'tensor', [(0, 1), (1, 0)])]
    ppermute x9 -> x10, starting transfers between devices: 13.9 us -> 13.6 us  [swap(): lax.ppermute(value, 'expert', [(i, i ^ offset) for i in range(count)])]
  transfers between devices with their start and end apart: 13 -> 15, of which waited for: 8 -> 8; matrix products, arithmetic and copies ran while one was open for 3% -> 1% of each run, Pallas kernels for 8% -> 32%
where the time goes in v2:
time: 47.4 us; the launch traced here: 47.3 us
  Pallas kernels  17.3 us (36%)
  waiting for transfers between devices  14.7 us (31%)
  starting transfers between devices  14 us (30%)
  between operations  0.87 us (2%)
    ppermute x10, starting transfers between devices, swap(): lax.ppermute(value, 'expert', [(i, i ^ offset) for i in range(count)])  13.6 us
    ppermute x10, waiting for transfers between devices, swap(): lax.ppermute(value, 'expert', [(i, i ^ offset) for i in range(count)])  12.3 us
    pallas_call x2, Pallas kernels, fetch(): pl.pallas_call(weight_kernel, out_shape=[pltpu.VMEM(weight.shape, weight....  5.73 us
    pallas_call x2, Pallas kernels, down(): call(functools.partial(down_kernel, steps, tokens, first), struct((half,...  2.82 us
    ppermute x4, waiting for transfers between devices, sibling(): return lax.ppermute(value, 'tensor', [(0, 1), (1, 0)])  2.44 us
    pallas_call x1, Pallas kernels, fast_shards(): call(functools.partial(resample_kernel, steps, early), (out, out), [SMEM]...  2.01 us
    pallas_call x1, Pallas kernels, fast_shards(): call(functools.partial(attend_kernel, steps, experts), (struct((rows, mai...  1.75 us
    pallas_call x1, Pallas kernels, fast_shards(): call(functools.partial(hidden_kernel, steps, tokens, experts), struct((co...  1.51 us
  transfers between devices with their start and end apart: 15, of which 8 were waited for; matrix products, arithmetic and copies ran while one was open for 1% of the time, Pallas kernels for 32%

profile of v2, /device:TPU:0, one launch (start us, length us, event | category | flops | bytes accessed | tf_op | source)
XLA Modules:
  0.0 47.3 jit_solution(14953171711751611880)
XLA Ops:
  0.6 1.3 %load.1 = (s32[3,4,8]{2,1,0:T(4,128)S(1)}, f32[3,4,8]{2,1,0:T(4,128)S(1)}, s32[4]{0:T(128)S(4)}, f32[1,4096]{1,0:T(1,128)S(1)}, bf16[3,4,4096]{2,1,0:T(4,128)(2,...) custom-call(s32[3,4,8]{2,1,0:T(4,128)} %ids_in.1, ...), custom_call_target="tpu_custom_call" | custom-call | tf_op jit(solution)/shard_map/load/pallas_call | solution.py:393
  1.9 3.0 %collective-permute-start.3 = (bf16[10,136,128]{2,1,0:T(8,128)(2,1)S(1)}, bf16[10,136,128]{2,1,0:T(8,128)(2,1)S(1)}, u32[]{:S(2)}, u32[]{:S(2)}) collective-permute-start(bf16[10,136,128]{2,1,0:T(8,128)(2,1)S(1)} %get-tuple-element.48), channel_id=1, source_target_pairs={{0,2},{2,0},{4,6},{6,4},{8,10},{10,8},{12,14},{14,12},{1,3},{3,1},... | collective-permute-start | bytes 1044488 | tf_op jit(solution)/shard_map/ppermute | solution.py:386
  4.9 1.8 %attend.1 = (bf16[16,1664]{1,0:T(8,128)(2,1)S(1)}, f32[16,1536]{1,0:T(8,128)S(1)}) custom-call(s32[3,4,8]{2,1,0:T(4,128)S(1)} %get-tuple-element.36.ids_ref, f32[3,4,8]{2,1,0:T(4,128)S(1)} %get-tuple-element.37.weights_ref, s32[4]{0:T(128)S(4)} %get-tuple-element.38.counts_ref, f32[1,4096]{1,0:T(1,128)S(1)} %get-tuple-element.39.gain_ref, ...), custom_call_target="tpu_custom_call" | custom-call | bytes 8049999 | tf_op jit(solution)/shard_map/attend/pallas_call | solution.py:403
  6.7 1.6 %collective-permute-start = (bf16[16,1664]{1,0:T(8,128)(2,1)S(1)}, bf16[16,1664]{1,0:T(8,128)(2,1)S(1)}, u32[]{:S(2)}, u32[]{:S(2)}) collective-permute-start(bf16[16,1664]{1,0:T(8,128)(2,1)S(1)} %get-tuple-element.47), channel_id=1, source_target_pairs={{0,4},{2,6},{4,0},{6,2},{8,12},{10,14},{12,8},{14,10},{1,5},{3,7},... | collective-permute-start | bytes 159752 | tf_op jit(solution)/shard_map/ppermute | solution.py:386
  8.3 2.6 %collective-permute-start.1 = (bf16[16,1664]{1,0:T(8,128)(2,1)S(1)}, bf16[16,1664]{1,0:T(8,128)(2,1)S(1)}, u32[]{:S(2)}, u32[]{:S(2)}) collective-permute-start(bf16[16,1664]{1,0:T(8,128)(2,1)S(1)} %get-tuple-element.47), channel_id=1, source_target_pairs={{0,8},{2,10},{4,12},{6,14},{8,0},{10,2},{12,4},{14,6},{1,9},{3,11}... | collective-permute-start | bytes 159752 | tf_op jit(solution)/shard_map/ppermute | solution.py:386
  10.9 0.2 collective-permute-start.2
  11.1 2.9 %gate.1 = (bf16[2,4096,384]{2,1,0:T(8,128)(2,1)S(1)}, f32[8,128]{1,0:T(8,128)S(1)}) custom-call(f32[16,1536]{1,0:T(8,128)S(1)} %get-tuple-element.46.after_ref.refs_0_, bf16[2,4096,384]{2,1,0:T(8,128)(2,1)} %source.2), custom_call_target="tpu_custom_call" | custom-call | bytes 7000000 | tf_op jit(solution)/shard_map/gate/pallas_call | solution.py:410
  14.0 0.0 collective-permute-done
  14.0 0.1 collective-permute-done.1
  14.1 2.7 %collective-permute-done.2 = bf16[16,1664]{1,0:T(8,128)(2,1)S(1)} collective-permute-done((bf16[16,1664]{1,0:T(8,128)(2,1)S(1)}, bf16[16,1664]{1,0:T(8,128)(2,1)S(1)}, u32[]{:S(2)}, u32[]{:S(2)}) %collective-permute-start.2) | collective-permute-done | bytes 53280 | tf_op jit(solution)/shard_map/ppermute | solution.py:386
  16.9 0.0 collective-permute-done.3.near_ref
  16.9 0.0 copy-start
  16.9 0.6 %collective-permute-start.4 = (bf16[64,1664]{1,0:T(8,128)(2,1)S(1)}, bf16[64,1664]{1,0:T(8,128)(2,1)S(1)}, u32[]{:S(2)}, u32[]{:S(2)}) collective-permute-start(bf16[64,1664]{1,0:T(8,128)(2,1)S(1)} %pad_maximum_fusion.1.after_ref.even_ref), channel_id=1, source_target_pairs={{0,2},{2,0},{4,6},{6,4},{8,10},{10,8},{12,14},{14,12},{1,3},{3,1},... | collective-permute-start | bytes 638984 | tf_op jit(solution)/shard_map/ppermute | solution.py:386
  17.5 0.0 collective-permute-start.5
  17.5 2.9 %up.1 = (bf16[2,4096,384]{2,1,0:T(8,128)(2,1)S(1)}, f32[8,128]{1,0:T(8,128)S(1)}) custom-call(bf16[64,1664]{1,0:T(8,128)(2,1)S(1)} %pad_maximum_fusion.1.after_ref.even_ref, bf16[2,4096,384]{2,1,0:T(8,128)(2,1)} %source.3), custom_call_target="tpu_custom_call" | custom-call | bytes 7000000 | tf_op jit(solution)/shard_map/up/pallas_call | solution.py:410
  20.4 2.4 %collective-permute-done.4.odd_ref = bf16[64,1664]{1,0:T(8,128)(2,1)S(1)} collective-permute-done((bf16[64,1664]{1,0:T(8,128)(2,1)S(1)}, bf16[64,1664]{1,0:T(8,128)(2,1)S(1)}, u32[]{:S(2)}, u32[]{:S(2)}) %collective-permute-start.4) | collective-permute-done | bytes 213024 | tf_op jit(solution)/shard_map/ppermute | solution.py:386
  22.8 0.0 collective-permute-start.6
  22.8 0.5 %collective-permute-start.8 = (bf16[6,136,128]{2,1,0:T(8,128)(2,1)S(1)}, bf16[6,136,128]{2,1,0:T(8,128)(2,1)S(1)}, u32[]{:S(2)}, u32[]{:S(2)}) collective-permute-start(bf16[6,136,128]{2,1,0:T(8,128)(2,1)S(1)} %get-tuple-element.58), channel_id=1, source_target_pairs={{0,2},{2,0},{4,6},{6,4},{8,10},{10,8},{12,14},{14,12},{1,3},{3,1},... | collective-permute-start | bytes 626696 | tf_op jit(solution)/shard_map/ppermute | solution.py:386
  23.3 1.5 %partial.1.partial_ref = f32[4,128,384]{2,1,0:T(8,128)S(1)} custom-call(f32[8,128]{1,0:T(8,128)S(1)} %get-tuple-element.50.after_ref, f32[8,128]{1,0:T(8,128)S(1)} %get-tuple-element.54.also_after_ref, bf16[64,1664]{1,0:T(8,128)(2,1)S(1)} %pad_maximum_fusion.1.after_ref.even_ref, bf16[64,1664]{1,0:T(8,128)(2,1)S(1)} %collective-permute-done.4.odd_ref, ...), custom_call_target="tpu_custom_call" | custom-call | bytes 35000 | tf_op jit(solution)/shard_map/partial/pallas_call | solution.py:426
  24.8 0.0 slice-start.1
  24.8 0.0 collective-permute-done.5.even_other_ref
  24.8 0.0 collective-permute-done.6.odd_other_ref
  24.8 1.5 %hidden.1.own_ref = bf16[128,768]{1,0:T(8,128)(2,1)S(1)} custom-call(f32[4,128,384]{2,1,0:T(8,128)S(1)} %partial.1.partial_ref, bf16[64,1664]{1,0:T(8,128)(2,1)S(1)} %pad_maximum_fusion.1.after_ref.even_ref, bf16[64,1664]{1,0:T(8,128)(2,1)S(1)} %collective-permute-done.4.odd_ref, bf16[64,1664]{1,0:T(8,128)(2,1)S(1)} %collective-permute-done.5.even_other_ref, ...), custom_call_target="tpu_custom_call" | custom-call | bytes 35000 | tf_op jit(solution)/shard_map/hidden/pallas_call | solution.py:429
  26.4 0.3 collective-permute-start.7
  26.7 1.2 %collective-permute-done.7.other_ref = bf16[128,768]{1,0:T(8,128)(2,1)S(1)} collective-permute-done((bf16[128,768]{1,0:T(8,128)(2,1)S(1)}, bf16[128,768]{1,0:T(8,128)(2,1)S(1)}, u32[]{:S(2)}, u32[]{:S(2)}) %collective-permute-start.7) | collective-permute-done | bytes 196640 | tf_op jit(solution)/shard_map/ppermute | solution.py:389
  27.9 0.0 slice-done
  27.9 0.0 slice-done.1
  27.9 1.4 %down.3 = bf16[64,1536]{1,0:T(8,128)(2,1)S(1)} custom-call(bf16[128,768]{1,0:T(8,128)(2,1)S(1)} %hidden.1.own_ref, bf16[128,768]{1,0:T(8,128)(2,1)S(1)} %collective-permute-done.7.other_ref, bf16[2,768,2048]{2,1,0:T(8,128)(2,1)S(1)} %bitcast.8), custom_call_target="tpu_custom_call" | custom-call | bytes 35000 | tf_op jit(solution)/shard_map/down/pallas_call | solution.py:437
  29.3 1.1 %collective-permute-done.8 = bf16[6,136,128]{2,1,0:T(8,128)(2,1)S(1)} collective-permute-done((bf16[6,136,128]{2,1,0:T(8,128)(2,1)S(1)}, bf16[6,136,128]{2,1,0:T(8,128)(2,1)S(1)}, u32[]{:S(2)}, u32[]{:S(2)}) %collective-permute-start.8) | collective-permute-done | bytes 208928 | tf_op jit(solution)/shard_map/ppermute | solution.py:386
  30.4 0.5 %collective-permute-start.9 = (bf16[64,1536]{1,0:T(8,128)(2,1)S(1)}, bf16[64,1536]{1,0:T(8,128)(2,1)S(1)}, u32[]{:S(2)}, u32[]{:S(2)}) collective-permute-start(bf16[64,1536]{1,0:T(8,128)(2,1)S(1)} %down.3), channel_id=1, source_target_pairs={{0,2},{2,0},{4,6},{6,4},{8,10},{10,8},{12,14},{14,12},{1,3},{3,1},... | collective-permute-start | bytes 589832 | tf_op jit(solution)/shard_map/ppermute | solution.py:386
  30.9 0.0 copy-done
  30.9 1.4 %down.2 = f32[64,1536]{1,0:T(8,128)S(1)} custom-call(bf16[128,768]{1,0:T(8,128)(2,1)S(1)} %hidden.1.own_ref, bf16[128,768]{1,0:T(8,128)(2,1)S(1)} %collective-permute-done.7.other_ref, bf16[2,768,2048]{2,1,0:T(8,128)(2,1)S(1)} %bitcast.8), custom_call_target="tpu_custom_call" | custom-call | bytes 35000 | tf_op jit(solution)/shard_map/down/pallas_call | solution.py:437
  32.4 0.0 slice-done.2
  32.4 0.1 collective-permute-start.10
  32.5 5.7 %collective-permute-done.9 = bf16[64,1536]{1,0:T(8,128)(2,1)S(1)} collective-permute-done((bf16[64,1536]{1,0:T(8,128)(2,1)S(1)}, bf16[64,1536]{1,0:T(8,128)(2,1)S(1)}, u32[]{:S(2)}, u32[]{:S(2)}) %collective-permute-start.9) | collective-permute-done | bytes 196640 | tf_op jit(solution)/shard_map/ppermute | solution.py:386
  38.3 0.1 collective-permute-start.11
  38.3 0.1 collective-permute-start.12
  38.4 4.3 %collective-permute-start.13 = (bf16[16,1536]{1,0:T(8,128)(2,1)S(1)}, bf16[16,1536]{1,0:T(8,128)(2,1)S(1)}, u32[]{:S(2)}, u32[]{:S(2)}) collective-permute-start(bf16[16,1536]{1,0:T(8,128)(2,1)S(1)} %get-tuple-element.69), channel_id=1, source_target_pairs={{0,12},{2,14},{4,8},{6,10},{8,4},{10,6},{12,0},{14,2},{1,13},{3,15... | collective-permute-start | bytes 147464 | tf_op jit(solution)/shard_map/ppermute | solution.py:386
  42.7 0.3 convert_reduce_fusion
  43.0 0.0 collective-permute-done.10.relay_ref
  43.1 0.0 copy-done.1
  43.1 2.0 %resample.1 = (bf16[4,131,2,128]{3,2,1,0:T(2,128)(2,1)}, bf16[4,131,2,128]{3,2,1,0:T(2,128)(2,1)}) custom-call(s32[8,4]{1,0:T(8,128)S(1)} %bitcast.11, bf16[10,136,128]{2,1,0:T(8,128)(2,1)S(1)} %copy-done.1, bf16[8,136,128]{2,1,0:T(8,128)(2,1)S(1)} %collective-permute-done.10.relay_ref, bf16[4,2,128,128]{3,2,1,0:T(8,128)(2,1)S(1)} %get-tuple-element.44.ck_ref, ...), custom_call_target="tpu_custom_call" | custom-call | bytes 7700000 | tf_op jit(solution)/shard_map/resample/pallas_call | solution.py:451
  45.1 0.0 collective-permute-done.11.refs_3_
  45.1 0.0 collective-permute-done.12.refs_4_
  45.1 0.2 collective-permute-done.13.refs_5_
  45.3 0.1 collective-permute-start.14
  45.4 1.2 %collective-permute-done.14.other_ref = bf16[16,1536]{1,0:T(8,128)(2,1)S(1)} collective-permute-done((bf16[16,1536]{1,0:T(8,128)(2,1)S(1)}, bf16[16,1536]{1,0:T(8,128)(2,1)S(1)}, u32[]{:S(2)}, u32[]{:S(2)}) %collective-permute-start.14) | collective-permute-done | bytes 49184 | tf_op jit(solution)/shard_map/ppermute | solution.py:389
  46.6 0.7 %unpack.1 = bf16[3,4,4096]{2,1,0:T(4,128)(2,1)} custom-call(bf16[16,1536]{1,0:T(8,128)(2,1)S(1)} %total.1.own_ref, bf16[16,1536]{1,0:T(8,128)(2,1)S(1)} %collective-permute-done.14.other_ref), custom_call_target="tpu_custom_call" | custom-call | bytes 1750000 | tf_op jit(solution)/shard_map/unpack/pallas_call | solution.py:459
  (14 shorter events, 0.2 us)
Async XLA Ops:
  1.9 15.0 %collective-permute-start.3 = (bf16[10,136,128]{2,1,0:T(8,128)(2,1)S(1)}, bf16[10,136,128]{2,1,0:T(8,128)(2,1)S(1)}, u32[]{:S(2)}, u32[]{:S(2)}) collective-permute-start(bf16[10,136,128]{2,1,0:T(8,128)(2,1)S(1)} %get-tuple-element.48), channel_id=1, source_target_pairs={{0,2},{2,0},{4,6},{6,4},{8,10},{10,8},{12,14},{14,12},{1,3},{3,1},... | collective-permute-start | bytes 1044488 | tf_op jit(solution)/shard_map/ppermute | solution.py:386
  6.7 7.3 %collective-permute-start = (bf16[16,1664]{1,0:T(8,128)(2,1)S(1)}, bf16[16,1664]{1,0:T(8,128)(2,1)S(1)}, u32[]{:S(2)}, u32[]{:S(2)}) collective-permute-start(bf16[16,1664]{1,0:T(8,128)(2,1)S(1)} %get-tuple-element.47), channel_id=1, source_target_pairs={{0,4},{2,6},{4,0},{6,2},{8,12},{10,14},{12,8},{14,10},{1,5},{3,7},... | collective-permute-start | bytes 159752 | tf_op jit(solution)/shard_map/ppermute | solution.py:386
  8.3 5.8 %collective-permute-start.1 = (bf16[16,1664]{1,0:T(8,128)(2,1)S(1)}, bf16[16,1664]{1,0:T(8,128)(2,1)S(1)}, u32[]{:S(2)}, u32[]{:S(2)}) collective-permute-start(bf16[16,1664]{1,0:T(8,128)(2,1)S(1)} %get-tuple-element.47), channel_id=1, source_target_pairs={{0,8},{2,10},{4,12},{6,14},{8,0},{10,2},{12,4},{14,6},{1,9},{3,11}... | collective-permute-start | bytes 159752 | tf_op jit(solution)/shard_map/ppermute | solution.py:386
  10.9 5.9 %collective-permute-start.2 = (bf16[16,1664]{1,0:T(8,128)(2,1)S(1)}, bf16[16,1664]{1,0:T(8,128)(2,1)S(1)}, u32[]{:S(2)}, u32[]{:S(2)}) collective-permute-start(bf16[16,1664]{1,0:T(8,128)(2,1)S(1)} %get-tuple-element.47), channel_id=1, source_target_pairs={{0,12},{2,14},{4,8},{6,10},{8,4},{10,6},{12,0},{14,2},{1,13},{3,15... | collective-permute-start | bytes 159752 | tf_op jit(solution)/shard_map/ppermute | solution.py:386
  16.9 14.0 %copy-start = (bf16[10,136,128]{2,1,0:T(8,128)(2,1)}, bf16[10,136,128]{2,1,0:T(8,128)(2,1)S(1)}, u32[]{:S(2)}) copy-start(bf16[10,136,128]{2,1,0:T(8,128)(2,1)S(1)} %collective-permute-done.3.near_ref) | copy-start | bytes 1044484
  16.9 5.9 %collective-permute-start.4 = (bf16[64,1664]{1,0:T(8,128)(2,1)S(1)}, bf16[64,1664]{1,0:T(8,128)(2,1)S(1)}, u32[]{:S(2)}, u32[]{:S(2)}) collective-permute-start(bf16[64,1664]{1,0:T(8,128)(2,1)S(1)} %pad_maximum_fusion.1.after_ref.even_ref), channel_id=1, source_target_pairs={{0,2},{2,0},{4,6},{6,4},{8,10},{10,8},{12,14},{14,12},{1,3},{3,1},... | collective-permute-start | bytes 638984 | tf_op jit(solution)/shard_map/ppermute | solution.py:386
  17.5 7.3 %collective-permute-start.5 = (bf16[64,1664]{1,0:T(8,128)(2,1)S(1)}, bf16[64,1664]{1,0:T(8,128)(2,1)S(1)}, u32[]{:S(2)}, u32[]{:S(2)}) collective-permute-start(bf16[64,1664]{1,0:T(8,128)(2,1)S(1)} %pad_maximum_fusion.1.after_ref.even_ref), channel_id=1, source_target_pairs={{0,1},{1,0},{2,3},{3,2},{4,5},{5,4},{6,7},{7,6},{8,9},{9,8},{10,11... | collective-permute-start | bytes 638984 | tf_op jit(solution)/shard_map/ppermute | solution.py:389
  22.8 2.0 %collective-permute-start.6 = (bf16[64,1664]{1,0:T(8,128)(2,1)S(1)}, bf16[64,1664]{1,0:T(8,128)(2,1)S(1)}, u32[]{:S(2)}, u32[]{:S(2)}) collective-permute-start(bf16[64,1664]{1,0:T(8,128)(2,1)S(1)} %collective-permute-done.4.odd_ref), channel_id=1, source_target_pairs={{0,1},{1,0},{2,3},{3,2},{4,5},{5,4},{6,7},{7,6},{8,9},{9,8},{10,11... | collective-permute-start | bytes 638984 | tf_op jit(solution)/shard_map/ppermute | solution.py:389
  22.8 7.6 %collective-permute-start.8 = (bf16[6,136,128]{2,1,0:T(8,128)(2,1)S(1)}, bf16[6,136,128]{2,1,0:T(8,128)(2,1)S(1)}, u32[]{:S(2)}, u32[]{:S(2)}) collective-permute-start(bf16[6,136,128]{2,1,0:T(8,128)(2,1)S(1)} %get-tuple-element.58), channel_id=1, source_target_pairs={{0,2},{2,0},{4,6},{6,4},{8,10},{10,8},{12,14},{14,12},{1,3},{3,1},... | collective-permute-start | bytes 626696 | tf_op jit(solution)/shard_map/ppermute | solution.py:386
  23.3 4.5 %slice-start = ((s8[6291456]{0:T(1024)(128)(4,1)}), s8[4194304]{0:T(1024)(128)(4,1)S(1)}, s32[]{:S(2)}) async-start(s8[6291456]{0:T(1024)(128)(4,1)} %bitcast.7), calls=%async_computation | async-start | bytes 8388608
  24.8 3.1 %slice-start.1 = ((s8[6291456]{0:T(1024)(128)(4,1)}), s8[2097152]{0:T(1024)(128)(4,1)S(1)}, s32[]{:S(2)}) async-start(s8[6291456]{0:T(1024)(128)(4,1)} %bitcast.7), calls=%async_computation.1 | async-start | bytes 4194304
  26.4 1.5 %collective-permute-start.7 = (bf16[128,768]{1,0:T(8,128)(2,1)S(1)}, bf16[128,768]{1,0:T(8,128)(2,1)S(1)}, u32[]{:S(2)}, u32[]{:S(2)}) collective-permute-start(bf16[128,768]{1,0:T(8,128)(2,1)S(1)} %hidden.1.own_ref), channel_id=1, source_target_pairs={{0,1},{1,0},{2,3},{3,2},{4,5},{5,4},{6,7},{7,6},{8,9},{9,8},{10,11... | collective-permute-start | bytes 589832 | tf_op jit(solution)/shard_map/ppermute | solution.py:389
  30.4 7.8 %collective-permute-start.9 = (bf16[64,1536]{1,0:T(8,128)(2,1)S(1)}, bf16[64,1536]{1,0:T(8,128)(2,1)S(1)}, u32[]{:S(2)}, u32[]{:S(2)}) collective-permute-start(bf16[64,1536]{1,0:T(8,128)(2,1)S(1)} %down.3), channel_id=1, source_target_pairs={{0,2},{2,0},{4,6},{6,4},{8,10},{10,8},{12,14},{14,12},{1,3},{3,1},... | collective-permute-start | bytes 589832 | tf_op jit(solution)/shard_map/ppermute | solution.py:386
  30.9 1.5 %slice-start.2 = ((bf16[10,136,128]{2,1,0:T(8,128)(2,1)}), bf16[2,136,128]{2,1,0:T(8,128)(2,1)S(1)}, s32[]{:S(2)}) async-start(bf16[10,136,128]{2,1,0:T(8,128)(2,1)} %copy-done), calls=%async_computation.2 | async-start | bytes 139264 | tf_op jit(solution)/shard_map/slice | solution.py:444
  30.9 12.1 %copy-start.1 = (bf16[10,136,128]{2,1,0:T(8,128)(2,1)S(1)}, bf16[10,136,128]{2,1,0:T(8,128)(2,1)}, u32[]{:S(2)}) copy-start(bf16[10,136,128]{2,1,0:T(8,128)(2,1)} %copy-done) | copy-start | bytes 1044484
  32.4 10.6 %collective-permute-start.10 = (bf16[8,136,128]{2,1,0:T(8,128)(2,1)S(1)}, bf16[8,136,128]{2,1,0:T(8,128)(2,1)S(1)}, u32[]{:S(2)}, u32[]{:S(2)}) collective-permute-start(bf16[8,136,128]{2,1,0:T(8,128)(2,1)S(1)} %pad_maximum_fusion), channel_id=1, source_target_pairs={{0,4},{2,0},{4,8},{6,2},{8,12},{10,6},{12,14},{14,10},{1,5},{3,1},... | collective-permute-start | bytes 835592 | tf_op jit(solution)/shard_map/ppermute | solution.py:444
  38.3 6.8 %collective-permute-start.11 = (bf16[16,1536]{1,0:T(8,128)(2,1)S(1)}, bf16[16,1536]{1,0:T(8,128)(2,1)S(1)}, u32[]{:S(2)}, u32[]{:S(2)}) collective-permute-start(bf16[16,1536]{1,0:T(8,128)(2,1)S(1)} %get-tuple-element.71), channel_id=1, source_target_pairs={{0,4},{2,6},{4,0},{6,2},{8,12},{10,14},{12,8},{14,10},{1,5},{3,7},... | collective-permute-start | bytes 147464 | tf_op jit(solution)/shard_map/ppermute | solution.py:386
  38.3 6.7 %collective-permute-start.12 = (bf16[16,1536]{1,0:T(8,128)(2,1)S(1)}, bf16[16,1536]{1,0:T(8,128)(2,1)S(1)}, u32[]{:S(2)}, u32[]{:S(2)}) collective-permute-start(bf16[16,1536]{1,0:T(8,128)(2,1)S(1)} %get-tuple-element.70), channel_id=1, source_target_pairs={{0,8},{2,10},{4,12},{6,14},{8,0},{10,2},{12,4},{14,6},{1,9},{3,11}... | collective-permute-start | bytes 147464 | tf_op jit(solution)/shard_map/ppermute | solution.py:386
  38.4 6.9 %collective-permute-start.13 = (bf16[16,1536]{1,0:T(8,128)(2,1)S(1)}, bf16[16,1536]{1,0:T(8,128)(2,1)S(1)}, u32[]{:S(2)}, u32[]{:S(2)}) collective-permute-start(bf16[16,1536]{1,0:T(8,128)(2,1)S(1)} %get-tuple-element.69), channel_id=1, source_target_pairs={{0,12},{2,14},{4,8},{6,10},{8,4},{10,6},{12,0},{14,2},{1,13},{3,15... | collective-permute-start | bytes 147464 | tf_op jit(solution)/shard_map/ppermute | solution.py:386
  45.3 1.3 %collective-permute-start.14 = (bf16[16,1536]{1,0:T(8,128)(2,1)S(1)}, bf16[16,1536]{1,0:T(8,128)(2,1)S(1)}, u32[]{:S(2)}, u32[]{:S(2)}) collective-permute-start(bf16[16,1536]{1,0:T(8,128)(2,1)S(1)} %total.1.own_ref), channel_id=1, source_target_pairs={{0,1},{1,0},{2,3},{3,2},{4,5},{5,4},{6,7},{7,6},{8,9},{9,8},{10,11... | collective-permute-start | bytes 147464 | tf_op jit(solution)/shard_map/ppermute | solution.py:389

commit v3 on v2

--- a/solution.py
+++ b/solution.py
@@ -251,24 +251,25 @@
         out_ref[:, e * units : (e + 1) * units] = hidden.astype(bf16)
 
 
-def down_kernel(steps, tokens, begin, own_ref, other_ref, down_ref, out_ref):
-    total, width = out_ref.shape[0], own_ref.shape[1]
+def down_kernel(steps, tokens, own_ref, other_ref, down_ref, kept_ref, leaving_ref):
+    total, width = own_ref.shape
     local, _, columns = down_ref.shape
     units = width // local
     rows = (steps + 1) * tokens
     part = columns // (steps + 1)
     main = steps * part
-    blocks = total // rows
     mine = lax.axis_index("tensor")
     product = 0.0
     for ref, half in ((own_ref, mine), (other_ref, 1 - mine)):
         start = pl.multiple_of(half * units, LANES)
         for e in range(local):
-            product += dot(ref[begin : begin + total, e * units : (e + 1) * units], down_ref[e, pl.ds(start, units), :])
+            product += dot(ref[:, e * units : (e + 1) * units], down_ref[e, pl.ds(start, units), :])
     last = product[:, main:].astype(bf16)
-    extra = jnp.concatenate([dot(unpacking(blocks, steps, tokens, s, True), last) for s in range(steps)], axis=1)
+    extra = jnp.concatenate([dot(unpacking(total // rows, steps, tokens, s, True), last) for s in range(steps)], axis=1)
     in_main = lax.rem(iota((total, main), 0), rows) < steps * tokens
-    out_ref[...] = jnp.where(in_main, product[:, :main], extra).astype(out_ref.dtype)
+    product = jnp.where(in_main, product[:, :main], extra)
+    kept_ref[...] = product[: total // 2]
+    leaving_ref[...] = product[total // 2 :].astype(bf16)
 
 
 def resample_kernel(steps, early, counts_ref, near_ref, relay_ref, ck_ref, cv_ref, nk_ref, nv_ref, keys_ref, values_ref):
@@ -433,16 +434,13 @@
     other_hidden = sibling(hidden)
     half = count // 2 * rows
 
-    def down(first, dtype):
-        return call(
-            functools.partial(down_kernel, steps, tokens, first), struct((half, main), dtype), [VMEM] * 3, "down", 0.01,
-        )(hidden, other_hidden, down_weight)
-
-    leaving, relayed = lax.optimization_barrier((down(half, bf16), relayed))
+    kept, leaving = call(
+        functools.partial(down_kernel, steps, tokens), (struct((half, main), f32), struct((half, main), bf16)), [VMEM] * 3, "down", 0.01,
+    )(hidden, other_hidden, down_weight)
+    leaving, relayed = lax.optimization_barrier((leaving, relayed))
     arrived = swap(leaving, 1)
-    ring = [(i, min(i + 2, count - 1) if i % 2 == 0 else max(i - 2, 0)) for i in range(count)]
+    ring = [(i, i + 2 if i % 2 == 0 else i - 2) for i in range(count) if (i < count - 2 if i % 2 == 0 else i > 1)]
     far = lax.ppermute(jnp.concatenate([near[2 * per :], relayed], axis=0), "expert", ring)
-    kept = down(0, f32)
     own_block, others = kept[:rows], call(add_kernel, struct((half - rows, main), bf16), [VMEM] * 2, "add", 0.1)(kept[rows:], arrived[rows:])
 
     counts = jnp.stack([even, odd], 0).reshape(2, count // 2, rows, main + LANES)[:, :, :tokens, main + 2 * experts + 2].astype(jnp.int32)

time: 47.4 us -> 46.5 us (0.981)
  Pallas kernels: 17.3 us -> 15.9 us
  starting transfers between devices: 14 us -> 15.3 us
  waiting for transfers between devices: 14.7 us -> 13.8 us
    pallas_call x2 -> x1, Pallas kernels: 2.82 us -> 1.49 us  [fast_shards(): call(functools.partial(down_kernel, steps, tokens), (struct((half, main),...]
    ppermute x1, starting transfers between devices: 0.06 us -> 1.31 us  [fast_shards(): lax.ppermute(jnp.concatenate([near[2 * per:], relayed], axis=0), 'expert'...]
    ppermute x10, waiting for transfers between devices: 12.3 us -> 11.4 us  [swap(): lax.ppermute(value, 'expert', [(i, i ^ offset) for i in range(count)])]
  transfers between devices with their start and end apart: 15 -> 15, of which waited for: 8 -> 8; matrix products, arithmetic and copies ran while one was open for 1% -> 1% of each run, Pallas kernels for 32% -> 30%
where the time goes in v3:
time: 46.5 us; the launch traced here: 46.3 us
  Pallas kernels  15.9 us (34%)
  starting transfers between devices  15.3 us (33%)
  waiting for transfers between devices  13.8 us (30%)
  between operations  0.83 us (2%)
    ppermute x10, starting transfers between devices, swap(): lax.ppermute(value, 'expert', [(i, i ^ offset) for i in range(count)])  13.6 us
    ppermute x10, waiting for transfers between devices, swap(): lax.ppermute(value, 'expert', [(i, i ^ offset) for i in range(count)])  11.4 us
    pallas_call x2, Pallas kernels, fetch(): pl.pallas_call(weight_kernel, out_shape=[pltpu.VMEM(weight.shape, weight....  5.73 us
    ppermute x4, waiting for transfers between devices, sibling(): return lax.ppermute(value, 'tensor', [(0, 1), (1, 0)])  2.42 us
    pallas_call x1, Pallas kernels, fast_shards(): call(functools.partial(resample_kernel, steps, early), (out, out), [SMEM]...  2.01 us
    pallas_call x1, Pallas kernels, fast_shards(): call(functools.partial(attend_kernel, steps, experts), (struct((rows, mai...  1.75 us
    pallas_call x1, Pallas kernels, fast_shards(): call(functools.partial(hidden_kernel, steps, tokens, experts), struct((co...  1.51 us
    pallas_call x1, Pallas kernels, fast_shards(): call(functools.partial(down_kernel, steps, tokens), (struct((half, main),...  1.49 us
  transfers between devices with their start and end apart: 15, of which 8 were waited for; matrix products, arithmetic and copies ran while one was open for 1% of the time, Pallas kernels for 30%

profile of v3, /device:TPU:0, one launch (start us, length us, event | category | flops | bytes accessed | tf_op | source)
XLA Modules:
  0.0 46.3 jit_solution(11449337902961539683)
XLA Ops:
  0.6 1.3 %load.1 = (s32[3,4,8]{2,1,0:T(4,128)S(1)}, f32[3,4,8]{2,1,0:T(4,128)S(1)}, s32[4]{0:T(128)S(4)}, f32[1,4096]{1,0:T(1,128)S(1)}, bf16[3,4,4096]{2,1,0:T(4,128)(2,...) custom-call(s32[3,4,8]{2,1,0:T(4,128)} %ids_in.1, ...), custom_call_target="tpu_custom_call" | custom-call | tf_op jit(solution)/shard_map/load/pallas_call | solution.py:394
  1.9 3.0 %collective-permute-start.3 = (bf16[10,136,128]{2,1,0:T(8,128)(2,1)S(1)}, bf16[10,136,128]{2,1,0:T(8,128)(2,1)S(1)}, u32[]{:S(2)}, u32[]{:S(2)}) collective-permute-start(bf16[10,136,128]{2,1,0:T(8,128)(2,1)S(1)} %get-tuple-element.50), channel_id=1, source_target_pairs={{0,2},{2,0},{4,6},{6,4},{8,10},{10,8},{12,14},{14,12},{1,3},{3,1},... | collective-permute-start | bytes 1044488 | tf_op jit(solution)/shard_map/ppermute | solution.py:387
  4.9 1.8 %attend.1 = (bf16[16,1664]{1,0:T(8,128)(2,1)S(1)}, f32[16,1536]{1,0:T(8,128)S(1)}) custom-call(s32[3,4,8]{2,1,0:T(4,128)S(1)} %get-tuple-element.38.ids_ref, f32[3,4,8]{2,1,0:T(4,128)S(1)} %get-tuple-element.39.weights_ref, s32[4]{0:T(128)S(4)} %get-tuple-element.40.counts_ref, f32[1,4096]{1,0:T(1,128)S(1)} %get-tuple-element.41.gain_ref, ...), custom_call_target="tpu_custom_call" | custom-call | bytes 8049999 | tf_op jit(solution)/shard_map/attend/pallas_call | solution.py:404
  6.7 1.6 %collective-permute-start = (bf16[16,1664]{1,0:T(8,128)(2,1)S(1)}, bf16[16,1664]{1,0:T(8,128)(2,1)S(1)}, u32[]{:S(2)}, u32[]{:S(2)}) collective-permute-start(bf16[16,1664]{1,0:T(8,128)(2,1)S(1)} %get-tuple-element.49), channel_id=1, source_target_pairs={{0,4},{2,6},{4,0},{6,2},{8,12},{10,14},{12,8},{14,10},{1,5},{3,7},... | collective-permute-start | bytes 159752 | tf_op jit(solution)/shard_map/ppermute | solution.py:387
  8.3 2.6 %collective-permute-start.1 = (bf16[16,1664]{1,0:T(8,128)(2,1)S(1)}, bf16[16,1664]{1,0:T(8,128)(2,1)S(1)}, u32[]{:S(2)}, u32[]{:S(2)}) collective-permute-start(bf16[16,1664]{1,0:T(8,128)(2,1)S(1)} %get-tuple-element.49), channel_id=1, source_target_pairs={{0,8},{2,10},{4,12},{6,14},{8,0},{10,2},{12,4},{14,6},{1,9},{3,11}... | collective-permute-start | bytes 159752 | tf_op jit(solution)/shard_map/ppermute | solution.py:387
  10.9 0.2 collective-permute-start.2
  11.1 2.9 %gate.1 = (bf16[2,4096,384]{2,1,0:T(8,128)(2,1)S(1)}, f32[8,128]{1,0:T(8,128)S(1)}) custom-call(f32[16,1536]{1,0:T(8,128)S(1)} %get-tuple-element.48.after_ref.refs_0_, bf16[2,4096,384]{2,1,0:T(8,128)(2,1)} %source.2), custom_call_target="tpu_custom_call" | custom-call | bytes 7000000 | tf_op jit(solution)/shard_map/gate/pallas_call | solution.py:411
  14.0 0.0 collective-permute-done
  14.0 0.1 collective-permute-done.1
  14.1 2.7 %collective-permute-done.2 = bf16[16,1664]{1,0:T(8,128)(2,1)S(1)} collective-permute-done((bf16[16,1664]{1,0:T(8,128)(2,1)S(1)}, bf16[16,1664]{1,0:T(8,128)(2,1)S(1)}, u32[]{:S(2)}, u32[]{:S(2)}) %collective-permute-start.2) | collective-permute-done | bytes 53280 | tf_op jit(solution)/shard_map/ppermute | solution.py:387
  16.9 0.0 collective-permute-done.3.near_ref
  16.9 0.6 %collective-permute-start.4 = (bf16[64,1664]{1,0:T(8,128)(2,1)S(1)}, bf16[64,1664]{1,0:T(8,128)(2,1)S(1)}, u32[]{:S(2)}, u32[]{:S(2)}) collective-permute-start(bf16[64,1664]{1,0:T(8,128)(2,1)S(1)} %pad_maximum_fusion.1.after_ref.even_ref), channel_id=1, source_target_pairs={{0,2},{2,0},{4,6},{6,4},{8,10},{10,8},{12,14},{14,12},{1,3},{3,1},... | collective-permute-start | bytes 638984 | tf_op jit(solution)/shard_map/ppermute | solution.py:387
  17.5 0.0 collective-permute-start.5
  17.5 2.9 %up.1 = (bf16[2,4096,384]{2,1,0:T(8,128)(2,1)S(1)}, f32[8,128]{1,0:T(8,128)S(1)}) custom-call(bf16[64,1664]{1,0:T(8,128)(2,1)S(1)} %pad_maximum_fusion.1.after_ref.even_ref, bf16[2,4096,384]{2,1,0:T(8,128)(2,1)} %source.3), custom_call_target="tpu_custom_call" | custom-call | bytes 7000000 | tf_op jit(solution)/shard_map/up/pallas_call | solution.py:411
  20.4 2.4 %collective-permute-done.4.odd_ref = bf16[64,1664]{1,0:T(8,128)(2,1)S(1)} collective-permute-done((bf16[64,1664]{1,0:T(8,128)(2,1)S(1)}, bf16[64,1664]{1,0:T(8,128)(2,1)S(1)}, u32[]{:S(2)}, u32[]{:S(2)}) %collective-permute-start.4) | collective-permute-done | bytes 213024 | tf_op jit(solution)/shard_map/ppermute | solution.py:387
  22.8 0.0 collective-permute-start.6
  22.8 0.5 %collective-permute-start.8 = (bf16[6,136,128]{2,1,0:T(8,128)(2,1)S(1)}, bf16[6,136,128]{2,1,0:T(8,128)(2,1)S(1)}, u32[]{:S(2)}, u32[]{:S(2)}) collective-permute-start(bf16[6,136,128]{2,1,0:T(8,128)(2,1)S(1)} %get-tuple-element.62), channel_id=1, source_target_pairs={{0,2},{2,0},{4,6},{6,4},{8,10},{10,8},{12,14},{14,12},{1,3},{3,1},... | collective-permute-start | bytes 626696 | tf_op jit(solution)/shard_map/ppermute | solution.py:387
  23.3 0.0 slice-start
  23.3 1.5 %partial.1.partial_ref = f32[4,128,384]{2,1,0:T(8,128)S(1)} custom-call(f32[8,128]{1,0:T(8,128)S(1)} %get-tuple-element.52.after_ref, f32[8,128]{1,0:T(8,128)S(1)} %get-tuple-element.56.also_after_ref, bf16[64,1664]{1,0:T(8,128)(2,1)S(1)} %pad_maximum_fusion.1.after_ref.even_ref, bf16[64,1664]{1,0:T(8,128)(2,1)S(1)} %collective-permute-done.4.odd_ref, ...), custom_call_target="tpu_custom_call" | custom-call | bytes 35000 | tf_op jit(solution)/shard_map/partial/pallas_call | solution.py:427
  24.8 0.0 slice-start.1
  24.8 0.0 collective-permute-done.5.even_other_ref
  24.8 0.0 collective-permute-done.6.odd_other_ref
  24.8 1.5 %hidden.1.own_ref = bf16[128,768]{1,0:T(8,128)(2,1)S(1)} custom-call(f32[4,128,384]{2,1,0:T(8,128)S(1)} %partial.1.partial_ref, bf16[64,1664]{1,0:T(8,128)(2,1)S(1)} %pad_maximum_fusion.1.after_ref.even_ref, bf16[64,1664]{1,0:T(8,128)(2,1)S(1)} %collective-permute-done.4.odd_ref, bf16[64,1664]{1,0:T(8,128)(2,1)S(1)} %collective-permute-done.5.even_other_ref, ...), custom_call_target="tpu_custom_call" | custom-call | bytes 35000 | tf_op jit(solution)/shard_map/hidden/pallas_call | solution.py:430
  26.3 0.3 collective-permute-start.7
  26.7 1.2 %collective-permute-done.7.other_ref = bf16[128,768]{1,0:T(8,128)(2,1)S(1)} collective-permute-done((bf16[128,768]{1,0:T(8,128)(2,1)S(1)}, bf16[128,768]{1,0:T(8,128)(2,1)S(1)}, u32[]{:S(2)}, u32[]{:S(2)}) %collective-permute-start.7) | collective-permute-done | bytes 196640 | tf_op jit(solution)/shard_map/ppermute | solution.py:390
  27.9 0.0 slice-done
  27.9 0.0 slice-done.1
  27.9 1.5 %down.1 = (f32[64,1536]{1,0:T(8,128)S(1)}, bf16[64,1536]{1,0:T(8,128)(2,1)S(1)}) custom-call(bf16[128,768]{1,0:T(8,128)(2,1)S(1)} %hidden.1.own_ref, bf16[128,768]{1,0:T(8,128)(2,1)S(1)} %collective-permute-done.7.other_ref, bf16[2,768,2048]{2,1,0:T(8,128)(2,1)S(1)} %bitcast.8), custom_call_target="tpu_custom_call" | custom-call | bytes 35000 | tf_op jit(solution)/shard_map/down/pallas_call | solution.py:437
  29.4 1.0 %collective-permute-done.8 = bf16[6,136,128]{2,1,0:T(8,128)(2,1)S(1)} collective-permute-done((bf16[6,136,128]{2,1,0:T(8,128)(2,1)S(1)}, bf16[6,136,128]{2,1,0:T(8,128)(2,1)S(1)}, u32[]{:S(2)}, u32[]{:S(2)}) %collective-permute-start.8) | collective-permute-done | bytes 208928 | tf_op jit(solution)/shard_map/ppermute | solution.py:387
  30.4 0.6 %collective-permute-start.9 = (bf16[64,1536]{1,0:T(8,128)(2,1)S(1)}, bf16[64,1536]{1,0:T(8,128)(2,1)S(1)}, u32[]{:S(2)}, u32[]{:S(2)}) collective-permute-start(bf16[64,1536]{1,0:T(8,128)(2,1)S(1)} %get-tuple-element.63), channel_id=1, source_target_pairs={{0,2},{2,0},{4,6},{6,4},{8,10},{10,8},{12,14},{14,12},{1,3},{3,1},... | collective-permute-start | bytes 589832 | tf_op jit(solution)/shard_map/ppermute | solution.py:387
  31.0 1.3 %collective-permute-start.10 = (bf16[8,136,128]{2,1,0:T(8,128)(2,1)S(1)}, bf16[8,136,128]{2,1,0:T(8,128)(2,1)S(1)}, u32[]{:S(2)}, u32[]{:S(2)}) collective-permute-start(bf16[8,136,128]{2,1,0:T(8,128)(2,1)S(1)} %pad_maximum_fusion), channel_id=1, source_target_pairs={{0,4},{4,8},{6,2},{8,12},{10,6},{14,10},{1,5},{5,9},{7,3},{9,13},{... | collective-permute-start | bytes 835592 | tf_op jit(solution)/shard_map/ppermute | solution.py:443
  32.3 4.6 %collective-permute-done.9 = bf16[64,1536]{1,0:T(8,128)(2,1)S(1)} collective-permute-done((bf16[64,1536]{1,0:T(8,128)(2,1)S(1)}, bf16[64,1536]{1,0:T(8,128)(2,1)S(1)}, u32[]{:S(2)}, u32[]{:S(2)}) %collective-permute-start.9) | collective-permute-done | bytes 196640 | tf_op jit(solution)/shard_map/ppermute | solution.py:387
  37.0 0.1 collective-permute-start.11
  37.1 1.4 %collective-permute-start.12 = (bf16[16,1536]{1,0:T(8,128)(2,1)S(1)}, bf16[16,1536]{1,0:T(8,128)(2,1)S(1)}, u32[]{:S(2)}, u32[]{:S(2)}) collective-permute-start(bf16[16,1536]{1,0:T(8,128)(2,1)S(1)} %get-tuple-element.74), channel_id=1, source_target_pairs={{0,8},{2,10},{4,12},{6,14},{8,0},{10,2},{12,4},{14,6},{1,9},{3,11}... | collective-permute-start | bytes 147464 | tf_op jit(solution)/shard_map/ppermute | solution.py:387
  38.4 3.0 %collective-permute-start.13 = (bf16[16,1536]{1,0:T(8,128)(2,1)S(1)}, bf16[16,1536]{1,0:T(8,128)(2,1)S(1)}, u32[]{:S(2)}, u32[]{:S(2)}) collective-permute-start(bf16[16,1536]{1,0:T(8,128)(2,1)S(1)} %get-tuple-element.73), channel_id=1, source_target_pairs={{0,12},{2,14},{4,8},{6,10},{8,4},{10,6},{12,0},{14,2},{1,13},{3,15... | collective-permute-start | bytes 147464 | tf_op jit(solution)/shard_map/ppermute | solution.py:387
  41.4 0.3 convert_reduce_fusion
  41.8 0.0 collective-permute-done.10.relay_ref
  41.8 2.0 %resample.1 = (bf16[4,131,2,128]{3,2,1,0:T(2,128)(2,1)}, bf16[4,131,2,128]{3,2,1,0:T(2,128)(2,1)}) custom-call(s32[8,4]{1,0:T(8,128)S(1)} %bitcast.11, bf16[10,136,128]{2,1,0:T(8,128)(2,1)S(1)} %collective-permute-done.3.near_ref, bf16[8,136,128]{2,1,0:T(8,128)(2,1)S(1)} %collective-permute-done.10.relay_ref, ...), custom_call_target="tpu_custom_call" | custom-call | bytes 7700000 | tf_op jit(solution)/shard_map/resample/pallas_call | solution.py:449
  43.8 0.0 collective-permute-done.11.refs_3_
  43.8 0.0 collective-permute-done.12.refs_4_
  43.8 0.5 %collective-permute-done.13.refs_5_ = bf16[16,1536]{1,0:T(8,128)(2,1)S(1)} collective-permute-done((bf16[16,1536]{1,0:T(8,128)(2,1)S(1)}, bf16[16,1536]{1,0:T(8,128)(2,1)S(1)}, u32[]{:S(2)}, u32[]{:S(2)}) %collective-permute-start.13) | collective-permute-done | bytes 49184 | tf_op jit(solution)/shard_map/ppermute | solution.py:387
  44.4 0.1 collective-permute-start.14
  44.4 1.2 %collective-permute-done.14.other_ref = bf16[16,1536]{1,0:T(8,128)(2,1)S(1)} collective-permute-done((bf16[16,1536]{1,0:T(8,128)(2,1)S(1)}, bf16[16,1536]{1,0:T(8,128)(2,1)S(1)}, u32[]{:S(2)}, u32[]{:S(2)}) %collective-permute-start.14) | collective-permute-done | bytes 49184 | tf_op jit(solution)/shard_map/ppermute | solution.py:390
  45.7 0.7 %unpack.1 = bf16[3,4,4096]{2,1,0:T(4,128)(2,1)} custom-call(bf16[16,1536]{1,0:T(8,128)(2,1)S(1)} %total.1.own_ref, bf16[16,1536]{1,0:T(8,128)(2,1)S(1)} %collective-permute-done.14.other_ref), custom_call_target="tpu_custom_call" | custom-call | bytes 1750000 | tf_op jit(solution)/shard_map/unpack/pallas_call | solution.py:457
  (12 shorter events, 0.2 us)
Async XLA Ops:
  1.9 15.0 %collective-permute-start.3 = (bf16[10,136,128]{2,1,0:T(8,128)(2,1)S(1)}, bf16[10,136,128]{2,1,0:T(8,128)(2,1)S(1)}, u32[]{:S(2)}, u32[]{:S(2)}) collective-permute-start(bf16[10,136,128]{2,1,0:T(8,128)(2,1)S(1)} %get-tuple-element.50), channel_id=1, source_target_pairs={{0,2},{2,0},{4,6},{6,4},{8,10},{10,8},{12,14},{14,12},{1,3},{3,1},... | collective-permute-start | bytes 1044488 | tf_op jit(solution)/shard_map/ppermute | solution.py:387
  6.7 7.3 %collective-permute-start = (bf16[16,1664]{1,0:T(8,128)(2,1)S(1)}, bf16[16,1664]{1,0:T(8,128)(2,1)S(1)}, u32[]{:S(2)}, u32[]{:S(2)}) collective-permute-start(bf16[16,1664]{1,0:T(8,128)(2,1)S(1)} %get-tuple-element.49), channel_id=1, source_target_pairs={{0,4},{2,6},{4,0},{6,2},{8,12},{10,14},{12,8},{14,10},{1,5},{3,7},... | collective-permute-start | bytes 159752 | tf_op jit(solution)/shard_map/ppermute | solution.py:387
  8.3 5.8 %collective-permute-start.1 = (bf16[16,1664]{1,0:T(8,128)(2,1)S(1)}, bf16[16,1664]{1,0:T(8,128)(2,1)S(1)}, u32[]{:S(2)}, u32[]{:S(2)}) collective-permute-start(bf16[16,1664]{1,0:T(8,128)(2,1)S(1)} %get-tuple-element.49), channel_id=1, source_target_pairs={{0,8},{2,10},{4,12},{6,14},{8,0},{10,2},{12,4},{14,6},{1,9},{3,11}... | collective-permute-start | bytes 159752 | tf_op jit(solution)/shard_map/ppermute | solution.py:387
  10.9 5.9 %collective-permute-start.2 = (bf16[16,1664]{1,0:T(8,128)(2,1)S(1)}, bf16[16,1664]{1,0:T(8,128)(2,1)S(1)}, u32[]{:S(2)}, u32[]{:S(2)}) collective-permute-start(bf16[16,1664]{1,0:T(8,128)(2,1)S(1)} %get-tuple-element.49), channel_id=1, source_target_pairs={{0,12},{2,14},{4,8},{6,10},{8,4},{10,6},{12,0},{14,2},{1,13},{3,15... | collective-permute-start | bytes 159752 | tf_op jit(solution)/shard_map/ppermute | solution.py:387
  16.9 5.9 %collective-permute-start.4 = (bf16[64,1664]{1,0:T(8,128)(2,1)S(1)}, bf16[64,1664]{1,0:T(8,128)(2,1)S(1)}, u32[]{:S(2)}, u32[]{:S(2)}) collective-permute-start(bf16[64,1664]{1,0:T(8,128)(2,1)S(1)} %pad_maximum_fusion.1.after_ref.even_ref), channel_id=1, source_target_pairs={{0,2},{2,0},{4,6},{6,4},{8,10},{10,8},{12,14},{14,12},{1,3},{3,1},... | collective-permute-start | bytes 638984 | tf_op jit(solution)/shard_map/ppermute | solution.py:387
  17.5 7.3 %collective-permute-start.5 = (bf16[64,1664]{1,0:T(8,128)(2,1)S(1)}, bf16[64,1664]{1,0:T(8,128)(2,1)S(1)}, u32[]{:S(2)}, u32[]{:S(2)}) collective-permute-start(bf16[64,1664]{1,0:T(8,128)(2,1)S(1)} %pad_maximum_fusion.1.after_ref.even_ref), channel_id=1, source_target_pairs={{0,1},{1,0},{2,3},{3,2},{4,5},{5,4},{6,7},{7,6},{8,9},{9,8},{10,11... | collective-permute-start | bytes 638984 | tf_op jit(solution)/shard_map/ppermute | solution.py:390
  22.8 2.0 %collective-permute-start.6 = (bf16[64,1664]{1,0:T(8,128)(2,1)S(1)}, bf16[64,1664]{1,0:T(8,128)(2,1)S(1)}, u32[]{:S(2)}, u32[]{:S(2)}) collective-permute-start(bf16[64,1664]{1,0:T(8,128)(2,1)S(1)} %collective-permute-done.4.odd_ref), channel_id=1, source_target_pairs={{0,1},{1,0},{2,3},{3,2},{4,5},{5,4},{6,7},{7,6},{8,9},{9,8},{10,11... | collective-permute-start | bytes 638984 | tf_op jit(solution)/shard_map/ppermute | solution.py:390
  22.8 7.6 %collective-permute-start.8 = (bf16[6,136,128]{2,1,0:T(8,128)(2,1)S(1)}, bf16[6,136,128]{2,1,0:T(8,128)(2,1)S(1)}, u32[]{:S(2)}, u32[]{:S(2)}) collective-permute-start(bf16[6,136,128]{2,1,0:T(8,128)(2,1)S(1)} %get-tuple-element.62), channel_id=1, source_target_pairs={{0,2},{2,0},{4,6},{6,4},{8,10},{10,8},{12,14},{14,12},{1,3},{3,1},... | collective-permute-start | bytes 626696 | tf_op jit(solution)/shard_map/ppermute | solution.py:387
  23.3 4.5 %slice-start = ((s8[6291456]{0:T(1024)(128)(4,1)}), s8[4194304]{0:T(1024)(128)(4,1)S(1)}, s32[]{:S(2)}) async-start(s8[6291456]{0:T(1024)(128)(4,1)} %bitcast.7), calls=%async_computation | async-start | bytes 8388608
  24.8 3.1 %slice-start.1 = ((s8[6291456]{0:T(1024)(128)(4,1)}), s8[2097152]{0:T(1024)(128)(4,1)S(1)}, s32[]{:S(2)}) async-start(s8[6291456]{0:T(1024)(128)(4,1)} %bitcast.7), calls=%async_computation.1 | async-start | bytes 4194304
  26.3 1.5 %collective-permute-start.7 = (bf16[128,768]{1,0:T(8,128)(2,1)S(1)}, bf16[128,768]{1,0:T(8,128)(2,1)S(1)}, u32[]{:S(2)}, u32[]{:S(2)}) collective-permute-start(bf16[128,768]{1,0:T(8,128)(2,1)S(1)} %hidden.1.own_ref), channel_id=1, source_target_pairs={{0,1},{1,0},{2,3},{3,2},{4,5},{5,4},{6,7},{7,6},{8,9},{9,8},{10,11... | collective-permute-start | bytes 589832 | tf_op jit(solution)/shard_map/ppermute | solution.py:390
  30.4 6.5 %collective-permute-start.9 = (bf16[64,1536]{1,0:T(8,128)(2,1)S(1)}, bf16[64,1536]{1,0:T(8,128)(2,1)S(1)}, u32[]{:S(2)}, u32[]{:S(2)}) collective-permute-start(bf16[64,1536]{1,0:T(8,128)(2,1)S(1)} %get-tuple-element.63), channel_id=1, source_target_pairs={{0,2},{2,0},{4,6},{6,4},{8,10},{10,8},{12,14},{14,12},{1,3},{3,1},... | collective-permute-start | bytes 589832 | tf_op jit(solution)/shard_map/ppermute | solution.py:387
  31.0 10.8 %collective-permute-start.10 = (bf16[8,136,128]{2,1,0:T(8,128)(2,1)S(1)}, bf16[8,136,128]{2,1,0:T(8,128)(2,1)S(1)}, u32[]{:S(2)}, u32[]{:S(2)}) collective-permute-start(bf16[8,136,128]{2,1,0:T(8,128)(2,1)S(1)} %pad_maximum_fusion), channel_id=1, source_target_pairs={{0,4},{4,8},{6,2},{8,12},{10,6},{14,10},{1,5},{5,9},{7,3},{9,13},{... | collective-permute-start | bytes 835592 | tf_op jit(solution)/shard_map/ppermute | solution.py:443
  37.0 6.8 %collective-permute-start.11 = (bf16[16,1536]{1,0:T(8,128)(2,1)S(1)}, bf16[16,1536]{1,0:T(8,128)(2,1)S(1)}, u32[]{:S(2)}, u32[]{:S(2)}) collective-permute-start(bf16[16,1536]{1,0:T(8,128)(2,1)S(1)} %get-tuple-element.75), channel_id=1, source_target_pairs={{0,4},{2,6},{4,0},{6,2},{8,12},{10,14},{12,8},{14,10},{1,5},{3,7},... | collective-permute-start | bytes 147464 | tf_op jit(solution)/shard_map/ppermute | solution.py:387
  37.1 6.7 %collective-permute-start.12 = (bf16[16,1536]{1,0:T(8,128)(2,1)S(1)}, bf16[16,1536]{1,0:T(8,128)(2,1)S(1)}, u32[]{:S(2)}, u32[]{:S(2)}) collective-permute-start(bf16[16,1536]{1,0:T(8,128)(2,1)S(1)} %get-tuple-element.74), channel_id=1, source_target_pairs={{0,8},{2,10},{4,12},{6,14},{8,0},{10,2},{12,4},{14,6},{1,9},{3,11}... | collective-permute-start | bytes 147464 | tf_op jit(solution)/shard_map/ppermute | solution.py:387
  38.4 5.9 %collective-permute-start.13 = (bf16[16,1536]{1,0:T(8,128)(2,1)S(1)}, bf16[16,1536]{1,0:T(8,128)(2,1)S(1)}, u32[]{:S(2)}, u32[]{:S(2)}) collective-permute-start(bf16[16,1536]{1,0:T(8,128)(2,1)S(1)} %get-tuple-element.73), channel_id=1, source_target_pairs={{0,12},{2,14},{4,8},{6,10},{8,4},{10,6},{12,0},{14,2},{1,13},{3,15... | collective-permute-start | bytes 147464 | tf_op jit(solution)/shard_map/ppermute | solution.py:387
  44.4 1.3 %collective-permute-start.14 = (bf16[16,1536]{1,0:T(8,128)(2,1)S(1)}, bf16[16,1536]{1,0:T(8,128)(2,1)S(1)}, u32[]{:S(2)}, u32[]{:S(2)}) collective-permute-start(bf16[16,1536]{1,0:T(8,128)(2,1)S(1)} %total.1.own_ref), channel_id=1, source_target_pairs={{0,1},{1,0},{2,3},{3,2},{4,5},{5,4},{6,7},{7,6},{8,9},{9,8},{10,11... | collective-permute-start | bytes 147464 | tf_op jit(solution)/shard_map/ppermute | solution.py:390

commit v4 on v3

--- a/solution.py
+++ b/solution.py
@@ -25,9 +25,22 @@
     return lax.broadcasted_iota(jnp.int32, shape, dim)
 
 
+def packing(steps, tokens, heads):
+    rows, per_part = (steps + 1) * tokens, heads // (steps + 1)
+    tiles, count = steps * per_part, tokens * steps * heads
+    target = iota((tiles * rows, count), 0)
+    tile, inner = lax.div(target, rows), lax.rem(target, rows)
+    is_extra = inner >= steps * tokens
+    step = jnp.where(is_extra, lax.div(tile, per_part), lax.div(inner, tokens))
+    token = lax.rem(inner, tokens)
+    head = jnp.where(is_extra, tiles + lax.rem(tile, per_part), tile)
+    chosen = (token * steps + step) * heads + head == iota((tiles * rows, count), 1)
+    return chosen.astype(f32).astype(bf16)
+
+
 def load_kernel(
     steps, ids_in, weights_in, counts_in, gain_in, hidden_in, q_in, nk_in, nv_in, ck_in, cv_in,
-    ids_ref, weights_ref, counts_ref, gain_ref, hidden_ref, q_ref, nk_ref, nv_ref, ck_ref, cv_ref, near_ref, far_ref, sems,
+    ids_ref, weights_ref, counts_ref, gain_ref, hidden_ref, q_ref, nk_ref, nv_ref, ck_ref, cv_ref, chosen_ref, near_ref, far_ref, sems,
 ):
     pairs = (
         (ck_in, ck_ref), (cv_in, cv_ref), (nk_in, nk_ref), (nv_in, nv_ref), (q_in, q_ref), (hidden_in, hidden_ref),
@@ -36,9 +49,10 @@
     copies = [pltpu.make_async_copy(source, target, sems.at[n]) for n, (source, target) in enumerate(pairs)]
     for copy in copies:
         copy.start()
+    tokens, kv_heads, cached, width = ck_ref.shape
+    chosen_ref[...] = packing(steps, tokens, q_ref.shape[2])
     for copy in copies:
         copy.wait()
-    tokens, kv_heads, cached, width = ck_ref.shape
 
     odd = lax.rem(lax.axis_index("expert"), 2)
     per = REACH * kv_heads
@@ -86,7 +100,7 @@
 
 
 def attend_kernel(
-    steps, experts, ids_ref, weights_ref, counts_ref, gain_ref, hidden_ref, q_ref, nk_ref, nv_ref, ck_ref, cv_ref,
+    steps, experts, ids_ref, weights_ref, counts_ref, gain_ref, hidden_ref, q_ref, nk_ref, nv_ref, ck_ref, cv_ref, chosen_ref,
     send_ref, residual_ref, scores_ref,
 ):
     tokens, heads, width = q_ref.shape[1:]
@@ -112,37 +126,28 @@
         & (lax.div(col, kv_heads) <= lax.div(row, heads))
         & (col < fresh)
     )
-    outputs = []
-    for p in range(tokens):
-        q = jnp.concatenate([q_ref[s, p] for s in range(steps)], axis=0)
-
-        def with_new(new_ref):
-            pieces = [new_ref[s, p].astype(f32) for s in range(steps)]
-            return jnp.concatenate(pieces + [jnp.zeros((fresh_rows - fresh, width), f32)], axis=0).astype(bf16)
-
-        keys = ck_ref[p].reshape(kv_heads * cached, width)
-        values = cv_ref[p].reshape(kv_heads * cached, width)
-        old = jnp.where(own_head, dot(q, keys, ((1,), (1,))) * scale, -1e30)
-        new = jnp.where(own_new, dot(q, with_new(nk_ref), ((1,), (1,))) * scale, -1e30)
-        top = jnp.maximum(jnp.max(old, axis=1, keepdims=True), jnp.max(new, axis=1, keepdims=True))
-        old = jnp.exp(old - top)
-        new = jnp.exp(new - top)
-        total = jnp.sum(old, axis=1, keepdims=True) + jnp.sum(new, axis=1, keepdims=True)
-        old = (old / total).astype(bf16)
-        new = (new / total).astype(bf16)
-        outputs.append((dot(old, values) + dot(new, with_new(nv_ref))).astype(bf16))
-    attended = jnp.concatenate(outputs, axis=0)
+    def with_new(new_ref, p):
+        pieces = [new_ref[s, p].astype(f32) for s in range(steps)]
+        return jnp.concatenate(pieces + [jnp.zeros((fresh_rows - fresh, width), f32)], axis=0).astype(bf16)
+
+    every = range(tokens)
+    q = [jnp.concatenate([q_ref[s, p] for s in range(steps)], axis=0) for p in every]
+    old = [dot(q[p], ck_ref[p].reshape(kv_heads * cached, width), ((1,), (1,))) for p in every]
+    new = [dot(q[p], with_new(nk_ref, p), ((1,), (1,))) for p in every]
+    old = [jnp.where(own_head, x * scale, -1e30) for x in old]
+    new = [jnp.where(own_new, x * scale, -1e30) for x in new]
+    top = [jnp.maximum(jnp.max(old[p], axis=1, keepdims=True), jnp.max(new[p], axis=1, keepdims=True)) for p in every]
+    old = [jnp.exp(old[p] - top[p]) for p in every]
+    new = [jnp.exp(new[p] - top[p]) for p in every]
+    inverse = [1.0 / (jnp.sum(old[p], axis=1, keepdims=True) + jnp.sum(new[p], axis=1, keepdims=True)) for p in every]
+    old = [(old[p] * inverse[p]).astype(bf16) for p in every]
+    new = [(new[p] * inverse[p]).astype(bf16) for p in every]
+    attended = jnp.concatenate([
+        (dot(old[p], cv_ref[p].reshape(kv_heads * cached, width)) + dot(new[p], with_new(nv_ref, p))).astype(bf16) for p in every
+    ], axis=0)
 
     tiles = main // width
-    count = tokens * q_rows
-    target = iota((tiles * rows, count), 0)
-    tile, inner = lax.div(target, rows), lax.rem(target, rows)
-    is_extra = inner >= steps * tokens
-    step = jnp.where(is_extra, lax.div(tile, part // width), lax.div(inner, tokens))
-    token = lax.rem(inner, tokens)
-    head = jnp.where(is_extra, tiles + lax.rem(tile, part // width), tile)
-    chosen = (token * q_rows + step * heads + head) == iota((tiles * rows, count), 1)
-    moved = dot(chosen.astype(f32).astype(bf16), attended)
+    moved = dot(chosen_ref[...], attended)
     for s in range(steps):
         residual_ref[s * tokens : (s + 1) * tokens, :] = hidden_ref[s, :, pl.ds(pl.multiple_of(base, LANES), main)].astype(f32)
         residual_ref[steps * tokens :, s * part : (s + 1) * part] = hidden_ref[
@@ -381,6 +386,8 @@
     rows = (steps + 1) * tokens
     per = REACH * kv_heads
     early = 2 * per + per // 2
+    square = steps * tokens * heads
+    chosen = pltpu.VMEM((square, square), bf16)
     halos = [pltpu.VMEM((slots, cached + PAD, width), bf16) for slots in (early, 4 * per - early)]
 
     def swap(value, offset):
@@ -393,20 +400,21 @@
     spaces = [pltpu.SMEM if value is ancestor_counts else pltpu.VMEM for value in inputs]
     loaded = pl.pallas_call(
         functools.partial(load_kernel, steps),
-        out_shape=[space(value.shape, value.dtype) for space, value in zip(spaces, inputs)] + halos,
-        in_specs=[HBM] * len(inputs), out_specs=[pl.BlockSpec(memory_space=space) for space in spaces] + [VMEM] * 2,
+        out_shape=[space(value.shape, value.dtype) for space, value in zip(spaces, inputs)] + [chosen] + halos,
+        in_specs=[HBM] * len(inputs), out_specs=[pl.BlockSpec(memory_space=space) for space in spaces] + [VMEM] * 3,
         scratch_shapes=[pltpu.SemaphoreType.DMA((len(inputs),))], name="load",
         compiler_params=pltpu.CompilerParams(vmem_limit_bytes=20 << 20),
     )(*(in_hbm(value) for value in inputs))
     *loaded, near, far = loaded
     near = swap(near, 1)
-    new_keys, new_values, cache_keys, cache_values = loaded[6:]
+    new_keys, new_values, cache_keys, cache_values = loaded[6:10]
     send, residual = call(
         functools.partial(attend_kernel, steps, experts),
         (struct((rows, main + LANES), bf16), struct((rows, main), f32)),
-        [VMEM, VMEM, SMEM] + [VMEM] * 7, "attend", 2.3, [pltpu.VMEM(((steps + 1) * rows, LANES), f32)],
+        [VMEM, VMEM, SMEM] + [VMEM] * 8, "attend", 2.3, [pltpu.VMEM(((steps + 1) * rows, LANES), f32)],
     )(*loaded)
 
+    far_first = range(count - 2, 0, -2)
     def fetch(after, weight, name):
         return pl.pallas_call(
             weight_kernel, out_shape=[pltpu.VMEM(weight.shape, weight.dtype), pltpu.VMEM((8, LANES), f32)],
@@ -416,7 +424,7 @@
         )(after, in_hbm(weight))
 
     gate, token = fetch(residual, gate_weight, "gate")
-    even = jnp.concatenate([send] + [swap(send, k) for k in range(2, count, 2)], axis=0)
+    even = jnp.concatenate([send] + [swap(send, k) for k in far_first], axis=0)
     even, near, token = lax.optimization_barrier((even, near, token))
     odd = swap(even, 1)
     even_other = sibling(even)
@@ -443,13 +451,14 @@
     far = lax.ppermute(jnp.concatenate([near[2 * per :], relayed], axis=0), "expert", ring)
     own_block, others = kept[:rows], call(add_kernel, struct((half - rows, main), bf16), [VMEM] * 2, "add", 0.1)(kept[rows:], arrived[rows:])
 
-    counts = jnp.stack([even, odd], 0).reshape(2, count // 2, rows, main + LANES)[:, :, :tokens, main + 2 * experts + 2].astype(jnp.int32)
-    counts = counts.transpose(1, 0, 2).reshape(count, tokens)
+    counts = [block.reshape(count // 2, rows, main + LANES)[:, :tokens, main + 2 * experts + 2].astype(jnp.int32) for block in (even, odd)]
+    place = [0, *far_first]
+    counts = jnp.stack([counts[k % 2][place.index(k - k % 2)] for k in range(count)])
     out = struct((tokens, cached + steps, kv_heads, width), bf16)
     keys, values = call(functools.partial(resample_kernel, steps, early), (out, out), [SMEM] + [VMEM] * 6, "resample", 2.2)(
         counts, near, far, cache_keys, cache_values, new_keys, new_values
     )
-    returned = [swap(others[(k // 2 - 1) * rows : k // 2 * rows], k) for k in range(2, count, 2)]
+    returned = [swap(others[n * rows : (n + 1) * rows], k) for n, k in enumerate(far_first)]
     keys, values, *returned = lax.optimization_barrier((keys, values, *returned))
     result = call(functools.partial(total_kernel, len(returned) + 2), struct((rows, main), bf16), [VMEM] * (len(returned) + 3), "total", 0.1)(
         residual, own_block, arrived[:rows], *returned

time: 46.5 us -> 45.2 us (0.972)
  waiting for transfers between devices: 13.8 us -> 11 us
  starting transfers between devices: 15.3 us -> 17.4 us
  Pallas kernels: 15.9 us -> 15.1 us
    ppermute x10, waiting for transfers between devices: 11.4 us -> 8.54 us  [swap(): lax.ppermute(value, 'expert', [(i, i ^ offset) for i in range(count)])]
    ppermute x1, starting transfers between devices: 1.31 us -> 3.39 us  [fast_shards(): lax.ppermute(jnp.concatenate([near[2 * per:], relayed], axis=0), 'expert'...]
    pallas_call x1, Pallas kernels: 1.75 us -> 0.91 us  [fast_shards(): call(functools.partial(attend_kernel, steps, experts), (struct((rows, mai...]
  transfers between devices with their start and end apart: 15 -> 15, of which waited for: 8 -> 7; matrix products, arithmetic and copies ran while one was open for 1% -> 1% of each run, Pallas kernels for 30% -> 29%
where the time goes in v4:
time: 45.2 us; the launch traced here: 44.8 us
  starting transfers between devices  17.4 us (38%)
  Pallas kernels  15.1 us (33%)
  waiting for transfers between devices  11 us (24%)
  between operations  0.82 us (2%)
  local copies, waits for them, and re-layouts  0.51 us (1%)
    ppermute x10, starting transfers between devices, swap(): lax.ppermute(value, 'expert', [(i, i ^ offset) for i in range(count)])  13.6 us
    ppermute x10, waiting for transfers between devices, swap(): lax.ppermute(value, 'expert', [(i, i ^ offset) for i in range(count)])  8.54 us
    pallas_call x2, Pallas kernels, fetch(): pl.pallas_call(weight_kernel, out_shape=[pltpu.VMEM(weight.shape, weight....  5.73 us
    ppermute x1, starting transfers between devices, fast_shards(): lax.ppermute(jnp.concatenate([near[2 * per:], relayed], axis=0), 'expert'...  3.39 us
    ppermute x4, waiting for transfers between devices, sibling(): return lax.ppermute(value, 'tensor', [(0, 1), (1, 0)])  2.43 us
    pallas_call x1, Pallas kernels, fast_shards(): call(functools.partial(resample_kernel, steps, early), (out, out), [SMEM]...  2.01 us
    pallas_call x1, Pallas kernels, fast_shards(): call(functools.partial(hidden_kernel, steps, tokens, experts), struct((co...  1.5 us
    pallas_call x1, Pallas kernels, fast_shards(): call(functools.partial(down_kernel, steps, tokens), (struct((half, main),...  1.49 us
  transfers between devices with their start and end apart: 15, of which 7 were waited for; matrix products, arithmetic and copies ran while one was open for 1% of the time, Pallas kernels for 29%

profile of v4, /device:TPU:0, one launch (start us, length us, event | category | flops | bytes accessed | tf_op | source)
XLA Modules:
  0.0 44.8 jit_solution(15077024912457375386)
XLA Ops:
  0.6 1.3 %load.1 = (s32[3,4,8]{2,1,0:T(4,128)S(1)}, f32[3,4,8]{2,1,0:T(4,128)S(1)}, s32[4]{0:T(128)S(4)}, f32[1,4096]{1,0:T(1,128)S(1)}, bf16[3,4,4096]{2,1,0:T(4,128)(2,...) custom-call(s32[3,4,8]{2,1,0:T(4,128)} %ids_in.1, ...), custom_call_target="tpu_custom_call" | custom-call | tf_op jit(solution)/shard_map/load/pallas_call | solution.py:401
  1.9 3.0 %collective-permute-start.3 = (bf16[10,136,128]{2,1,0:T(8,128)(2,1)S(1)}, bf16[10,136,128]{2,1,0:T(8,128)(2,1)S(1)}, u32[]{:S(2)}, u32[]{:S(2)}) collective-permute-start(bf16[10,136,128]{2,1,0:T(8,128)(2,1)S(1)} %get-tuple-element.52), channel_id=1, source_target_pairs={{0,2},{2,0},{4,6},{6,4},{8,10},{10,8},{12,14},{14,12},{1,3},{3,1},... | collective-permute-start | bytes 1044488 | tf_op jit(solution)/shard_map/ppermute | solution.py:394
  4.9 0.9 %attend.1 = (bf16[16,1664]{1,0:T(8,128)(2,1)S(1)}, f32[16,1536]{1,0:T(8,128)S(1)}) custom-call(s32[3,4,8]{2,1,0:T(4,128)S(1)} %get-tuple-element.39.ids_ref, f32[3,4,8]{2,1,0:T(4,128)S(1)} %get-tuple-element.40.weights_ref, s32[4]{0:T(128)S(4)} %get-tuple-element.41.counts_ref, f32[1,4096]{1,0:T(1,128)S(1)} %get-tuple-element.42.gain_ref, ...), custom_call_target="tpu_custom_call" | custom-call | bytes 8049999 | tf_op jit(solution)/shard_map/attend/pallas_call | solution.py:411
  5.8 3.7 %collective-permute-start = (bf16[16,1664]{1,0:T(8,128)(2,1)S(1)}, bf16[16,1664]{1,0:T(8,128)(2,1)S(1)}, u32[]{:S(2)}, u32[]{:S(2)}) collective-permute-start(bf16[16,1664]{1,0:T(8,128)(2,1)S(1)} %get-tuple-element.51), channel_id=1, source_target_pairs={{0,12},{2,14},{4,8},{6,10},{8,4},{10,6},{12,0},{14,2},{1,13},{3,15... | collective-permute-start | bytes 159752 | tf_op jit(solution)/shard_map/ppermute | solution.py:394
  9.5 0.0 collective-permute-start.1
  9.5 0.8 %collective-permute-start.2 = (bf16[16,1664]{1,0:T(8,128)(2,1)S(1)}, bf16[16,1664]{1,0:T(8,128)(2,1)S(1)}, u32[]{:S(2)}, u32[]{:S(2)}) collective-permute-start(bf16[16,1664]{1,0:T(8,128)(2,1)S(1)} %get-tuple-element.51), channel_id=1, source_target_pairs={{0,4},{2,6},{4,0},{6,2},{8,12},{10,14},{12,8},{14,10},{1,5},{3,7},... | collective-permute-start | bytes 159752 | tf_op jit(solution)/shard_map/ppermute | solution.py:394
  10.3 2.9 %gate.1 = (bf16[2,4096,384]{2,1,0:T(8,128)(2,1)S(1)}, f32[8,128]{1,0:T(8,128)S(1)}) custom-call(f32[16,1536]{1,0:T(8,128)S(1)} %get-tuple-element.50.after_ref.refs_0_, bf16[2,4096,384]{2,1,0:T(8,128)(2,1)} %source.2), custom_call_target="tpu_custom_call" | custom-call | bytes 7000000 | tf_op jit(solution)/shard_map/gate/pallas_call | solution.py:419
  13.2 0.0 collective-permute-done
  13.2 1.4 %collective-permute-done.1 = bf16[16,1664]{1,0:T(8,128)(2,1)S(1)} collective-permute-done((bf16[16,1664]{1,0:T(8,128)(2,1)S(1)}, bf16[16,1664]{1,0:T(8,128)(2,1)S(1)}, u32[]{:S(2)}, u32[]{:S(2)}) %collective-permute-start.1) | collective-permute-done | bytes 53280 | tf_op jit(solution)/shard_map/ppermute | solution.py:394
  14.5 0.0 collective-permute-done.2
  14.6 0.0 collective-permute-done.3.near_ref
  14.6 0.6 %collective-permute-start.4 = (bf16[64,1664]{1,0:T(8,128)(2,1)S(1)}, bf16[64,1664]{1,0:T(8,128)(2,1)S(1)}, u32[]{:S(2)}, u32[]{:S(2)}) collective-permute-start(bf16[64,1664]{1,0:T(8,128)(2,1)S(1)} %pad_maximum_fusion.1.after_ref.even_ref), channel_id=1, source_target_pairs={{0,2},{2,0},{4,6},{6,4},{8,10},{10,8},{12,14},{14,12},{1,3},{3,1},... | collective-permute-start | bytes 638984 | tf_op jit(solution)/shard_map/ppermute | solution.py:394
  15.2 0.0 collective-permute-start.5
  15.2 2.9 %up.1 = (bf16[2,4096,384]{2,1,0:T(8,128)(2,1)S(1)}, f32[8,128]{1,0:T(8,128)S(1)}) custom-call(bf16[64,1664]{1,0:T(8,128)(2,1)S(1)} %pad_maximum_fusion.1.after_ref.even_ref, bf16[2,4096,384]{2,1,0:T(8,128)(2,1)} %source.3), custom_call_target="tpu_custom_call" | custom-call | bytes 7000000 | tf_op jit(solution)/shard_map/up/pallas_call | solution.py:419
  18.1 2.4 %collective-permute-done.4.odd_ref = bf16[64,1664]{1,0:T(8,128)(2,1)S(1)} collective-permute-done((bf16[64,1664]{1,0:T(8,128)(2,1)S(1)}, bf16[64,1664]{1,0:T(8,128)(2,1)S(1)}, u32[]{:S(2)}, u32[]{:S(2)}) %collective-permute-start.4) | collective-permute-done | bytes 213024 | tf_op jit(solution)/shard_map/ppermute | solution.py:394
  20.5 0.0 collective-permute-start.6
  20.5 0.5 %collective-permute-start.8 = (bf16[6,136,128]{2,1,0:T(8,128)(2,1)S(1)}, bf16[6,136,128]{2,1,0:T(8,128)(2,1)S(1)}, u32[]{:S(2)}, u32[]{:S(2)}) collective-permute-start(bf16[6,136,128]{2,1,0:T(8,128)(2,1)S(1)} %get-tuple-element.64), channel_id=1, source_target_pairs={{0,2},{2,0},{4,6},{6,4},{8,10},{10,8},{12,14},{14,12},{1,3},{3,1},... | collective-permute-start | bytes 626696 | tf_op jit(solution)/shard_map/ppermute | solution.py:394
  21.0 0.0 slice-start
  21.0 1.5 %partial.1.partial_ref = f32[4,128,384]{2,1,0:T(8,128)S(1)} custom-call(f32[8,128]{1,0:T(8,128)S(1)} %get-tuple-element.54.after_ref, f32[8,128]{1,0:T(8,128)S(1)} %get-tuple-element.58.also_after_ref, bf16[64,1664]{1,0:T(8,128)(2,1)S(1)} %pad_maximum_fusion.1.after_ref.even_ref, bf16[64,1664]{1,0:T(8,128)(2,1)S(1)} %collective-permute-done.4.odd_ref, ...), custom_call_target="tpu_custom_call" | custom-call | bytes 35000 | tf_op jit(solution)/shard_map/partial/pallas_call | solution.py:435
  22.5 0.0 slice-start.1
  22.5 0.0 collective-permute-done.5.even_other_ref
  22.5 0.0 collective-permute-done.6.odd_other_ref
  22.5 1.5 %hidden.1.own_ref = bf16[128,768]{1,0:T(8,128)(2,1)S(1)} custom-call(f32[4,128,384]{2,1,0:T(8,128)S(1)} %partial.1.partial_ref, bf16[64,1664]{1,0:T(8,128)(2,1)S(1)} %pad_maximum_fusion.1.after_ref.even_ref, bf16[64,1664]{1,0:T(8,128)(2,1)S(1)} %collective-permute-done.4.odd_ref, bf16[64,1664]{1,0:T(8,128)(2,1)S(1)} %collective-permute-done.5.even_other_ref, ...), custom_call_target="tpu_custom_call" | custom-call | bytes 35000 | tf_op jit(solution)/shard_map/hidden/pallas_call | solution.py:438
  24.0 0.3 collective-permute-start.7
  24.3 1.2 %collective-permute-done.7.other_ref = bf16[128,768]{1,0:T(8,128)(2,1)S(1)} collective-permute-done((bf16[128,768]{1,0:T(8,128)(2,1)S(1)}, bf16[128,768]{1,0:T(8,128)(2,1)S(1)}, u32[]{:S(2)}, u32[]{:S(2)}) %collective-permute-start.7) | collective-permute-done | bytes 196640 | tf_op jit(solution)/shard_map/ppermute | solution.py:397
  25.5 0.0 slice-done
  25.5 0.0 slice-done.1
  25.5 1.5 %down.1 = (f32[64,1536]{1,0:T(8,128)S(1)}, bf16[64,1536]{1,0:T(8,128)(2,1)S(1)}) custom-call(bf16[128,768]{1,0:T(8,128)(2,1)S(1)} %hidden.1.own_ref, bf16[128,768]{1,0:T(8,128)(2,1)S(1)} %collective-permute-done.7.other_ref, bf16[2,768,2048]{2,1,0:T(8,128)(2,1)S(1)} %bitcast.22), custom_call_target="tpu_custom_call" | custom-call | bytes 35000 | tf_op jit(solution)/shard_map/down/pallas_call | solution.py:445
  27.0 1.0 %collective-permute-done.8 = bf16[6,136,128]{2,1,0:T(8,128)(2,1)S(1)} collective-permute-done((bf16[6,136,128]{2,1,0:T(8,128)(2,1)S(1)}, bf16[6,136,128]{2,1,0:T(8,128)(2,1)S(1)}, u32[]{:S(2)}, u32[]{:S(2)}) %collective-permute-start.8) | collective-permute-done | bytes 208928 | tf_op jit(solution)/shard_map/ppermute | solution.py:394
  28.1 0.5 %collective-permute-start.9 = (bf16[64,1536]{1,0:T(8,128)(2,1)S(1)}, bf16[64,1536]{1,0:T(8,128)(2,1)S(1)}, u32[]{:S(2)}, u32[]{:S(2)}) collective-permute-start(bf16[64,1536]{1,0:T(8,128)(2,1)S(1)} %get-tuple-element.65), channel_id=1, source_target_pairs={{0,2},{2,0},{4,6},{6,4},{8,10},{10,8},{12,14},{14,12},{1,3},{3,1},... | collective-permute-start | bytes 589832 | tf_op jit(solution)/shard_map/ppermute | solution.py:394
  28.6 0.1 slice.105
  28.7 0.1 copy.18
  28.8 0.1 slice.107
  28.9 0.1 copy.19
  29.1 3.4 %collective-permute-start.10 = (bf16[8,136,128]{2,1,0:T(8,128)(2,1)S(1)}, bf16[8,136,128]{2,1,0:T(8,128)(2,1)S(1)}, u32[]{:S(2)}, u32[]{:S(2)}) collective-permute-start(bf16[8,136,128]{2,1,0:T(8,128)(2,1)S(1)} %pad_maximum_fusion), channel_id=1, source_target_pairs={{0,4},{4,8},{6,2},{8,12},{10,6},{14,10},{1,5},{5,9},{7,3},{9,13},{... | collective-permute-start | bytes 835592 | tf_op jit(solution)/shard_map/ppermute | solution.py:451
  32.5 2.1 %collective-permute-done.9 = bf16[64,1536]{1,0:T(8,128)(2,1)S(1)} collective-permute-done((bf16[64,1536]{1,0:T(8,128)(2,1)S(1)}, bf16[64,1536]{1,0:T(8,128)(2,1)S(1)}, u32[]{:S(2)}, u32[]{:S(2)}) %collective-permute-start.9) | collective-permute-done | bytes 196640 | tf_op jit(solution)/shard_map/ppermute | solution.py:394
  34.7 3.1 %collective-permute-start.11 = (bf16[16,1536]{1,0:T(8,128)(2,1)S(1)}, bf16[16,1536]{1,0:T(8,128)(2,1)S(1)}, u32[]{:S(2)}, u32[]{:S(2)}) collective-permute-start(bf16[16,1536]{1,0:T(8,128)(2,1)S(1)} %get-tuple-element.77), channel_id=1, source_target_pairs={{0,12},{2,14},{4,8},{6,10},{8,4},{10,6},{12,0},{14,2},{1,13},{3,15... | collective-permute-start | bytes 147464 | tf_op jit(solution)/shard_map/ppermute | solution.py:394
  37.8 0.0 collective-permute-start.12
  37.8 1.3 %collective-permute-start.13 = (bf16[16,1536]{1,0:T(8,128)(2,1)S(1)}, bf16[16,1536]{1,0:T(8,128)(2,1)S(1)}, u32[]{:S(2)}, u32[]{:S(2)}) collective-permute-start(bf16[16,1536]{1,0:T(8,128)(2,1)S(1)} %get-tuple-element.75), channel_id=1, source_target_pairs={{0,4},{2,6},{4,0},{6,2},{8,12},{10,14},{12,8},{14,10},{1,5},{3,7},... | collective-permute-start | bytes 147464 | tf_op jit(solution)/shard_map/ppermute | solution.py:394
  39.2 0.0 collective-permute-done.10.relay_ref
  39.2 2.0 %resample.1 = (bf16[4,131,2,128]{3,2,1,0:T(2,128)(2,1)}, bf16[4,131,2,128]{3,2,1,0:T(2,128)(2,1)}) custom-call(s32[8,4]{1,0:T(8,128)S(1)} %stack.3.counts_ref, bf16[10,136,128]{2,1,0:T(8,128)(2,1)S(1)} %collective-permute-done.3.near_ref, bf16[8,136,128]{2,1,0:T(8,128)(2,1)S(1)} %collective-permute-done.10.relay_ref, ...), custom_call_target="tpu_custom_call" | custom-call | bytes 7700000 | tf_op jit(solution)/shard_map/resample/pallas_call | solution.py:458
  41.2 0.0 collective-permute-done.11.refs_3_
  41.2 1.6 %collective-permute-done.12.refs_4_ = bf16[16,1536]{1,0:T(8,128)(2,1)S(1)} collective-permute-done((bf16[16,1536]{1,0:T(8,128)(2,1)S(1)}, bf16[16,1536]{1,0:T(8,128)(2,1)S(1)}, u32[]{:S(2)}, u32[]{:S(2)}) %collective-permute-start.12) | collective-permute-done | bytes 49184 | tf_op jit(solution)/shard_map/ppermute | solution.py:394
  42.8 0.0 collective-permute-done.13.refs_5_
  42.9 0.1 collective-permute-start.14
  42.9 1.2 %collective-permute-done.14.other_ref = bf16[16,1536]{1,0:T(8,128)(2,1)S(1)} collective-permute-done((bf16[16,1536]{1,0:T(8,128)(2,1)S(1)}, bf16[16,1536]{1,0:T(8,128)(2,1)S(1)}, u32[]{:S(2)}, u32[]{:S(2)}) %collective-permute-start.14) | collective-permute-done | bytes 49184 | tf_op jit(solution)/shard_map/ppermute | solution.py:397
  44.2 0.7 %unpack.1 = bf16[3,4,4096]{2,1,0:T(4,128)(2,1)} custom-call(bf16[16,1536]{1,0:T(8,128)(2,1)S(1)} %total.1.own_ref, bf16[16,1536]{1,0:T(8,128)(2,1)S(1)} %collective-permute-done.14.other_ref), custom_call_target="tpu_custom_call" | custom-call | bytes 1750000 | tf_op jit(solution)/shard_map/unpack/pallas_call | solution.py:466
  (15 shorter events, 0.2 us)
Async XLA Ops:
  1.9 12.7 %collective-permute-start.3 = (bf16[10,136,128]{2,1,0:T(8,128)(2,1)S(1)}, bf16[10,136,128]{2,1,0:T(8,128)(2,1)S(1)}, u32[]{:S(2)}, u32[]{:S(2)}) collective-permute-start(bf16[10,136,128]{2,1,0:T(8,128)(2,1)S(1)} %get-tuple-element.52), channel_id=1, source_target_pairs={{0,2},{2,0},{4,6},{6,4},{8,10},{10,8},{12,14},{14,12},{1,3},{3,1},... | collective-permute-start | bytes 1044488 | tf_op jit(solution)/shard_map/ppermute | solution.py:394
  5.8 7.3 %collective-permute-start = (bf16[16,1664]{1,0:T(8,128)(2,1)S(1)}, bf16[16,1664]{1,0:T(8,128)(2,1)S(1)}, u32[]{:S(2)}, u32[]{:S(2)}) collective-permute-start(bf16[16,1664]{1,0:T(8,128)(2,1)S(1)} %get-tuple-element.51), channel_id=1, source_target_pairs={{0,12},{2,14},{4,8},{6,10},{8,4},{10,6},{12,0},{14,2},{1,13},{3,15... | collective-permute-start | bytes 159752 | tf_op jit(solution)/shard_map/ppermute | solution.py:394
  9.5 5.0 %collective-permute-start.1 = (bf16[16,1664]{1,0:T(8,128)(2,1)S(1)}, bf16[16,1664]{1,0:T(8,128)(2,1)S(1)}, u32[]{:S(2)}, u32[]{:S(2)}) collective-permute-start(bf16[16,1664]{1,0:T(8,128)(2,1)S(1)} %get-tuple-element.51), channel_id=1, source_target_pairs={{0,8},{2,10},{4,12},{6,14},{8,0},{10,2},{12,4},{14,6},{1,9},{3,11}... | collective-permute-start | bytes 159752 | tf_op jit(solution)/shard_map/ppermute | solution.py:394
  9.5 5.0 %collective-permute-start.2 = (bf16[16,1664]{1,0:T(8,128)(2,1)S(1)}, bf16[16,1664]{1,0:T(8,128)(2,1)S(1)}, u32[]{:S(2)}, u32[]{:S(2)}) collective-permute-start(bf16[16,1664]{1,0:T(8,128)(2,1)S(1)} %get-tuple-element.51), channel_id=1, source_target_pairs={{0,4},{2,6},{4,0},{6,2},{8,12},{10,14},{12,8},{14,10},{1,5},{3,7},... | collective-permute-start | bytes 159752 | tf_op jit(solution)/shard_map/ppermute | solution.py:394
  14.6 5.9 %collective-permute-start.4 = (bf16[64,1664]{1,0:T(8,128)(2,1)S(1)}, bf16[64,1664]{1,0:T(8,128)(2,1)S(1)}, u32[]{:S(2)}, u32[]{:S(2)}) collective-permute-start(bf16[64,1664]{1,0:T(8,128)(2,1)S(1)} %pad_maximum_fusion.1.after_ref.even_ref), channel_id=1, source_target_pairs={{0,2},{2,0},{4,6},{6,4},{8,10},{10,8},{12,14},{14,12},{1,3},{3,1},... | collective-permute-start | bytes 638984 | tf_op jit(solution)/shard_map/ppermute | solution.py:394
  15.2 7.3 %collective-permute-start.5 = (bf16[64,1664]{1,0:T(8,128)(2,1)S(1)}, bf16[64,1664]{1,0:T(8,128)(2,1)S(1)}, u32[]{:S(2)}, u32[]{:S(2)}) collective-permute-start(bf16[64,1664]{1,0:T(8,128)(2,1)S(1)} %pad_maximum_fusion.1.after_ref.even_ref), channel_id=1, source_target_pairs={{0,1},{1,0},{2,3},{3,2},{4,5},{5,4},{6,7},{7,6},{8,9},{9,8},{10,11... | collective-permute-start | bytes 638984 | tf_op jit(solution)/shard_map/ppermute | solution.py:397
  20.5 2.0 %collective-permute-start.6 = (bf16[64,1664]{1,0:T(8,128)(2,1)S(1)}, bf16[64,1664]{1,0:T(8,128)(2,1)S(1)}, u32[]{:S(2)}, u32[]{:S(2)}) collective-permute-start(bf16[64,1664]{1,0:T(8,128)(2,1)S(1)} %collective-permute-done.4.odd_ref), channel_id=1, source_target_pairs={{0,1},{1,0},{2,3},{3,2},{4,5},{5,4},{6,7},{7,6},{8,9},{9,8},{10,11... | collective-permute-start | bytes 638984 | tf_op jit(solution)/shard_map/ppermute | solution.py:397
  20.5 7.6 %collective-permute-start.8 = (bf16[6,136,128]{2,1,0:T(8,128)(2,1)S(1)}, bf16[6,136,128]{2,1,0:T(8,128)(2,1)S(1)}, u32[]{:S(2)}, u32[]{:S(2)}) collective-permute-start(bf16[6,136,128]{2,1,0:T(8,128)(2,1)S(1)} %get-tuple-element.64), channel_id=1, source_target_pairs={{0,2},{2,0},{4,6},{6,4},{8,10},{10,8},{12,14},{14,12},{1,3},{3,1},... | collective-permute-start | bytes 626696 | tf_op jit(solution)/shard_map/ppermute | solution.py:394
  21.0 4.5 %slice-start = ((s8[6291456]{0:T(1024)(128)(4,1)}), s8[4194304]{0:T(1024)(128)(4,1)S(1)}, s32[]{:S(2)}) async-start(s8[6291456]{0:T(1024)(128)(4,1)} %bitcast.21), calls=%async_computation | async-start | bytes 8388608
  22.5 3.1 %slice-start.1 = ((s8[6291456]{0:T(1024)(128)(4,1)}), s8[2097152]{0:T(1024)(128)(4,1)S(1)}, s32[]{:S(2)}) async-start(s8[6291456]{0:T(1024)(128)(4,1)} %bitcast.21), calls=%async_computation.1 | async-start | bytes 4194304
  24.0 1.5 %collective-permute-start.7 = (bf16[128,768]{1,0:T(8,128)(2,1)S(1)}, bf16[128,768]{1,0:T(8,128)(2,1)S(1)}, u32[]{:S(2)}, u32[]{:S(2)}) collective-permute-start(bf16[128,768]{1,0:T(8,128)(2,1)S(1)} %hidden.1.own_ref), channel_id=1, source_target_pairs={{0,1},{1,0},{2,3},{3,2},{4,5},{5,4},{6,7},{7,6},{8,9},{9,8},{10,11... | collective-permute-start | bytes 589832 | tf_op jit(solution)/shard_map/ppermute | solution.py:397
  28.1 6.5 %collective-permute-start.9 = (bf16[64,1536]{1,0:T(8,128)(2,1)S(1)}, bf16[64,1536]{1,0:T(8,128)(2,1)S(1)}, u32[]{:S(2)}, u32[]{:S(2)}) collective-permute-start(bf16[64,1536]{1,0:T(8,128)(2,1)S(1)} %get-tuple-element.65), channel_id=1, source_target_pairs={{0,2},{2,0},{4,6},{6,4},{8,10},{10,8},{12,14},{14,12},{1,3},{3,1},... | collective-permute-start | bytes 589832 | tf_op jit(solution)/shard_map/ppermute | solution.py:394
  29.1 10.1 %collective-permute-start.10 = (bf16[8,136,128]{2,1,0:T(8,128)(2,1)S(1)}, bf16[8,136,128]{2,1,0:T(8,128)(2,1)S(1)}, u32[]{:S(2)}, u32[]{:S(2)}) collective-permute-start(bf16[8,136,128]{2,1,0:T(8,128)(2,1)S(1)} %pad_maximum_fusion), channel_id=1, source_target_pairs={{0,4},{4,8},{6,2},{8,12},{10,6},{14,10},{1,5},{5,9},{7,3},{9,13},{... | collective-permute-start | bytes 835592 | tf_op jit(solution)/shard_map/ppermute | solution.py:451
  34.7 6.5 %collective-permute-start.11 = (bf16[16,1536]{1,0:T(8,128)(2,1)S(1)}, bf16[16,1536]{1,0:T(8,128)(2,1)S(1)}, u32[]{:S(2)}, u32[]{:S(2)}) collective-permute-start(bf16[16,1536]{1,0:T(8,128)(2,1)S(1)} %get-tuple-element.77), channel_id=1, source_target_pairs={{0,12},{2,14},{4,8},{6,10},{8,4},{10,6},{12,0},{14,2},{1,13},{3,15... | collective-permute-start | bytes 147464 | tf_op jit(solution)/shard_map/ppermute | solution.py:394
  37.8 5.0 %collective-permute-start.12 = (bf16[16,1536]{1,0:T(8,128)(2,1)S(1)}, bf16[16,1536]{1,0:T(8,128)(2,1)S(1)}, u32[]{:S(2)}, u32[]{:S(2)}) collective-permute-start(bf16[16,1536]{1,0:T(8,128)(2,1)S(1)} %get-tuple-element.76), channel_id=1, source_target_pairs={{0,8},{2,10},{4,12},{6,14},{8,0},{10,2},{12,4},{14,6},{1,9},{3,11}... | collective-permute-start | bytes 147464 | tf_op jit(solution)/shard_map/ppermute | solution.py:394
  37.8 5.0 %collective-permute-start.13 = (bf16[16,1536]{1,0:T(8,128)(2,1)S(1)}, bf16[16,1536]{1,0:T(8,128)(2,1)S(1)}, u32[]{:S(2)}, u32[]{:S(2)}) collective-permute-start(bf16[16,1536]{1,0:T(8,128)(2,1)S(1)} %get-tuple-element.75), channel_id=1, source_target_pairs={{0,4},{2,6},{4,0},{6,2},{8,12},{10,14},{12,8},{14,10},{1,5},{3,7},... | collective-permute-start | bytes 147464 | tf_op jit(solution)/shard_map/ppermute | solution.py:394
  42.9 1.3 %collective-permute-start.14 = (bf16[16,1536]{1,0:T(8,128)(2,1)S(1)}, bf16[16,1536]{1,0:T(8,128)(2,1)S(1)}, u32[]{:S(2)}, u32[]{:S(2)}) collective-permute-start(bf16[16,1536]{1,0:T(8,128)(2,1)S(1)} %total.1.own_ref), channel_id=1, source_target_pairs={{0,1},{1,0},{2,3},{3,2},{4,5},{5,4},{6,7},{7,6},{8,9},{9,8},{10,11... | collective-permute-start | bytes 147464 | tf_op jit(solution)/shard_map/ppermute | solution.py:397

commit v5 on v4

--- a/solution.py
+++ b/solution.py
@@ -194,13 +194,24 @@
     send_ref[:, main:] = jnp.concatenate(pieces, axis=0).astype(bf16)
 
 
-def unpacking(blocks, steps, tokens, s, back):
-    rows = (steps + 1) * tokens
-    target, source = iota((blocks * rows, blocks * rows), 0), iota((blocks * rows, blocks * rows), 1)
-    if back:
-        target, source = source, target
-    hit = (target + (steps - s) * tokens == source) & (lax.div(lax.rem(target, rows), tokens) == s)
-    return hit.astype(f32).astype(bf16)
+def unpacked(packed, steps, tokens):
+    rows, part = (steps + 1) * tokens, packed.shape[1] // steps
+    cube = packed.reshape(packed.shape[0] // rows, rows, packed.shape[1])
+    step = lax.div(iota((1, rows, part), 1), tokens)
+    last = jnp.zeros((cube.shape[0], rows, part), f32)
+    for s in range(steps):
+        last = jnp.where(step == s, pltpu.roll(cube[:, :, s * part : (s + 1) * part], rows - (steps - s) * tokens, 1), last)
+    return last.reshape(packed.shape[0], part)
+
+
+def packed(plain, steps, tokens):
+    rows, part = (steps + 1) * tokens, plain.shape[1] // (steps + 1)
+    main = steps * part
+    cube = plain.reshape(plain.shape[0] // rows, rows, plain.shape[1])
+    last = cube[:, :, main:]
+    extra = jnp.concatenate([pltpu.roll(last, (steps - s) * tokens, 1) for s in range(steps)], axis=2)
+    in_main = iota((1, rows, main), 1) < steps * tokens
+    return jnp.where(in_main, cube[:, :, :main], extra).reshape(plain.shape[0], main)
 
 
 def halves(even_ref, odd_ref, at):
@@ -208,15 +219,11 @@
 
 
 def expert_products(steps, tokens, features, gate_ref, up_ref, half):
-    total, main = features.shape
-    rows = (steps + 1) * tokens
+    main = features.shape[1]
     part = main // steps
     columns = main + part
     local = gate_ref.shape[0]
-    blocks = total // rows
-    extra = sum(
-        dot(unpacking(blocks, steps, tokens, s, False), features[:, s * part : (s + 1) * part]) for s in range(steps)
-    ).astype(bf16)
+    extra = unpacked(features.astype(f32), steps, tokens).astype(bf16)
     first = pl.ds(pl.multiple_of(half * columns, LANES), main)
     last = pl.ds(pl.multiple_of(half * columns + main, LANES), part)
     return [
@@ -260,19 +267,13 @@
     total, width = own_ref.shape
     local, _, columns = down_ref.shape
     units = width // local
-    rows = (steps + 1) * tokens
-    part = columns // (steps + 1)
-    main = steps * part
     mine = lax.axis_index("tensor")
     product = 0.0
     for ref, half in ((own_ref, mine), (other_ref, 1 - mine)):
         start = pl.multiple_of(half * units, LANES)
         for e in range(local):
             product += dot(ref[:, e * units : (e + 1) * units], down_ref[e, pl.ds(start, units), :])
-    last = product[:, main:].astype(bf16)
-    extra = jnp.concatenate([dot(unpacking(total // rows, steps, tokens, s, True), last) for s in range(steps)], axis=1)
-    in_main = lax.rem(iota((total, main), 0), rows) < steps * tokens
-    product = jnp.where(in_main, product[:, :main], extra)
+    product = packed(product, steps, tokens)
     kept_ref[...] = product[: total // 2]
     leaving_ref[...] = product[total // 2 :].astype(bf16)
 

time: 45.2 us -> 45.1 us (level)
  Pallas kernels: 15.1 us -> 14.5 us
  transfers between devices with their start and end apart: 15 -> 15, of which waited for: 7 -> 8; matrix products, arithmetic and copies ran while one was open for 1% -> 1% of each run, Pallas kernels for 29% -> 28%
where the time goes in v5:
time: 45.1 us; the launch traced here: 44.3 us
  starting transfers between devices  17.3 us (38%)
  Pallas kernels  14.5 us (32%)
  waiting for transfers between devices  11.1 us (25%)
  between operations  0.81 us (2%)
  local copies, waits for them, and re-layouts  0.51 us (1%)
    ppermute x10, starting transfers between devices, swap(): lax.ppermute(value, 'expert', [(i, i ^ offset) for i in range(count)])  13.6 us
    ppermute x10, waiting for transfers between devices, swap(): lax.ppermute(value, 'expert', [(i, i ^ offset) for i in range(count)])  8.24 us
    pallas_call x2, Pallas kernels, fetch(): pl.pallas_call(weight_kernel, out_shape=[pltpu.VMEM(weight.shape, weight....  5.73 us
    ppermute x1, starting transfers between devices, fast_shards(): lax.ppermute(jnp.concatenate([near[2 * per:], relayed], axis=0), 'expert'...  3.41 us
    ppermute x4, waiting for transfers between devices, sibling(): return lax.ppermute(value, 'tensor', [(0, 1), (1, 0)])  2.44 us
    pallas_call x1, Pallas kernels, fast_shards(): call(functools.partial(resample_kernel, steps, early), (out, out), [SMEM]...  2 us
    pallas_call x1, Pallas kernels, fast_shards(): call(functools.partial(hidden_kernel, steps, tokens, experts), struct((co...  1.31 us
    pallas_call x1, Pallas kernels, fast_shards(): pl.pallas_call(functools.partial(load_kernel, steps), out_shape=[space(va...  1.27 us
  transfers between devices with their start and end apart: 15, of which 8 were waited for; matrix products, arithmetic and copies ran while one was open for 1% of the time, Pallas kernels for 28%

profile of v5, /device:TPU:0, one launch (start us, length us, event | category | flops | bytes accessed | tf_op | source)
XLA Modules:
  0.0 44.3 jit_solution(566184816297705762)
XLA Ops:
  0.6 1.3 %load.1 = (s32[3,4,8]{2,1,0:T(4,128)S(1)}, f32[3,4,8]{2,1,0:T(4,128)S(1)}, s32[4]{0:T(128)S(4)}, f32[1,4096]{1,0:T(1,128)S(1)}, bf16[3,4,4096]{2,1,0:T(4,128)(2,...) custom-call(s32[3,4,8]{2,1,0:T(4,128)} %ids_in.1, ...), custom_call_target="tpu_custom_call" | custom-call | tf_op jit(solution)/shard_map/load/pallas_call | solution.py:402
  1.9 3.0 %collective-permute-start.3 = (bf16[10,136,128]{2,1,0:T(8,128)(2,1)S(1)}, bf16[10,136,128]{2,1,0:T(8,128)(2,1)S(1)}, u32[]{:S(2)}, u32[]{:S(2)}) collective-permute-start(bf16[10,136,128]{2,1,0:T(8,128)(2,1)S(1)} %get-tuple-element.52), channel_id=1, source_target_pairs={{0,2},{2,0},{4,6},{6,4},{8,10},{10,8},{12,14},{14,12},{1,3},{3,1},... | collective-permute-start | bytes 1044488 | tf_op jit(solution)/shard_map/ppermute | solution.py:395
  4.9 0.9 %attend.1 = (bf16[16,1664]{1,0:T(8,128)(2,1)S(1)}, f32[16,1536]{1,0:T(8,128)S(1)}) custom-call(s32[3,4,8]{2,1,0:T(4,128)S(1)} %get-tuple-element.39.ids_ref, f32[3,4,8]{2,1,0:T(4,128)S(1)} %get-tuple-element.40.weights_ref, s32[4]{0:T(128)S(4)} %get-tuple-element.41.counts_ref, f32[1,4096]{1,0:T(1,128)S(1)} %get-tuple-element.42.gain_ref, ...), custom_call_target="tpu_custom_call" | custom-call | bytes 8049999 | tf_op jit(solution)/shard_map/attend/pallas_call | solution.py:412
  5.8 3.7 %collective-permute-start = (bf16[16,1664]{1,0:T(8,128)(2,1)S(1)}, bf16[16,1664]{1,0:T(8,128)(2,1)S(1)}, u32[]{:S(2)}, u32[]{:S(2)}) collective-permute-start(bf16[16,1664]{1,0:T(8,128)(2,1)S(1)} %get-tuple-element.51), channel_id=1, source_target_pairs={{0,12},{2,14},{4,8},{6,10},{8,4},{10,6},{12,0},{14,2},{1,13},{3,15... | collective-permute-start | bytes 159752 | tf_op jit(solution)/shard_map/ppermute | solution.py:395
  9.5 0.0 collective-permute-start.1
  9.5 0.8 %collective-permute-start.2 = (bf16[16,1664]{1,0:T(8,128)(2,1)S(1)}, bf16[16,1664]{1,0:T(8,128)(2,1)S(1)}, u32[]{:S(2)}, u32[]{:S(2)}) collective-permute-start(bf16[16,1664]{1,0:T(8,128)(2,1)S(1)} %get-tuple-element.51), channel_id=1, source_target_pairs={{0,4},{2,6},{4,0},{6,2},{8,12},{10,14},{12,8},{14,10},{1,5},{3,7},... | collective-permute-start | bytes 159752 | tf_op jit(solution)/shard_map/ppermute | solution.py:395
  10.3 2.9 %gate.1 = (bf16[2,4096,384]{2,1,0:T(8,128)(2,1)S(1)}, f32[8,128]{1,0:T(8,128)S(1)}) custom-call(f32[16,1536]{1,0:T(8,128)S(1)} %get-tuple-element.50.after_ref.refs_0_, bf16[2,4096,384]{2,1,0:T(8,128)(2,1)} %source.2), custom_call_target="tpu_custom_call" | custom-call | bytes 7000000 | tf_op jit(solution)/shard_map/gate/pallas_call | solution.py:420
  13.2 0.0 collective-permute-done
  13.2 1.4 %collective-permute-done.1 = bf16[16,1664]{1,0:T(8,128)(2,1)S(1)} collective-permute-done((bf16[16,1664]{1,0:T(8,128)(2,1)S(1)}, bf16[16,1664]{1,0:T(8,128)(2,1)S(1)}, u32[]{:S(2)}, u32[]{:S(2)}) %collective-permute-start.1) | collective-permute-done | bytes 53280 | tf_op jit(solution)/shard_map/ppermute | solution.py:395
  14.5 0.0 collective-permute-done.2
  14.6 0.0 collective-permute-done.3.near_ref
  14.6 0.6 %collective-permute-start.4 = (bf16[64,1664]{1,0:T(8,128)(2,1)S(1)}, bf16[64,1664]{1,0:T(8,128)(2,1)S(1)}, u32[]{:S(2)}, u32[]{:S(2)}) collective-permute-start(bf16[64,1664]{1,0:T(8,128)(2,1)S(1)} %pad_maximum_fusion.1.after_ref.even_ref), channel_id=1, source_target_pairs={{0,2},{2,0},{4,6},{6,4},{8,10},{10,8},{12,14},{14,12},{1,3},{3,1},... | collective-permute-start | bytes 638984 | tf_op jit(solution)/shard_map/ppermute | solution.py:395
  15.2 0.0 collective-permute-start.5
  15.2 2.9 %up.1 = (bf16[2,4096,384]{2,1,0:T(8,128)(2,1)S(1)}, f32[8,128]{1,0:T(8,128)S(1)}) custom-call(bf16[64,1664]{1,0:T(8,128)(2,1)S(1)} %pad_maximum_fusion.1.after_ref.even_ref, bf16[2,4096,384]{2,1,0:T(8,128)(2,1)} %source.3), custom_call_target="tpu_custom_call" | custom-call | bytes 7000000 | tf_op jit(solution)/shard_map/up/pallas_call | solution.py:420
  18.1 2.4 %collective-permute-done.4.odd_ref = bf16[64,1664]{1,0:T(8,128)(2,1)S(1)} collective-permute-done((bf16[64,1664]{1,0:T(8,128)(2,1)S(1)}, bf16[64,1664]{1,0:T(8,128)(2,1)S(1)}, u32[]{:S(2)}, u32[]{:S(2)}) %collective-permute-start.4) | collective-permute-done | bytes 213024 | tf_op jit(solution)/shard_map/ppermute | solution.py:395
  20.5 0.0 collective-permute-start.6
  20.5 0.5 %collective-permute-start.8 = (bf16[6,136,128]{2,1,0:T(8,128)(2,1)S(1)}, bf16[6,136,128]{2,1,0:T(8,128)(2,1)S(1)}, u32[]{:S(2)}, u32[]{:S(2)}) collective-permute-start(bf16[6,136,128]{2,1,0:T(8,128)(2,1)S(1)} %get-tuple-element.64), channel_id=1, source_target_pairs={{0,2},{2,0},{4,6},{6,4},{8,10},{10,8},{12,14},{14,12},{1,3},{3,1},... | collective-permute-start | bytes 626696 | tf_op jit(solution)/shard_map/ppermute | solution.py:395
  21.0 0.0 slice-start
  21.0 1.3 %partial.1.partial_ref = f32[4,128,384]{2,1,0:T(8,128)S(1)} custom-call(f32[8,128]{1,0:T(8,128)S(1)} %get-tuple-element.54.after_ref, f32[8,128]{1,0:T(8,128)S(1)} %get-tuple-element.58.also_after_ref, bf16[64,1664]{1,0:T(8,128)(2,1)S(1)} %pad_maximum_fusion.1.after_ref.even_ref, bf16[64,1664]{1,0:T(8,128)(2,1)S(1)} %collective-permute-done.4.odd_ref, ...), custom_call_target="tpu_custom_call" | custom-call | bytes 35000 | tf_op jit(solution)/shard_map/partial/pallas_call | solution.py:436
  22.3 0.0 slice-start.1
  22.3 0.0 collective-permute-done.5.even_other_ref
  22.3 0.0 collective-permute-done.6.odd_other_ref
  22.3 1.3 %hidden.1.own_ref = bf16[128,768]{1,0:T(8,128)(2,1)S(1)} custom-call(f32[4,128,384]{2,1,0:T(8,128)S(1)} %partial.1.partial_ref, bf16[64,1664]{1,0:T(8,128)(2,1)S(1)} %pad_maximum_fusion.1.after_ref.even_ref, bf16[64,1664]{1,0:T(8,128)(2,1)S(1)} %collective-permute-done.4.odd_ref, bf16[64,1664]{1,0:T(8,128)(2,1)S(1)} %collective-permute-done.5.even_other_ref, ...), custom_call_target="tpu_custom_call" | custom-call | bytes 35000 | tf_op jit(solution)/shard_map/hidden/pallas_call | solution.py:439
  23.7 0.3 collective-permute-start.7
  23.9 1.2 %collective-permute-done.7.other_ref = bf16[128,768]{1,0:T(8,128)(2,1)S(1)} collective-permute-done((bf16[128,768]{1,0:T(8,128)(2,1)S(1)}, bf16[128,768]{1,0:T(8,128)(2,1)S(1)}, u32[]{:S(2)}, u32[]{:S(2)}) %collective-permute-start.7) | collective-permute-done | bytes 196640 | tf_op jit(solution)/shard_map/ppermute | solution.py:398
  25.2 0.0 slice-done
  25.2 0.0 slice-done.1
  25.2 1.3 %down.1 = (f32[64,1536]{1,0:T(8,128)S(1)}, bf16[64,1536]{1,0:T(8,128)(2,1)S(1)}) custom-call(bf16[128,768]{1,0:T(8,128)(2,1)S(1)} %hidden.1.own_ref, bf16[128,768]{1,0:T(8,128)(2,1)S(1)} %collective-permute-done.7.other_ref, bf16[2,768,2048]{2,1,0:T(8,128)(2,1)S(1)} %bitcast.22), custom_call_target="tpu_custom_call" | custom-call | bytes 35000 | tf_op jit(solution)/shard_map/down/pallas_call | solution.py:446
  26.4 1.6 %collective-permute-done.8 = bf16[6,136,128]{2,1,0:T(8,128)(2,1)S(1)} collective-permute-done((bf16[6,136,128]{2,1,0:T(8,128)(2,1)S(1)}, bf16[6,136,128]{2,1,0:T(8,128)(2,1)S(1)}, u32[]{:S(2)}, u32[]{:S(2)}) %collective-permute-start.8) | collective-permute-done | bytes 208928 | tf_op jit(solution)/shard_map/ppermute | solution.py:395
  28.1 0.5 %collective-permute-start.9 = (bf16[64,1536]{1,0:T(8,128)(2,1)S(1)}, bf16[64,1536]{1,0:T(8,128)(2,1)S(1)}, u32[]{:S(2)}, u32[]{:S(2)}) collective-permute-start(bf16[64,1536]{1,0:T(8,128)(2,1)S(1)} %get-tuple-element.65), channel_id=1, source_target_pairs={{0,2},{2,0},{4,6},{6,4},{8,10},{10,8},{12,14},{14,12},{1,3},{3,1},... | collective-permute-start | bytes 589832 | tf_op jit(solution)/shard_map/ppermute | solution.py:395
  28.6 0.1 slice.105
  28.7 0.1 copy.18
  28.8 0.1 slice.107
  28.9 0.1 copy.19
  29.1 3.4 %collective-permute-start.10 = (bf16[8,136,128]{2,1,0:T(8,128)(2,1)S(1)}, bf16[8,136,128]{2,1,0:T(8,128)(2,1)S(1)}, u32[]{:S(2)}, u32[]{:S(2)}) collective-permute-start(bf16[8,136,128]{2,1,0:T(8,128)(2,1)S(1)} %pad_maximum_fusion), channel_id=1, source_target_pairs={{0,4},{4,8},{6,2},{8,12},{10,6},{14,10},{1,5},{5,9},{7,3},{9,13},{... | collective-permute-start | bytes 835592 | tf_op jit(solution)/shard_map/ppermute | solution.py:452
  32.5 2.1 %collective-permute-done.9 = bf16[64,1536]{1,0:T(8,128)(2,1)S(1)} collective-permute-done((bf16[64,1536]{1,0:T(8,128)(2,1)S(1)}, bf16[64,1536]{1,0:T(8,128)(2,1)S(1)}, u32[]{:S(2)}, u32[]{:S(2)}) %collective-permute-start.9) | collective-permute-done | bytes 196640 | tf_op jit(solution)/shard_map/ppermute | solution.py:395
  34.7 2.6 %collective-permute-start.11 = (bf16[16,1536]{1,0:T(8,128)(2,1)S(1)}, bf16[16,1536]{1,0:T(8,128)(2,1)S(1)}, u32[]{:S(2)}, u32[]{:S(2)}) collective-permute-start(bf16[16,1536]{1,0:T(8,128)(2,1)S(1)} %get-tuple-element.77), channel_id=1, source_target_pairs={{0,12},{2,14},{4,8},{6,10},{8,4},{10,6},{12,0},{14,2},{1,13},{3,15... | collective-permute-start | bytes 147464 | tf_op jit(solution)/shard_map/ppermute | solution.py:395
  37.3 0.0 collective-permute-start.12
  37.3 1.8 %collective-permute-start.13 = (bf16[16,1536]{1,0:T(8,128)(2,1)S(1)}, bf16[16,1536]{1,0:T(8,128)(2,1)S(1)}, u32[]{:S(2)}, u32[]{:S(2)}) collective-permute-start(bf16[16,1536]{1,0:T(8,128)(2,1)S(1)} %get-tuple-element.75), channel_id=1, source_target_pairs={{0,4},{2,6},{4,0},{6,2},{8,12},{10,14},{12,8},{14,10},{1,5},{3,7},... | collective-permute-start | bytes 147464 | tf_op jit(solution)/shard_map/ppermute | solution.py:395
  39.2 0.4 collective-permute-done.10.relay_ref
  39.6 2.0 %resample.1 = (bf16[4,131,2,128]{3,2,1,0:T(2,128)(2,1)}, bf16[4,131,2,128]{3,2,1,0:T(2,128)(2,1)}) custom-call(s32[8,4]{1,0:T(8,128)S(1)} %stack.3.counts_ref, bf16[10,136,128]{2,1,0:T(8,128)(2,1)S(1)} %collective-permute-done.3.near_ref, bf16[8,136,128]{2,1,0:T(8,128)(2,1)S(1)} %collective-permute-done.10.relay_ref, ...), custom_call_target="tpu_custom_call" | custom-call | bytes 7700000 | tf_op jit(solution)/shard_map/resample/pallas_call | solution.py:459
  41.6 0.0 collective-permute-done.11.refs_3_
  41.6 0.7 %collective-permute-done.12.refs_4_ = bf16[16,1536]{1,0:T(8,128)(2,1)S(1)} collective-permute-done((bf16[16,1536]{1,0:T(8,128)(2,1)S(1)}, bf16[16,1536]{1,0:T(8,128)(2,1)S(1)}, u32[]{:S(2)}, u32[]{:S(2)}) %collective-permute-start.12) | collective-permute-done | bytes 49184 | tf_op jit(solution)/shard_map/ppermute | solution.py:395
  42.3 0.0 collective-permute-done.13.refs_5_
  42.3 0.1 collective-permute-start.14
  42.4 1.2 %collective-permute-done.14.other_ref = bf16[16,1536]{1,0:T(8,128)(2,1)S(1)} collective-permute-done((bf16[16,1536]{1,0:T(8,128)(2,1)S(1)}, bf16[16,1536]{1,0:T(8,128)(2,1)S(1)}, u32[]{:S(2)}, u32[]{:S(2)}) %collective-permute-start.14) | collective-permute-done | bytes 49184 | tf_op jit(solution)/shard_map/ppermute | solution.py:398
  43.6 0.7 %unpack.1 = bf16[3,4,4096]{2,1,0:T(4,128)(2,1)} custom-call(bf16[16,1536]{1,0:T(8,128)(2,1)S(1)} %total.1.own_ref, bf16[16,1536]{1,0:T(8,128)(2,1)S(1)} %collective-permute-done.14.other_ref), custom_call_target="tpu_custom_call" | custom-call | bytes 1750000 | tf_op jit(solution)/shard_map/unpack/pallas_call | solution.py:467
  (15 shorter events, 0.2 us)
Async XLA Ops:
  1.9 12.7 %collective-permute-start.3 = (bf16[10,136,128]{2,1,0:T(8,128)(2,1)S(1)}, bf16[10,136,128]{2,1,0:T(8,128)(2,1)S(1)}, u32[]{:S(2)}, u32[]{:S(2)}) collective-permute-start(bf16[10,136,128]{2,1,0:T(8,128)(2,1)S(1)} %get-tuple-element.52), channel_id=1, source_target_pairs={{0,2},{2,0},{4,6},{6,4},{8,10},{10,8},{12,14},{14,12},{1,3},{3,1},... | collective-permute-start | bytes 1044488 | tf_op jit(solution)/shard_map/ppermute | solution.py:395
  5.8 7.3 %collective-permute-start = (bf16[16,1664]{1,0:T(8,128)(2,1)S(1)}, bf16[16,1664]{1,0:T(8,128)(2,1)S(1)}, u32[]{:S(2)}, u32[]{:S(2)}) collective-permute-start(bf16[16,1664]{1,0:T(8,128)(2,1)S(1)} %get-tuple-element.51), channel_id=1, source_target_pairs={{0,12},{2,14},{4,8},{6,10},{8,4},{10,6},{12,0},{14,2},{1,13},{3,15... | collective-permute-start | bytes 159752 | tf_op jit(solution)/shard_map/ppermute | solution.py:395
  9.5 5.0 %collective-permute-start.1 = (bf16[16,1664]{1,0:T(8,128)(2,1)S(1)}, bf16[16,1664]{1,0:T(8,128)(2,1)S(1)}, u32[]{:S(2)}, u32[]{:S(2)}) collective-permute-start(bf16[16,1664]{1,0:T(8,128)(2,1)S(1)} %get-tuple-element.51), channel_id=1, source_target_pairs={{0,8},{2,10},{4,12},{6,14},{8,0},{10,2},{12,4},{14,6},{1,9},{3,11}... | collective-permute-start | bytes 159752 | tf_op jit(solution)/shard_map/ppermute | solution.py:395
  9.5 5.0 %collective-permute-start.2 = (bf16[16,1664]{1,0:T(8,128)(2,1)S(1)}, bf16[16,1664]{1,0:T(8,128)(2,1)S(1)}, u32[]{:S(2)}, u32[]{:S(2)}) collective-permute-start(bf16[16,1664]{1,0:T(8,128)(2,1)S(1)} %get-tuple-element.51), channel_id=1, source_target_pairs={{0,4},{2,6},{4,0},{6,2},{8,12},{10,14},{12,8},{14,10},{1,5},{3,7},... | collective-permute-start | bytes 159752 | tf_op jit(solution)/shard_map/ppermute | solution.py:395
  14.6 5.9 %collective-permute-start.4 = (bf16[64,1664]{1,0:T(8,128)(2,1)S(1)}, bf16[64,1664]{1,0:T(8,128)(2,1)S(1)}, u32[]{:S(2)}, u32[]{:S(2)}) collective-permute-start(bf16[64,1664]{1,0:T(8,128)(2,1)S(1)} %pad_maximum_fusion.1.after_ref.even_ref), channel_id=1, source_target_pairs={{0,2},{2,0},{4,6},{6,4},{8,10},{10,8},{12,14},{14,12},{1,3},{3,1},... | collective-permute-start | bytes 638984 | tf_op jit(solution)/shard_map/ppermute | solution.py:395
  15.2 7.1 %collective-permute-start.5 = (bf16[64,1664]{1,0:T(8,128)(2,1)S(1)}, bf16[64,1664]{1,0:T(8,128)(2,1)S(1)}, u32[]{:S(2)}, u32[]{:S(2)}) collective-permute-start(bf16[64,1664]{1,0:T(8,128)(2,1)S(1)} %pad_maximum_fusion.1.after_ref.even_ref), channel_id=1, source_target_pairs={{0,1},{1,0},{2,3},{3,2},{4,5},{5,4},{6,7},{7,6},{8,9},{9,8},{10,11... | collective-permute-start | bytes 638984 | tf_op jit(solution)/shard_map/ppermute | solution.py:398
  20.5 1.8 %collective-permute-start.6 = (bf16[64,1664]{1,0:T(8,128)(2,1)S(1)}, bf16[64,1664]{1,0:T(8,128)(2,1)S(1)}, u32[]{:S(2)}, u32[]{:S(2)}) collective-permute-start(bf16[64,1664]{1,0:T(8,128)(2,1)S(1)} %collective-permute-done.4.odd_ref), channel_id=1, source_target_pairs={{0,1},{1,0},{2,3},{3,2},{4,5},{5,4},{6,7},{7,6},{8,9},{9,8},{10,11... | collective-permute-start | bytes 638984 | tf_op jit(solution)/shard_map/ppermute | solution.py:398
  20.5 7.6 %collective-permute-start.8 = (bf16[6,136,128]{2,1,0:T(8,128)(2,1)S(1)}, bf16[6,136,128]{2,1,0:T(8,128)(2,1)S(1)}, u32[]{:S(2)}, u32[]{:S(2)}) collective-permute-start(bf16[6,136,128]{2,1,0:T(8,128)(2,1)S(1)} %get-tuple-element.64), channel_id=1, source_target_pairs={{0,2},{2,0},{4,6},{6,4},{8,10},{10,8},{12,14},{14,12},{1,3},{3,1},... | collective-permute-start | bytes 626696 | tf_op jit(solution)/shard_map/ppermute | solution.py:395
  21.0 4.1 %slice-start = ((s8[6291456]{0:T(1024)(128)(4,1)}), s8[4194304]{0:T(1024)(128)(4,1)S(1)}, s32[]{:S(2)}) async-start(s8[6291456]{0:T(1024)(128)(4,1)} %bitcast.21), calls=%async_computation | async-start | bytes 8388608
  22.3 2.9 %slice-start.1 = ((s8[6291456]{0:T(1024)(128)(4,1)}), s8[2097152]{0:T(1024)(128)(4,1)S(1)}, s32[]{:S(2)}) async-start(s8[6291456]{0:T(1024)(128)(4,1)} %bitcast.21), calls=%async_computation.1 | async-start | bytes 4194304
  23.7 1.5 %collective-permute-start.7 = (bf16[128,768]{1,0:T(8,128)(2,1)S(1)}, bf16[128,768]{1,0:T(8,128)(2,1)S(1)}, u32[]{:S(2)}, u32[]{:S(2)}) collective-permute-start(bf16[128,768]{1,0:T(8,128)(2,1)S(1)} %hidden.1.own_ref), channel_id=1, source_target_pairs={{0,1},{1,0},{2,3},{3,2},{4,5},{5,4},{6,7},{7,6},{8,9},{9,8},{10,11... | collective-permute-start | bytes 589832 | tf_op jit(solution)/shard_map/ppermute | solution.py:398
  28.1 6.5 %collective-permute-start.9 = (bf16[64,1536]{1,0:T(8,128)(2,1)S(1)}, bf16[64,1536]{1,0:T(8,128)(2,1)S(1)}, u32[]{:S(2)}, u32[]{:S(2)}) collective-permute-start(bf16[64,1536]{1,0:T(8,128)(2,1)S(1)} %get-tuple-element.65), channel_id=1, source_target_pairs={{0,2},{2,0},{4,6},{6,4},{8,10},{10,8},{12,14},{14,12},{1,3},{3,1},... | collective-permute-start | bytes 589832 | tf_op jit(solution)/shard_map/ppermute | solution.py:395
  29.1 10.5 %collective-permute-start.10 = (bf16[8,136,128]{2,1,0:T(8,128)(2,1)S(1)}, bf16[8,136,128]{2,1,0:T(8,128)(2,1)S(1)}, u32[]{:S(2)}, u32[]{:S(2)}) collective-permute-start(bf16[8,136,128]{2,1,0:T(8,128)(2,1)S(1)} %pad_maximum_fusion), channel_id=1, source_target_pairs={{0,4},{4,8},{6,2},{8,12},{10,6},{14,10},{1,5},{5,9},{7,3},{9,13},{... | collective-permute-start | bytes 835592 | tf_op jit(solution)/shard_map/ppermute | solution.py:452
  34.7 6.9 %collective-permute-start.11 = (bf16[16,1536]{1,0:T(8,128)(2,1)S(1)}, bf16[16,1536]{1,0:T(8,128)(2,1)S(1)}, u32[]{:S(2)}, u32[]{:S(2)}) collective-permute-start(bf16[16,1536]{1,0:T(8,128)(2,1)S(1)} %get-tuple-element.77), channel_id=1, source_target_pairs={{0,12},{2,14},{4,8},{6,10},{8,4},{10,6},{12,0},{14,2},{1,13},{3,15... | collective-permute-start | bytes 147464 | tf_op jit(solution)/shard_map/ppermute | solution.py:395
  37.3 5.0 %collective-permute-start.12 = (bf16[16,1536]{1,0:T(8,128)(2,1)S(1)}, bf16[16,1536]{1,0:T(8,128)(2,1)S(1)}, u32[]{:S(2)}, u32[]{:S(2)}) collective-permute-start(bf16[16,1536]{1,0:T(8,128)(2,1)S(1)} %get-tuple-element.76), channel_id=1, source_target_pairs={{0,8},{2,10},{4,12},{6,14},{8,0},{10,2},{12,4},{14,6},{1,9},{3,11}... | collective-permute-start | bytes 147464 | tf_op jit(solution)/shard_map/ppermute | solution.py:395
  37.3 5.0 %collective-permute-start.13 = (bf16[16,1536]{1,0:T(8,128)(2,1)S(1)}, bf16[16,1536]{1,0:T(8,128)(2,1)S(1)}, u32[]{:S(2)}, u32[]{:S(2)}) collective-permute-start(bf16[16,1536]{1,0:T(8,128)(2,1)S(1)} %get-tuple-element.75), channel_id=1, source_target_pairs={{0,4},{2,6},{4,0},{6,2},{8,12},{10,14},{12,8},{14,10},{1,5},{3,7},... | collective-permute-start | bytes 147464 | tf_op jit(solution)/shard_map/ppermute | solution.py:395
  42.3 1.3 %collective-permute-start.14 = (bf16[16,1536]{1,0:T(8,128)(2,1)S(1)}, bf16[16,1536]{1,0:T(8,128)(2,1)S(1)}, u32[]{:S(2)}, u32[]{:S(2)}) collective-permute-start(bf16[16,1536]{1,0:T(8,128)(2,1)S(1)} %total.1.own_ref), channel_id=1, source_target_pairs={{0,1},{1,0},{2,3},{3,2},{4,5},{5,4},{6,7},{7,6},{8,9},{9,8},{10,11... | collective-permute-start | bytes 147464 | tf_op jit(solution)/shard_map/ppermute | solution.py:398

commit v6 on v5

--- a/solution.py
+++ b/solution.py
@@ -10,7 +10,6 @@
 
 REACH = 2
 LANES = 128
-PAD = 8
 f32, bf16 = jnp.float32, jnp.bfloat16
 
 epsilon = 1e-06
@@ -57,41 +56,44 @@
     odd = lax.rem(lax.axis_index("expert"), 2)
     per = REACH * kv_heads
 
-    early = near_ref.shape[0]
+    early = 2 * per + per // 2
 
     def halo(start, kinds, slot):
         for cache_ref, new_ref in kinds:
             for r in range(REACH):
                 for h in range(kv_heads):
                     out_ref, at = (near_ref, slot) if slot < early else (far_ref, slot - early)
-                    out_ref[at, :cached, :] = cache_ref[start + r, h]
-                    new = jnp.concatenate(
-                        [new_ref[s, start + r, h : h + 1, :].astype(f32) for s in range(steps)]
-                        + [jnp.zeros((PAD - steps, width), f32)], axis=0)
-                    out_ref[at, cached:, :] = new.astype(bf16)
+                    out_ref[at * cached : (at + 1) * cached, :] = cache_ref[start + r, h]
+                    yield from (new_ref[s, start + r, h : h + 1, :].astype(f32) for s in range(steps))
                     slot += 1
+
+    def fill(near, far):
+        rows = [*halo(near, (keys, values), 0), *halo(far, (keys, values), 2 * per)]
+        for out_ref, own in ((near_ref, rows[: early * steps]), (far_ref, rows[early * steps :])):
+            below = out_ref.shape[0] - len(own) // steps * cached
+            block = jnp.concatenate(own + [jnp.zeros((below - len(own), width), f32)], axis=0)
+            out_ref[out_ref.shape[0] - below :, :] = block.astype(bf16)
 
     keys, values = (ck_ref, nk_ref), (cv_ref, nv_ref)
     tail = tokens - REACH
 
     @pl.when(odd == 0)
     def _():
-        halo(tail, (keys, values), 0)
-        halo(0, (keys, values), 2 * per)
+        fill(tail, 0)
 
     @pl.when(odd == 1)
     def _():
-        halo(0, (keys, values), 0)
-        halo(tail, (keys, values), 2 * per)
-
-
-def weight_kernel(after_ref, source, target, token_ref, sems):
+        fill(0, tail)
+
+
+def weight_kernel(after_ref, source, own_ref, other_ref, token_ref, sems):
+    half = own_ref.shape[1]
+    mine = lax.axis_index("tensor")
     copies = []
-    part = source.shape[1] // 2
-    for e in range(source.shape[0]):
-        for k in range(2):
-            at = pl.ds(k * part, part)
-            copies.append(pltpu.make_async_copy(source.at[e, at], target.at[e, at], sems.at[len(copies)]))
+    for target, place in ((own_ref, mine), (other_ref, 1 - mine)):
+        rows = pl.ds(pl.multiple_of(place * half, LANES), half)
+        for e in range(source.shape[0]):
+            copies.append(pltpu.make_async_copy(source.at[e, rows], target.at[e], sems.at[len(copies)]))
     for copy in copies:
         copy.start()
     for copy in copies:
@@ -218,22 +220,18 @@
     return jnp.concatenate([even_ref[:, at], odd_ref[:, at]], axis=0)
 
 
-def expert_products(steps, tokens, features, gate_ref, up_ref, half):
+def expert_products(steps, tokens, features, gate_ref, up_ref):
     main = features.shape[1]
-    part = main // steps
-    columns = main + part
     local = gate_ref.shape[0]
     extra = unpacked(features.astype(f32), steps, tokens).astype(bf16)
-    first = pl.ds(pl.multiple_of(half * columns, LANES), main)
-    last = pl.ds(pl.multiple_of(half * columns + main, LANES), part)
     return [
-        dot(features, ref[e, first, :]) + dot(extra, ref[e, last, :]) for ref in (gate_ref, up_ref) for e in range(local)
+        dot(features, ref[e, :main, :]) + dot(extra, ref[e, main:, :]) for ref in (gate_ref, up_ref) for e in range(local)
     ]
 
 
 def partial_kernel(steps, tokens, after_ref, also_after_ref, even_ref, odd_ref, gate_ref, up_ref, out_ref):
     main = even_ref.shape[1] - LANES
-    products = expert_products(steps, tokens, halves(even_ref, odd_ref, slice(0, main)), gate_ref, up_ref, lax.axis_index("tensor"))
+    products = expert_products(steps, tokens, halves(even_ref, odd_ref, slice(0, main)), gate_ref, up_ref)
     for n, product in enumerate(products):
         out_ref[n] = product
 
@@ -245,7 +243,7 @@
     columns = main + main // steps
     local, _, units = gate_ref.shape
     features = halves(even_other_ref, odd_other_ref, slice(0, main))
-    products = expert_products(steps, tokens, features, gate_ref, up_ref, 1 - lax.axis_index("tensor"))
+    products = expert_products(steps, tokens, features, gate_ref, up_ref)
     meta = halves(even_ref, odd_ref, slice(main, None)).astype(f32)
     meta_other = halves(even_other_ref, odd_other_ref, slice(main, None)).astype(f32)
     lane = iota(meta.shape, 1)
@@ -278,6 +276,12 @@
     leaving_ref[...] = product[total // 2 :].astype(bf16)
 
 
+def join_kernel(near_ref, rest_ref, out_ref):
+    ahead = out_ref.shape[0] - rest_ref.shape[0]
+    out_ref[:ahead, :] = near_ref[near_ref.shape[0] - ahead :, :]
+    out_ref[ahead:, :] = rest_ref[...]
+
+
 def resample_kernel(steps, early, counts_ref, near_ref, relay_ref, ck_ref, cv_ref, nk_ref, nv_ref, keys_ref, values_ref):
     tokens, kv_heads, cached, width = ck_ref.shape
     devices = counts_ref.shape[0]
@@ -304,23 +308,42 @@
                 for s in range(steps):
                     out_ref[i, cached + s] = new_ref[s, offset]
 
-        def from_halo(ref, at):
+        def near_rows(slot):
+            return slot * cached, early * cached + slot * steps
+
+        def far_rows(slot):
+            ahead = early - 2 * per
+            if slot < ahead:
+                return slot * cached, ahead * cached + (2 * per + slot) * steps
+            begin = near_ref.shape[0] - 2 * per * cached
+            return begin + (slot - ahead) * cached, begin + (2 * per - ahead) * cached + (slot - ahead) * steps
+
+        def from_halo(ref, rows_of, at):
             for kind, out_ref in enumerate((keys_ref, values_ref)):
-                slots = ref[pl.ds(kind * per + at * kv_heads, kv_heads)]
-                out_ref[i] = jnp.swapaxes(slots[:, : cached + steps], 0, 1)
-
-        left = offset < 0
-        near = (left & (odd == 1)) | ((offset >= tokens) & (odd == 0))
-        far = (left & (odd == 0)) | ((offset >= tokens) & (odd == 1))
+                places = [rows_of(kind * per + at * kv_heads + h) for h in range(kv_heads)]
+                first_row, first_new = places[0]
+                block = ref[first_row : first_row + kv_heads * cached, :].reshape(kv_heads, cached, width)
+                out_ref[i, :cached] = jnp.swapaxes(block, 0, 1)
+                aligned = first_new // 16 * 16
+                fresh = ref[aligned : aligned + 32, :].astype(f32) if aligned + 32 <= ref.shape[0] else ref[ref.shape[0] - 32 :, :].astype(f32)
+                aligned = min(aligned, ref.shape[0] - 32)
+                for s in range(steps):
+                    pair = [fresh[place + s - aligned : place + s - aligned + 1] for _, place in places]
+                    out_ref[i, cached + s] = jnp.concatenate(pair, axis=0).astype(bf16)
+
+        left, right = offset < 0, offset >= tokens
+        near = (left & (odd == 1)) | (right & (odd == 0))
+        far = (left & (odd == 0)) | (right & (odd == 1))
         at = jnp.where(left, offset + REACH, offset - tokens)
-
-        @pl.when(near)
-        def _():
-            from_halo(near_ref, at)
-
-        @pl.when(far)
-        def _():
-            from_halo(relay_ref, at)
+        for n in range(REACH):
+
+            @pl.when(near & (at == n))
+            def _():
+                from_halo(near_ref, near_rows, n)
+
+            @pl.when(far & (at == n))
+            def _():
+                from_halo(relay_ref, far_rows, n)
 
 
 def add_kernel(a_ref, b_ref, out_ref):
@@ -389,7 +412,7 @@
     early = 2 * per + per // 2
     square = steps * tokens * heads
     chosen = pltpu.VMEM((square, square), bf16)
-    halos = [pltpu.VMEM((slots, cached + PAD, width), bf16) for slots in (early, 4 * per - early)]
+    halos = [pltpu.VMEM((slots * cached + -(-slots * steps // 16) * 16, width), bf16) for slots in (early, 4 * per - early)]
 
     def swap(value, offset):
         return lax.ppermute(value, "expert", [(i, i ^ offset) for i in range(count)])
@@ -417,29 +440,30 @@
 
     far_first = range(count - 2, 0, -2)
     def fetch(after, weight, name):
+        half = pltpu.VMEM((local, columns, units), weight.dtype)
         return pl.pallas_call(
-            weight_kernel, out_shape=[pltpu.VMEM(weight.shape, weight.dtype), pltpu.VMEM((8, LANES), f32)],
-            in_specs=[VMEM, HBM], out_specs=[VMEM] * 2, scratch_shapes=[pltpu.SemaphoreType.DMA((2 * local,))], name=name,
+            weight_kernel, out_shape=[half, half, pltpu.VMEM((8, LANES), f32)],
+            in_specs=[VMEM, HBM], out_specs=[VMEM] * 3, scratch_shapes=[pltpu.SemaphoreType.DMA((2 * local,))], name=name,
             cost_estimate=pl.CostEstimate(flops=0, bytes_accessed=7_000_000, transcendentals=0),
             compiler_params=pltpu.CompilerParams(vmem_limit_bytes=16 << 20),
         )(after, in_hbm(weight))
 
-    gate, token = fetch(residual, gate_weight, "gate")
+    gate_own, gate_other, token = fetch(residual, gate_weight, "gate")
     even = jnp.concatenate([send] + [swap(send, k) for k in far_first], axis=0)
     even, near, token = lax.optimization_barrier((even, near, token))
     odd = swap(even, 1)
     even_other = sibling(even)
-    up, token_up = fetch(even, up_weight, "up")
+    up_own, up_other, token_up = fetch(even, up_weight, "up")
     odd, token_up, far = lax.optimization_barrier((odd, token_up, far))
     relayed = swap(far, 1)
     odd_other = sibling(odd)
     partial = call(
         functools.partial(partial_kernel, steps, tokens), struct((2 * local, count * rows, units), f32), [VMEM] * 6, "partial", 0.01,
-    )(token, token_up, even, odd, gate, up)
+    )(token, token_up, even, odd, gate_own, up_own)
     hidden = call(
         functools.partial(hidden_kernel, steps, tokens, experts),
         struct((count * rows, local * units), bf16), [VMEM] * 7, "hidden", 0.01,
-    )(partial, even, odd, even_other, odd_other, gate, up)
+    )(partial, even, odd, even_other, odd_other, gate_other, up_other)
     other_hidden = sibling(hidden)
     half = count // 2 * rows
 
@@ -449,7 +473,8 @@
     leaving, relayed = lax.optimization_barrier((leaving, relayed))
     arrived = swap(leaving, 1)
     ring = [(i, i + 2 if i % 2 == 0 else i - 2) for i in range(count) if (i < count - 2 if i % 2 == 0 else i > 1)]
-    far = lax.ppermute(jnp.concatenate([near[2 * per :], relayed], axis=0), "expert", ring)
+    joined = struct((near.shape[0] - 2 * per * cached + relayed.shape[0], width), bf16)
+    far = lax.ppermute(call(join_kernel, joined, [VMEM] * 2, "join", 0.1)(near, relayed), "expert", ring)
     own_block, others = kept[:rows], call(add_kernel, struct((half - rows, main), bf16), [VMEM] * 2, "add", 0.1)(kept[rows:], arrived[rows:])
 
     counts = [block.reshape(count // 2, rows, main + LANES)[:, :tokens, main + 2 * experts + 2].astype(jnp.int32) for block in (even, odd)]

time: 45.1 us -> 44.8 us (level)
    pallas_call x2 -> x3, Pallas kernels: 5.73 us -> 5.75 us  [the longest x2 5.73 us: fetch(): pl.pallas_call(weight_kernel, out_shape=[half, half, pltpu.VMEM((8, LANES...]
  transfers between devices with their start and end apart: 15 -> 15, of which waited for: 8 -> 8; matrix products, arithmetic and copies ran while one was open for 1% -> 1% of each run, Pallas kernels for 28% -> 29%
where the time goes in v6:
time: 44.8 us; the launch traced here: 44.2 us
  starting transfers between devices  17.1 us (38%)
  Pallas kernels  14.6 us (33%)
  waiting for transfers between devices  11.2 us (25%)
  between operations  0.81 us (2%)
  local copies, waits for them, and re-layouts  0.5 us (1%)
    ppermute x10, starting transfers between devices, swap(): lax.ppermute(value, 'expert', [(i, i ^ offset) for i in range(count)])  13.6 us
    ppermute x10, waiting for transfers between devices, swap(): lax.ppermute(value, 'expert', [(i, i ^ offset) for i in range(count)])  8.64 us
    pallas_call x2, Pallas kernels, fetch(): pl.pallas_call(weight_kernel, out_shape=[half, half, pltpu.VMEM((8, LANES...  5.73 us
    ppermute x1, starting transfers between devices, fast_shards(): lax.ppermute(call(join_kernel, joined, [VMEM] * 2, 'join', 0.1)(near, rel...  3.14 us
    ppermute x4, waiting for transfers between devices, sibling(): return lax.ppermute(value, 'tensor', [(0, 1), (1, 0)])  2.44 us
    pallas_call x1, Pallas kernels, fast_shards(): call(functools.partial(resample_kernel, steps, early), (out, out), [SMEM]...  2.06 us
    pallas_call x1, Pallas kernels, fast_shards(): call(functools.partial(hidden_kernel, steps, tokens, experts), struct((co...  1.32 us
    pallas_call x1, Pallas kernels, fast_shards(): pl.pallas_call(functools.partial(load_kernel, steps), out_shape=[space(va...  1.28 us
  transfers between devices with their start and end apart: 15, of which 8 were waited for; matrix products, arithmetic and copies ran while one was open for 1% of the time, Pallas kernels for 29%

profile of v6, /device:TPU:0, one launch (start us, length us, event | category | flops | bytes accessed | tf_op | source)
XLA Modules:
  0.0 44.2 jit_solution(8702419163636357597)
XLA Ops:
  0.6 1.3 %load.1 = (s32[3,4,8]{2,1,0:T(4,128)S(1)}, f32[3,4,8]{2,1,0:T(4,128)S(1)}, s32[4]{0:T(128)S(4)}, f32[1,4096]{1,0:T(1,128)S(1)}, bf16[3,4,4096]{2,1,0:T(4,128)(2,...) custom-call(s32[3,4,8]{2,1,0:T(4,128)} %ids_in.1, ...), custom_call_target="tpu_custom_call" | custom-call | tf_op jit(solution)/shard_map/load/pallas_call | solution.py:425
  1.9 3.0 %collective-permute-start.3 = (bf16[1312,128]{1,0:T(8,128)(2,1)S(1)}, bf16[1312,128]{1,0:T(8,128)(2,1)S(1)}, u32[]{:S(2)}, u32[]{:S(2)}) collective-permute-start(bf16[1312,128]{1,0:T(8,128)(2,1)S(1)} %get-tuple-element.54), channel_id=1, source_target_pairs={{0,2},{2,0},{4,6},{6,4},{8,10},{10,8},{12,14},{14,12},{1,3},{3,1},... | collective-permute-start | bytes 1007624 | tf_op jit(solution)/shard_map/ppermute | solution.py:418
  4.9 0.9 %attend.1 = (bf16[16,1664]{1,0:T(8,128)(2,1)S(1)}, f32[16,1536]{1,0:T(8,128)S(1)}) custom-call(s32[3,4,8]{2,1,0:T(4,128)S(1)} %get-tuple-element.41.ids_ref, f32[3,4,8]{2,1,0:T(4,128)S(1)} %get-tuple-element.42.weights_ref, s32[4]{0:T(128)S(4)} %get-tuple-element.43.counts_ref, f32[1,4096]{1,0:T(1,128)S(1)} %get-tuple-element.44.gain_ref, ...), custom_call_target="tpu_custom_call" | custom-call | bytes 8049999 | tf_op jit(solution)/shard_map/attend/pallas_call | solution.py:435
  5.9 3.7 %collective-permute-start = (bf16[16,1664]{1,0:T(8,128)(2,1)S(1)}, bf16[16,1664]{1,0:T(8,128)(2,1)S(1)}, u32[]{:S(2)}, u32[]{:S(2)}) collective-permute-start(bf16[16,1664]{1,0:T(8,128)(2,1)S(1)} %get-tuple-element.53), channel_id=1, source_target_pairs={{0,12},{2,14},{4,8},{6,10},{8,4},{10,6},{12,0},{14,2},{1,13},{3,15... | collective-permute-start | bytes 159752 | tf_op jit(solution)/shard_map/ppermute | solution.py:418
  9.5 0.0 collective-permute-start.1
  9.5 0.8 %collective-permute-start.2 = (bf16[16,1664]{1,0:T(8,128)(2,1)S(1)}, bf16[16,1664]{1,0:T(8,128)(2,1)S(1)}, u32[]{:S(2)}, u32[]{:S(2)}) collective-permute-start(bf16[16,1664]{1,0:T(8,128)(2,1)S(1)} %get-tuple-element.53), channel_id=1, source_target_pairs={{0,4},{2,6},{4,0},{6,2},{8,12},{10,14},{12,8},{14,10},{1,5},{3,7},... | collective-permute-start | bytes 159752 | tf_op jit(solution)/shard_map/ppermute | solution.py:418
  10.3 2.9 %gate.1 = (bf16[2,2048,384]{2,1,0:T(8,128)(2,1)S(1)}, bf16[2,2048,384]{2,1,0:T(8,128)(2,1)S(1)}, f32[8,128]{1,0:T(8,128)S(1)}) custom-call(f32[16,1536]{1,0:T(8,128)S(1)} %get-tuple-element.52.after_ref.refs_0_, bf16[2,4096,384]{2,1,0:T(8,128)(2,1)} %source.2), custom_call_target="tpu_custom_call" | custom-call | bytes 7000000 | tf_op jit(solution)/shard_map/gate/pallas_call | solution.py:444
  13.2 0.0 collective-permute-done
  13.2 1.4 %collective-permute-done.1 = bf16[16,1664]{1,0:T(8,128)(2,1)S(1)} collective-permute-done((bf16[16,1664]{1,0:T(8,128)(2,1)S(1)}, bf16[16,1664]{1,0:T(8,128)(2,1)S(1)}, u32[]{:S(2)}, u32[]{:S(2)}) %collective-permute-start.1) | collective-permute-done | bytes 53280 | tf_op jit(solution)/shard_map/ppermute | solution.py:418
  14.6 0.0 collective-permute-done.2
  14.6 0.0 collective-permute-done.3.near_ref
  14.6 0.6 %collective-permute-start.4 = (bf16[64,1664]{1,0:T(8,128)(2,1)S(1)}, bf16[64,1664]{1,0:T(8,128)(2,1)S(1)}, u32[]{:S(2)}, u32[]{:S(2)}) collective-permute-start(bf16[64,1664]{1,0:T(8,128)(2,1)S(1)} %pad_maximum_fusion.after_ref.even_ref), channel_id=1, source_target_pairs={{0,2},{2,0},{4,6},{6,4},{8,10},{10,8},{12,14},{14,12},{1,3},{3,1},... | collective-permute-start | bytes 638984 | tf_op jit(solution)/shard_map/ppermute | solution.py:418
  15.2 0.0 collective-permute-start.5
  15.2 2.9 %up.1 = (bf16[2,2048,384]{2,1,0:T(8,128)(2,1)S(1)}, bf16[2,2048,384]{2,1,0:T(8,128)(2,1)S(1)}, f32[8,128]{1,0:T(8,128)S(1)}) custom-call(bf16[64,1664]{1,0:T(8,128)(2,1)S(1)} %pad_maximum_fusion.after_ref.even_ref, bf16[2,4096,384]{2,1,0:T(8,128)(2,1)} %source.3), custom_call_target="tpu_custom_call" | custom-call | bytes 7000000 | tf_op jit(solution)/shard_map/up/pallas_call | solution.py:444
  18.1 2.4 %collective-permute-done.4.odd_ref = bf16[64,1664]{1,0:T(8,128)(2,1)S(1)} collective-permute-done((bf16[64,1664]{1,0:T(8,128)(2,1)S(1)}, bf16[64,1664]{1,0:T(8,128)(2,1)S(1)}, u32[]{:S(2)}, u32[]{:S(2)}) %collective-permute-start.4) | collective-permute-done | bytes 213024 | tf_op jit(solution)/shard_map/ppermute | solution.py:418
  20.5 0.0 collective-permute-start.6
  20.5 0.5 %collective-permute-start.8 = (bf16[800,128]{1,0:T(8,128)(2,1)S(1)}, bf16[800,128]{1,0:T(8,128)(2,1)S(1)}, u32[]{:S(2)}, u32[]{:S(2)}) collective-permute-start(bf16[800,128]{1,0:T(8,128)(2,1)S(1)} %get-tuple-element.68), channel_id=1, source_target_pairs={{0,2},{2,0},{4,6},{6,4},{8,10},{10,8},{12,14},{14,12},{1,3},{3,1},... | collective-permute-start | bytes 614408 | tf_op jit(solution)/shard_map/ppermute | solution.py:418
  21.0 0.0 slice-start
  21.0 1.3 %partial.1.partial_ref = f32[4,128,384]{2,1,0:T(8,128)S(1)} custom-call(f32[8,128]{1,0:T(8,128)S(1)} %get-tuple-element.56.after_ref, f32[8,128]{1,0:T(8,128)S(1)} %get-tuple-element.60.also_after_ref, bf16[64,1664]{1,0:T(8,128)(2,1)S(1)} %pad_maximum_fusion.after_ref.even_ref, bf16[64,1664]{1,0:T(8,128)(2,1)S(1)} %collective-permute-done.4.odd_ref, ...), custom_call_target="tpu_custom_call" | custom-call | bytes 35000 | tf_op jit(solution)/shard_map/partial/pallas_call | solution.py:460
  22.3 0.0 collective-permute-done.5.even_other_ref
  22.3 0.0 collective-permute-done.6.odd_other_ref
  22.3 0.0 slice-start.1
  22.4 1.3 %hidden.1.own_ref = bf16[128,768]{1,0:T(8,128)(2,1)S(1)} custom-call(f32[4,128,384]{2,1,0:T(8,128)S(1)} %partial.1.partial_ref, bf16[64,1664]{1,0:T(8,128)(2,1)S(1)} %pad_maximum_fusion.after_ref.even_ref, bf16[64,1664]{1,0:T(8,128)(2,1)S(1)} %collective-permute-done.4.odd_ref, bf16[64,1664]{1,0:T(8,128)(2,1)S(1)} %collective-permute-done.5.even_other_ref, ...), custom_call_target="tpu_custom_call" | custom-call | bytes 35000 | tf_op jit(solution)/shard_map/hidden/pallas_call | solution.py:463
  23.7 0.3 collective-permute-start.7
  24.0 1.2 %collective-permute-done.7.other_ref = bf16[128,768]{1,0:T(8,128)(2,1)S(1)} collective-permute-done((bf16[128,768]{1,0:T(8,128)(2,1)S(1)}, bf16[128,768]{1,0:T(8,128)(2,1)S(1)}, u32[]{:S(2)}, u32[]{:S(2)}) %collective-permute-start.7) | collective-permute-done | bytes 196640 | tf_op jit(solution)/shard_map/ppermute | solution.py:421
  25.2 0.0 slice-done
  25.2 0.0 slice-done.1
  25.2 1.3 %down.1 = (f32[64,1536]{1,0:T(8,128)S(1)}, bf16[64,1536]{1,0:T(8,128)(2,1)S(1)}) custom-call(bf16[128,768]{1,0:T(8,128)(2,1)S(1)} %hidden.1.own_ref, bf16[128,768]{1,0:T(8,128)(2,1)S(1)} %collective-permute-done.7.other_ref, bf16[2,768,2048]{2,1,0:T(8,128)(2,1)S(1)} %bitcast.22), custom_call_target="tpu_custom_call" | custom-call | bytes 35000 | tf_op jit(solution)/shard_map/down/pallas_call | solution.py:470
  26.5 1.5 %collective-permute-done.8.rest_ref = bf16[800,128]{1,0:T(8,128)(2,1)S(1)} collective-permute-done((bf16[800,128]{1,0:T(8,128)(2,1)S(1)}, bf16[800,128]{1,0:T(8,128)(2,1)S(1)}, u32[]{:S(2)}, u32[]{:S(2)}) %collective-permute-start.8) | collective-permute-done | bytes 204832 | tf_op jit(solution)/shard_map/ppermute | solution.py:418
  28.0 0.5 %collective-permute-start.9 = (bf16[64,1536]{1,0:T(8,128)(2,1)S(1)}, bf16[64,1536]{1,0:T(8,128)(2,1)S(1)}, u32[]{:S(2)}, u32[]{:S(2)}) collective-permute-start(bf16[64,1536]{1,0:T(8,128)(2,1)S(1)} %get-tuple-element.69), channel_id=1, source_target_pairs={{0,2},{2,0},{4,6},{6,4},{8,10},{10,8},{12,14},{14,12},{1,3},{3,1},... | collective-permute-start | bytes 589832 | tf_op jit(solution)/shard_map/ppermute | solution.py:418
  28.5 0.1 slice.101
  28.6 0.1 copy.18
  28.7 0.1 slice.103
  28.8 0.1 copy.19
  29.0 3.1 %collective-permute-start.10 = (bf16[1088,128]{1,0:T(8,128)(2,1)S(1)}, bf16[1088,128]{1,0:T(8,128)(2,1)S(1)}, u32[]{:S(2)}, u32[]{:S(2)}) collective-permute-start(bf16[1088,128]{1,0:T(8,128)(2,1)S(1)} %join.1), channel_id=1, source_target_pairs={{0,4},{4,8},{6,2},{8,12},{10,6},{14,10},{1,5},{5,9},{7,3},{9,13},{... | collective-permute-start | bytes 835592 | tf_op jit(solution)/shard_map/ppermute | solution.py:477
  32.2 2.4 %collective-permute-done.9 = bf16[64,1536]{1,0:T(8,128)(2,1)S(1)} collective-permute-done((bf16[64,1536]{1,0:T(8,128)(2,1)S(1)}, bf16[64,1536]{1,0:T(8,128)(2,1)S(1)}, u32[]{:S(2)}, u32[]{:S(2)}) %collective-permute-start.9) | collective-permute-done | bytes 196640 | tf_op jit(solution)/shard_map/ppermute | solution.py:418
  34.6 2.4 %collective-permute-start.11 = (bf16[16,1536]{1,0:T(8,128)(2,1)S(1)}, bf16[16,1536]{1,0:T(8,128)(2,1)S(1)}, u32[]{:S(2)}, u32[]{:S(2)}) collective-permute-start(bf16[16,1536]{1,0:T(8,128)(2,1)S(1)} %get-tuple-element.81), channel_id=1, source_target_pairs={{0,12},{2,14},{4,8},{6,10},{8,4},{10,6},{12,0},{14,2},{1,13},{3,15... | collective-permute-start | bytes 147464 | tf_op jit(solution)/shard_map/ppermute | solution.py:418
  37.0 0.0 collective-permute-start.12
  37.0 2.1 %collective-permute-start.13 = (bf16[16,1536]{1,0:T(8,128)(2,1)S(1)}, bf16[16,1536]{1,0:T(8,128)(2,1)S(1)}, u32[]{:S(2)}, u32[]{:S(2)}) collective-permute-start(bf16[16,1536]{1,0:T(8,128)(2,1)S(1)} %get-tuple-element.79), channel_id=1, source_target_pairs={{0,4},{2,6},{4,0},{6,2},{8,12},{10,14},{12,8},{14,10},{1,5},{3,7},... | collective-permute-start | bytes 147464 | tf_op jit(solution)/shard_map/ppermute | solution.py:418
  39.1 0.1 collective-permute-done.10.relay_ref
  39.2 2.1 %resample.1 = (bf16[4,131,2,128]{3,2,1,0:T(2,128)(2,1)}, bf16[4,131,2,128]{3,2,1,0:T(2,128)(2,1)}) custom-call(s32[8,4]{1,0:T(8,128)S(1)} %stack.3.counts_ref, bf16[1312,128]{1,0:T(8,128)(2,1)S(1)} %collective-permute-done.3.near_ref, bf16[1088,128]{1,0:T(8,128)(2,1)S(1)} %collective-permute-done.10.relay_ref, ...), custom_call_target="tpu_custom_call" | custom-call | bytes 7700000 | tf_op jit(solution)/shard_map/resample/pallas_call | solution.py:484
  41.3 0.0 collective-permute-done.11.refs_3_
  41.3 0.9 %collective-permute-done.12.refs_4_ = bf16[16,1536]{1,0:T(8,128)(2,1)S(1)} collective-permute-done((bf16[16,1536]{1,0:T(8,128)(2,1)S(1)}, bf16[16,1536]{1,0:T(8,128)(2,1)S(1)}, u32[]{:S(2)}, u32[]{:S(2)}) %collective-permute-start.12) | collective-permute-done | bytes 49184 | tf_op jit(solution)/shard_map/ppermute | solution.py:418
  42.2 0.0 collective-permute-done.13.refs_5_
  42.3 0.1 collective-permute-start.14
  42.3 1.2 %collective-permute-done.14.other_ref = bf16[16,1536]{1,0:T(8,128)(2,1)S(1)} collective-permute-done((bf16[16,1536]{1,0:T(8,128)(2,1)S(1)}, bf16[16,1536]{1,0:T(8,128)(2,1)S(1)}, u32[]{:S(2)}, u32[]{:S(2)}) %collective-permute-start.14) | collective-permute-done | bytes 49184 | tf_op jit(solution)/shard_map/ppermute | solution.py:421
  43.5 0.7 %unpack.1 = bf16[3,4,4096]{2,1,0:T(4,128)(2,1)} custom-call(bf16[16,1536]{1,0:T(8,128)(2,1)S(1)} %total.1.own_ref, bf16[16,1536]{1,0:T(8,128)(2,1)S(1)} %collective-permute-done.14.other_ref), custom_call_target="tpu_custom_call" | custom-call | bytes 1750000 | tf_op jit(solution)/shard_map/unpack/pallas_call | solution.py:492
  (14 shorter events, 0.2 us)
Async XLA Ops:
  1.9 12.7 %collective-permute-start.3 = (bf16[1312,128]{1,0:T(8,128)(2,1)S(1)}, bf16[1312,128]{1,0:T(8,128)(2,1)S(1)}, u32[]{:S(2)}, u32[]{:S(2)}) collective-permute-start(bf16[1312,128]{1,0:T(8,128)(2,1)S(1)} %get-tuple-element.54), channel_id=1, source_target_pairs={{0,2},{2,0},{4,6},{6,4},{8,10},{10,8},{12,14},{14,12},{1,3},{3,1},... | collective-permute-start | bytes 1007624 | tf_op jit(solution)/shard_map/ppermute | solution.py:418
  5.9 7.3 %collective-permute-start = (bf16[16,1664]{1,0:T(8,128)(2,1)S(1)}, bf16[16,1664]{1,0:T(8,128)(2,1)S(1)}, u32[]{:S(2)}, u32[]{:S(2)}) collective-permute-start(bf16[16,1664]{1,0:T(8,128)(2,1)S(1)} %get-tuple-element.53), channel_id=1, source_target_pairs={{0,12},{2,14},{4,8},{6,10},{8,4},{10,6},{12,0},{14,2},{1,13},{3,15... | collective-permute-start | bytes 159752 | tf_op jit(solution)/shard_map/ppermute | solution.py:418
  9.5 5.0 %collective-permute-start.1 = (bf16[16,1664]{1,0:T(8,128)(2,1)S(1)}, bf16[16,1664]{1,0:T(8,128)(2,1)S(1)}, u32[]{:S(2)}, u32[]{:S(2)}) collective-permute-start(bf16[16,1664]{1,0:T(8,128)(2,1)S(1)} %get-tuple-element.53), channel_id=1, source_target_pairs={{0,8},{2,10},{4,12},{6,14},{8,0},{10,2},{12,4},{14,6},{1,9},{3,11}... | collective-permute-start | bytes 159752 | tf_op jit(solution)/shard_map/ppermute | solution.py:418
  9.5 5.0 %collective-permute-start.2 = (bf16[16,1664]{1,0:T(8,128)(2,1)S(1)}, bf16[16,1664]{1,0:T(8,128)(2,1)S(1)}, u32[]{:S(2)}, u32[]{:S(2)}) collective-permute-start(bf16[16,1664]{1,0:T(8,128)(2,1)S(1)} %get-tuple-element.53), channel_id=1, source_target_pairs={{0,4},{2,6},{4,0},{6,2},{8,12},{10,14},{12,8},{14,10},{1,5},{3,7},... | collective-permute-start | bytes 159752 | tf_op jit(solution)/shard_map/ppermute | solution.py:418
  14.6 5.9 %collective-permute-start.4 = (bf16[64,1664]{1,0:T(8,128)(2,1)S(1)}, bf16[64,1664]{1,0:T(8,128)(2,1)S(1)}, u32[]{:S(2)}, u32[]{:S(2)}) collective-permute-start(bf16[64,1664]{1,0:T(8,128)(2,1)S(1)} %pad_maximum_fusion.after_ref.even_ref), channel_id=1, source_target_pairs={{0,2},{2,0},{4,6},{6,4},{8,10},{10,8},{12,14},{14,12},{1,3},{3,1},... | collective-permute-start | bytes 638984 | tf_op jit(solution)/shard_map/ppermute | solution.py:418
  15.2 7.1 %collective-permute-start.5 = (bf16[64,1664]{1,0:T(8,128)(2,1)S(1)}, bf16[64,1664]{1,0:T(8,128)(2,1)S(1)}, u32[]{:S(2)}, u32[]{:S(2)}) collective-permute-start(bf16[64,1664]{1,0:T(8,128)(2,1)S(1)} %pad_maximum_fusion.after_ref.even_ref), channel_id=1, source_target_pairs={{0,1},{1,0},{2,3},{3,2},{4,5},{5,4},{6,7},{7,6},{8,9},{9,8},{10,11... | collective-permute-start | bytes 638984 | tf_op jit(solution)/shard_map/ppermute | solution.py:421
  20.5 1.8 %collective-permute-start.6 = (bf16[64,1664]{1,0:T(8,128)(2,1)S(1)}, bf16[64,1664]{1,0:T(8,128)(2,1)S(1)}, u32[]{:S(2)}, u32[]{:S(2)}) collective-permute-start(bf16[64,1664]{1,0:T(8,128)(2,1)S(1)} %collective-permute-done.4.odd_ref), channel_id=1, source_target_pairs={{0,1},{1,0},{2,3},{3,2},{4,5},{5,4},{6,7},{7,6},{8,9},{9,8},{10,11... | collective-permute-start | bytes 638984 | tf_op jit(solution)/shard_map/ppermute | solution.py:421
  20.5 7.5 %collective-permute-start.8 = (bf16[800,128]{1,0:T(8,128)(2,1)S(1)}, bf16[800,128]{1,0:T(8,128)(2,1)S(1)}, u32[]{:S(2)}, u32[]{:S(2)}) collective-permute-start(bf16[800,128]{1,0:T(8,128)(2,1)S(1)} %get-tuple-element.68), channel_id=1, source_target_pairs={{0,2},{2,0},{4,6},{6,4},{8,10},{10,8},{12,14},{14,12},{1,3},{3,1},... | collective-permute-start | bytes 614408 | tf_op jit(solution)/shard_map/ppermute | solution.py:418
  21.0 4.2 %slice-start = ((s8[6291456]{0:T(1024)(128)(4,1)}), s8[4194304]{0:T(1024)(128)(4,1)S(1)}, s32[]{:S(2)}) async-start(s8[6291456]{0:T(1024)(128)(4,1)} %bitcast.21), calls=%async_computation | async-start | bytes 8388608
  22.3 2.9 %slice-start.1 = ((s8[6291456]{0:T(1024)(128)(4,1)}), s8[2097152]{0:T(1024)(128)(4,1)S(1)}, s32[]{:S(2)}) async-start(s8[6291456]{0:T(1024)(128)(4,1)} %bitcast.21), calls=%async_computation.1 | async-start | bytes 4194304
  23.7 1.5 %collective-permute-start.7 = (bf16[128,768]{1,0:T(8,128)(2,1)S(1)}, bf16[128,768]{1,0:T(8,128)(2,1)S(1)}, u32[]{:S(2)}, u32[]{:S(2)}) collective-permute-start(bf16[128,768]{1,0:T(8,128)(2,1)S(1)} %hidden.1.own_ref), channel_id=1, source_target_pairs={{0,1},{1,0},{2,3},{3,2},{4,5},{5,4},{6,7},{7,6},{8,9},{9,8},{10,11... | collective-permute-start | bytes 589832 | tf_op jit(solution)/shard_map/ppermute | solution.py:421
  28.0 6.5 %collective-permute-start.9 = (bf16[64,1536]{1,0:T(8,128)(2,1)S(1)}, bf16[64,1536]{1,0:T(8,128)(2,1)S(1)}, u32[]{:S(2)}, u32[]{:S(2)}) collective-permute-start(bf16[64,1536]{1,0:T(8,128)(2,1)S(1)} %get-tuple-element.69), channel_id=1, source_target_pairs={{0,2},{2,0},{4,6},{6,4},{8,10},{10,8},{12,14},{14,12},{1,3},{3,1},... | collective-permute-start | bytes 589832 | tf_op jit(solution)/shard_map/ppermute | solution.py:418
  29.0 10.2 %collective-permute-start.10 = (bf16[1088,128]{1,0:T(8,128)(2,1)S(1)}, bf16[1088,128]{1,0:T(8,128)(2,1)S(1)}, u32[]{:S(2)}, u32[]{:S(2)}) collective-permute-start(bf16[1088,128]{1,0:T(8,128)(2,1)S(1)} %join.1), channel_id=1, source_target_pairs={{0,4},{4,8},{6,2},{8,12},{10,6},{14,10},{1,5},{5,9},{7,3},{9,13},{... | collective-permute-start | bytes 835592 | tf_op jit(solution)/shard_map/ppermute | solution.py:477
  34.6 6.7 %collective-permute-start.11 = (bf16[16,1536]{1,0:T(8,128)(2,1)S(1)}, bf16[16,1536]{1,0:T(8,128)(2,1)S(1)}, u32[]{:S(2)}, u32[]{:S(2)}) collective-permute-start(bf16[16,1536]{1,0:T(8,128)(2,1)S(1)} %get-tuple-element.81), channel_id=1, source_target_pairs={{0,12},{2,14},{4,8},{6,10},{8,4},{10,6},{12,0},{14,2},{1,13},{3,15... | collective-permute-start | bytes 147464 | tf_op jit(solution)/shard_map/ppermute | solution.py:418
  37.0 5.2 %collective-permute-start.12 = (bf16[16,1536]{1,0:T(8,128)(2,1)S(1)}, bf16[16,1536]{1,0:T(8,128)(2,1)S(1)}, u32[]{:S(2)}, u32[]{:S(2)}) collective-permute-start(bf16[16,1536]{1,0:T(8,128)(2,1)S(1)} %get-tuple-element.80), channel_id=1, source_target_pairs={{0,8},{2,10},{4,12},{6,14},{8,0},{10,2},{12,4},{14,6},{1,9},{3,11}... | collective-permute-start | bytes 147464 | tf_op jit(solution)/shard_map/ppermute | solution.py:418
  37.0 5.2 %collective-permute-start.13 = (bf16[16,1536]{1,0:T(8,128)(2,1)S(1)}, bf16[16,1536]{1,0:T(8,128)(2,1)S(1)}, u32[]{:S(2)}, u32[]{:S(2)}) collective-permute-start(bf16[16,1536]{1,0:T(8,128)(2,1)S(1)} %get-tuple-element.79), channel_id=1, source_target_pairs={{0,4},{2,6},{4,0},{6,2},{8,12},{10,14},{12,8},{14,10},{1,5},{3,7},... | collective-permute-start | bytes 147464 | tf_op jit(solution)/shard_map/ppermute | solution.py:418
  42.3 1.3 %collective-permute-start.14 = (bf16[16,1536]{1,0:T(8,128)(2,1)S(1)}, bf16[16,1536]{1,0:T(8,128)(2,1)S(1)}, u32[]{:S(2)}, u32[]{:S(2)}) collective-permute-start(bf16[16,1536]{1,0:T(8,128)(2,1)S(1)} %total.1.own_ref), channel_id=1, source_target_pairs={{0,1},{1,0},{2,3},{3,2},{4,5},{5,4},{6,7},{7,6},{8,9},{9,8},{10,11... | collective-permute-start | bytes 147464 | tf_op jit(solution)/shard_map/ppermute | solution.py:421

commit v7 on v6

--- a/solution.py
+++ b/solution.py
@@ -86,11 +86,13 @@
         fill(0, tail)
 
 
-def weight_kernel(after_ref, source, own_ref, other_ref, token_ref, sems):
-    half = own_ref.shape[1]
+def weight_kernel(sides, after_ref, *refs):
+    sources, targets, token_ref, sems = refs[: len(sides)], refs[len(sides) : -2], refs[-2], refs[-1]
     mine = lax.axis_index("tensor")
     copies = []
-    for target, place in ((own_ref, mine), (other_ref, 1 - mine)):
+    for side, source, target in zip(sides, sources, targets):
+        half = target.shape[1]
+        place = mine if side == 0 else 1 - mine
         rows = pl.ds(pl.multiple_of(place * half, LANES), half)
         for e in range(source.shape[0]):
             copies.append(pltpu.make_async_copy(source.at[e, rows], target.at[e], sems.at[len(copies)]))
@@ -439,21 +441,23 @@
     )(*loaded)
 
     far_first = range(count - 2, 0, -2)
-    def fetch(after, weight, name):
-        half = pltpu.VMEM((local, columns, units), weight.dtype)
+    def fetch(after, parts, name):
+        half = pltpu.VMEM((local, columns, units), gate_weight.dtype)
+        sides = tuple(side for _, side in parts)
         return pl.pallas_call(
-            weight_kernel, out_shape=[half, half, pltpu.VMEM((8, LANES), f32)],
-            in_specs=[VMEM, HBM], out_specs=[VMEM] * 3, scratch_shapes=[pltpu.SemaphoreType.DMA((2 * local,))], name=name,
+            functools.partial(weight_kernel, sides), out_shape=[half] * len(parts) + [pltpu.VMEM((8, LANES), f32)],
+            in_specs=[VMEM] + [HBM] * len(parts), out_specs=[VMEM] * (len(parts) + 1),
+            scratch_shapes=[pltpu.SemaphoreType.DMA((len(parts) * local,))], name=name,
             cost_estimate=pl.CostEstimate(flops=0, bytes_accessed=7_000_000, transcendentals=0),
             compiler_params=pltpu.CompilerParams(vmem_limit_bytes=16 << 20),
-        )(after, in_hbm(weight))
-
-    gate_own, gate_other, token = fetch(residual, gate_weight, "gate")
+        )(after, *(in_hbm(weight) for weight, _ in parts))
+
+    gate_own, token = fetch(residual, [(gate_weight, 0)], "gate")
     even = jnp.concatenate([send] + [swap(send, k) for k in far_first], axis=0)
     even, near, token = lax.optimization_barrier((even, near, token))
     odd = swap(even, 1)
     even_other = sibling(even)
-    up_own, up_other, token_up = fetch(even, up_weight, "up")
+    gate_other, up_own, up_other, token_up = fetch(even, [(gate_weight, 1), (up_weight, 0), (up_weight, 1)], "rest")
     odd, token_up, far = lax.optimization_barrier((odd, token_up, far))
     relayed = swap(far, 1)
     odd_other = sibling(odd)
@@ -472,7 +476,7 @@
     )(hidden, other_hidden, down_weight)
     leaving, relayed = lax.optimization_barrier((leaving, relayed))
     arrived = swap(leaving, 1)
-    ring = [(i, i + 2 if i % 2 == 0 else i - 2) for i in range(count) if (i < count - 2 if i % 2 == 0 else i > 1)]
+    ring = [(i, min(i + 2, count - 1) if i % 2 == 0 else max(i - 2, 0)) for i in range(count) if i != 1]
     joined = struct((near.shape[0] - 2 * per * cached + relayed.shape[0], width), bf16)
     far = lax.ppermute(call(join_kernel, joined, [VMEM] * 2, "join", 0.1)(near, relayed), "expert", ring)
     own_block, others = kept[:rows], call(add_kernel, struct((half - rows, main), bf16), [VMEM] * 2, "add", 0.1)(kept[rows:], arrived[rows:])

time: 44.8 us -> 44.8 us (level)
  transfers between devices with their start and end apart: 15 -> 15, of which waited for: 8 -> 9; matrix products, arithmetic and copies ran while one was open for 1% -> 1% of each run, Pallas kernels for 29% -> 29%
where the time goes in v7:
time: 44.8 us; the launch traced here: 44.2 us
  starting transfers between devices  17.1 us (38%)
  Pallas kernels  14.6 us (33%)
  waiting for transfers between devices  11.2 us (25%)
  between operations  0.8 us (2%)
  local copies, waits for them, and re-layouts  0.5 us (1%)
    ppermute x10, starting transfers between devices, swap(): lax.ppermute(value, 'expert', [(i, i ^ offset) for i in range(count)])  13.6 us
    ppermute x10, waiting for transfers between devices, swap(): lax.ppermute(value, 'expert', [(i, i ^ offset) for i in range(count)])  8.64 us
    pallas_call x2, Pallas kernels, fetch(): pl.pallas_call(functools.partial(weight_kernel, sides), out_shape=[half]...  5.68 us
    ppermute x1, starting transfers between devices, fast_shards(): lax.ppermute(call(join_kernel, joined, [VMEM] * 2, 'join', 0.1)(near, rel...  3.14 us
    ppermute x4, waiting for transfers between devices, sibling(): return lax.ppermute(value, 'tensor', [(0, 1), (1, 0)])  2.46 us
    pallas_call x1, Pallas kernels, fast_shards(): call(functools.partial(resample_kernel, steps, early), (out, out), [SMEM]...  2.06 us
    pallas_call x1, Pallas kernels, fast_shards(): call(functools.partial(hidden_kernel, steps, tokens, experts), struct((co...  1.36 us
    pallas_call x1, Pallas kernels, fast_shards(): pl.pallas_call(functools.partial(load_kernel, steps), out_shape=[space(va...  1.28 us
  transfers between devices with their start and end apart: 15, of which 9 were waited for; matrix products, arithmetic and copies ran while one was open for 1% of the time, Pallas kernels for 29%

profile of v7, /device:TPU:0, one launch (start us, length us, event | category | flops | bytes accessed | tf_op | source)
XLA Modules:
  0.0 44.2 jit_solution(15859223681698106145)
XLA Ops:
  0.6 1.3 %load.1 = (s32[3,4,8]{2,1,0:T(4,128)S(1)}, f32[3,4,8]{2,1,0:T(4,128)S(1)}, s32[4]{0:T(128)S(4)}, f32[1,4096]{1,0:T(1,128)S(1)}, bf16[3,4,4096]{2,1,0:T(4,128)(2,...) custom-call(s32[3,4,8]{2,1,0:T(4,128)} %ids_in.1, ...), custom_call_target="tpu_custom_call" | custom-call | tf_op jit(solution)/shard_map/load/pallas_call | solution.py:427
  1.9 3.0 %collective-permute-start.3 = (bf16[1312,128]{1,0:T(8,128)(2,1)S(1)}, bf16[1312,128]{1,0:T(8,128)(2,1)S(1)}, u32[]{:S(2)}, u32[]{:S(2)}) collective-permute-start(bf16[1312,128]{1,0:T(8,128)(2,1)S(1)} %get-tuple-element.54), channel_id=1, source_target_pairs={{0,2},{2,0},{4,6},{6,4},{8,10},{10,8},{12,14},{14,12},{1,3},{3,1},... | collective-permute-start | bytes 1007624 | tf_op jit(solution)/shard_map/ppermute | solution.py:420
  4.9 0.9 %attend.1 = (bf16[16,1664]{1,0:T(8,128)(2,1)S(1)}, f32[16,1536]{1,0:T(8,128)S(1)}) custom-call(s32[3,4,8]{2,1,0:T(4,128)S(1)} %get-tuple-element.41.ids_ref, f32[3,4,8]{2,1,0:T(4,128)S(1)} %get-tuple-element.42.weights_ref, s32[4]{0:T(128)S(4)} %get-tuple-element.43.counts_ref, f32[1,4096]{1,0:T(1,128)S(1)} %get-tuple-element.44.gain_ref, ...), custom_call_target="tpu_custom_call" | custom-call | bytes 8049999 | tf_op jit(solution)/shard_map/attend/pallas_call | solution.py:437
  5.9 3.7 %collective-permute-start = (bf16[16,1664]{1,0:T(8,128)(2,1)S(1)}, bf16[16,1664]{1,0:T(8,128)(2,1)S(1)}, u32[]{:S(2)}, u32[]{:S(2)}) collective-permute-start(bf16[16,1664]{1,0:T(8,128)(2,1)S(1)} %get-tuple-element.53), channel_id=1, source_target_pairs={{0,12},{2,14},{4,8},{6,10},{8,4},{10,6},{12,0},{14,2},{1,13},{3,15... | collective-permute-start | bytes 159752 | tf_op jit(solution)/shard_map/ppermute | solution.py:420
  9.5 0.0 collective-permute-start.1
  9.5 0.8 %collective-permute-start.2 = (bf16[16,1664]{1,0:T(8,128)(2,1)S(1)}, bf16[16,1664]{1,0:T(8,128)(2,1)S(1)}, u32[]{:S(2)}, u32[]{:S(2)}) collective-permute-start(bf16[16,1664]{1,0:T(8,128)(2,1)S(1)} %get-tuple-element.53), channel_id=1, source_target_pairs={{0,4},{2,6},{4,0},{6,2},{8,12},{10,14},{12,8},{14,10},{1,5},{3,7},... | collective-permute-start | bytes 159752 | tf_op jit(solution)/shard_map/ppermute | solution.py:420
  10.3 1.9 %gate.1 = (bf16[2,2048,384]{2,1,0:T(8,128)(2,1)S(1)}, f32[8,128]{1,0:T(8,128)S(1)}) custom-call(f32[16,1536]{1,0:T(8,128)S(1)} %get-tuple-element.52.after_ref.refs_0_, bf16[2,4096,384]{2,1,0:T(8,128)(2,1)} %refs_0_.3), custom_call_target="tpu_custom_call" | custom-call | bytes 7000000 | tf_op jit(solution)/shard_map/gate/pallas_call | solution.py:447
  12.2 0.3 collective-permute-done
  12.5 2.1 %collective-permute-done.1 = bf16[16,1664]{1,0:T(8,128)(2,1)S(1)} collective-permute-done((bf16[16,1664]{1,0:T(8,128)(2,1)S(1)}, bf16[16,1664]{1,0:T(8,128)(2,1)S(1)}, u32[]{:S(2)}, u32[]{:S(2)}) %collective-permute-start.1) | collective-permute-done | bytes 53280 | tf_op jit(solution)/shard_map/ppermute | solution.py:420
  14.6 0.0 collective-permute-done.2
  14.6 0.0 collective-permute-done.3.near_ref
  14.6 0.6 %collective-permute-start.4 = (bf16[64,1664]{1,0:T(8,128)(2,1)S(1)}, bf16[64,1664]{1,0:T(8,128)(2,1)S(1)}, u32[]{:S(2)}, u32[]{:S(2)}) collective-permute-start(bf16[64,1664]{1,0:T(8,128)(2,1)S(1)} %pad_maximum_fusion.after_ref.even_ref), channel_id=1, source_target_pairs={{0,2},{2,0},{4,6},{6,4},{8,10},{10,8},{12,14},{14,12},{1,3},{3,1},... | collective-permute-start | bytes 638984 | tf_op jit(solution)/shard_map/ppermute | solution.py:420
  15.2 0.0 collective-permute-start.5
  15.2 3.8 %rest.1 = (bf16[2,2048,384]{2,1,0:T(8,128)(2,1)S(1)}, bf16[2,2048,384]{2,1,0:T(8,128)(2,1)S(1)}, bf16[2,2048,384]{2,1,0:T(8,128)(2,1)S(1)}, f32[8,128]{1,0:T(8,128)S(1)}) custom-call(bf16[64,1664]{1,0:T(8,128)(2,1)S(1)} %pad_maximum_fusion.after_ref.even_ref, bf16[2,4096,384]{2,1,0:T(8,128)(2,1)} %refs_0_.3, bf16[2,4096,384]{2,1,0:T(8,128)(2,1)} %refs_2_.1, ...), custom_call_target="tpu_custom_call" | custom-call | bytes 7000000 | tf_op jit(solution)/shard_map/rest/pallas_call | solution.py:447
  19.0 1.5 %collective-permute-done.4.odd_ref = bf16[64,1664]{1,0:T(8,128)(2,1)S(1)} collective-permute-done((bf16[64,1664]{1,0:T(8,128)(2,1)S(1)}, bf16[64,1664]{1,0:T(8,128)(2,1)S(1)}, u32[]{:S(2)}, u32[]{:S(2)}) %collective-permute-start.4) | collective-permute-done | bytes 213024 | tf_op jit(solution)/shard_map/ppermute | solution.py:420
  20.5 0.0 collective-permute-start.6
  20.5 0.6 %collective-permute-start.8 = (bf16[800,128]{1,0:T(8,128)(2,1)S(1)}, bf16[800,128]{1,0:T(8,128)(2,1)S(1)}, u32[]{:S(2)}, u32[]{:S(2)}) collective-permute-start(bf16[800,128]{1,0:T(8,128)(2,1)S(1)} %get-tuple-element.68), channel_id=1, source_target_pairs={{0,2},{2,0},{4,6},{6,4},{8,10},{10,8},{12,14},{14,12},{1,3},{3,1},... | collective-permute-start | bytes 614408 | tf_op jit(solution)/shard_map/ppermute | solution.py:420
  21.1 0.0 slice-start
  21.1 1.3 %partial.1.partial_ref = f32[4,128,384]{2,1,0:T(8,128)S(1)} custom-call(f32[8,128]{1,0:T(8,128)S(1)} %get-tuple-element.56.after_ref, f32[8,128]{1,0:T(8,128)S(1)} %get-tuple-element.60.also_after_ref, bf16[64,1664]{1,0:T(8,128)(2,1)S(1)} %pad_maximum_fusion.after_ref.even_ref, bf16[64,1664]{1,0:T(8,128)(2,1)S(1)} %collective-permute-done.4.odd_ref, ...), custom_call_target="tpu_custom_call" | custom-call | bytes 35000 | tf_op jit(solution)/shard_map/partial/pallas_call | solution.py:464
  22.3 0.0 collective-permute-done.5.even_other_ref
  22.4 0.0 collective-permute-done.6.odd_other_ref
  22.4 0.0 slice-start.1
  22.4 1.4 %hidden.1.own_ref = bf16[128,768]{1,0:T(8,128)(2,1)S(1)} custom-call(f32[4,128,384]{2,1,0:T(8,128)S(1)} %partial.1.partial_ref, bf16[64,1664]{1,0:T(8,128)(2,1)S(1)} %pad_maximum_fusion.after_ref.even_ref, bf16[64,1664]{1,0:T(8,128)(2,1)S(1)} %collective-permute-done.4.odd_ref, bf16[64,1664]{1,0:T(8,128)(2,1)S(1)} %collective-permute-done.5.even_other_ref, ...), custom_call_target="tpu_custom_call" | custom-call | bytes 35000 | tf_op jit(solution)/shard_map/hidden/pallas_call | solution.py:467
  23.7 0.3 collective-permute-start.7
  24.0 1.2 %collective-permute-done.7.other_ref = bf16[128,768]{1,0:T(8,128)(2,1)S(1)} collective-permute-done((bf16[128,768]{1,0:T(8,128)(2,1)S(1)}, bf16[128,768]{1,0:T(8,128)(2,1)S(1)}, u32[]{:S(2)}, u32[]{:S(2)}) %collective-permute-start.7) | collective-permute-done | bytes 196640 | tf_op jit(solution)/shard_map/ppermute | solution.py:423
  25.3 0.0 slice-done
  25.3 0.0 slice-done.1
  25.3 1.3 %down.1 = (f32[64,1536]{1,0:T(8,128)S(1)}, bf16[64,1536]{1,0:T(8,128)(2,1)S(1)}) custom-call(bf16[128,768]{1,0:T(8,128)(2,1)S(1)} %hidden.1.own_ref, bf16[128,768]{1,0:T(8,128)(2,1)S(1)} %collective-permute-done.7.other_ref, bf16[2,768,2048]{2,1,0:T(8,128)(2,1)S(1)} %bitcast.22), custom_call_target="tpu_custom_call" | custom-call | bytes 35000 | tf_op jit(solution)/shard_map/down/pallas_call | solution.py:474
  26.5 1.5 %collective-permute-done.8.rest_ref = bf16[800,128]{1,0:T(8,128)(2,1)S(1)} collective-permute-done((bf16[800,128]{1,0:T(8,128)(2,1)S(1)}, bf16[800,128]{1,0:T(8,128)(2,1)S(1)}, u32[]{:S(2)}, u32[]{:S(2)}) %collective-permute-start.8) | collective-permute-done | bytes 204832 | tf_op jit(solution)/shard_map/ppermute | solution.py:420
  28.0 0.5 %collective-permute-start.9 = (bf16[64,1536]{1,0:T(8,128)(2,1)S(1)}, bf16[64,1536]{1,0:T(8,128)(2,1)S(1)}, u32[]{:S(2)}, u32[]{:S(2)}) collective-permute-start(bf16[64,1536]{1,0:T(8,128)(2,1)S(1)} %get-tuple-element.69), channel_id=1, source_target_pairs={{0,2},{2,0},{4,6},{6,4},{8,10},{10,8},{12,14},{14,12},{1,3},{3,1},... | collective-permute-start | bytes 589832 | tf_op jit(solution)/shard_map/ppermute | solution.py:420
  28.5 0.1 slice.101
  28.6 0.1 copy.18
  28.7 0.1 slice.103
  28.8 0.1 copy.19
  29.0 3.1 %collective-permute-start.10 = (bf16[1088,128]{1,0:T(8,128)(2,1)S(1)}, bf16[1088,128]{1,0:T(8,128)(2,1)S(1)}, u32[]{:S(2)}, u32[]{:S(2)}) collective-permute-start(bf16[1088,128]{1,0:T(8,128)(2,1)S(1)} %join.1), channel_id=1, source_target_pairs={{0,4},{4,8},{6,2},{8,12},{10,6},{12,14},{14,10},{1,5},{5,9},{7,3},... | collective-permute-start | bytes 835592 | tf_op jit(solution)/shard_map/ppermute | solution.py:481
  32.2 2.4 %collective-permute-done.9 = bf16[64,1536]{1,0:T(8,128)(2,1)S(1)} collective-permute-done((bf16[64,1536]{1,0:T(8,128)(2,1)S(1)}, bf16[64,1536]{1,0:T(8,128)(2,1)S(1)}, u32[]{:S(2)}, u32[]{:S(2)}) %collective-permute-start.9) | collective-permute-done | bytes 196640 | tf_op jit(solution)/shard_map/ppermute | solution.py:420
  34.6 2.6 %collective-permute-start.11 = (bf16[16,1536]{1,0:T(8,128)(2,1)S(1)}, bf16[16,1536]{1,0:T(8,128)(2,1)S(1)}, u32[]{:S(2)}, u32[]{:S(2)}) collective-permute-start(bf16[16,1536]{1,0:T(8,128)(2,1)S(1)} %get-tuple-element.81), channel_id=1, source_target_pairs={{0,12},{2,14},{4,8},{6,10},{8,4},{10,6},{12,0},{14,2},{1,13},{3,15... | collective-permute-start | bytes 147464 | tf_op jit(solution)/shard_map/ppermute | solution.py:420
  37.2 0.0 collective-permute-start.12
  37.2 1.8 %collective-permute-start.13 = (bf16[16,1536]{1,0:T(8,128)(2,1)S(1)}, bf16[16,1536]{1,0:T(8,128)(2,1)S(1)}, u32[]{:S(2)}, u32[]{:S(2)}) collective-permute-start(bf16[16,1536]{1,0:T(8,128)(2,1)S(1)} %get-tuple-element.79), channel_id=1, source_target_pairs={{0,4},{2,6},{4,0},{6,2},{8,12},{10,14},{12,8},{14,10},{1,5},{3,7},... | collective-permute-start | bytes 147464 | tf_op jit(solution)/shard_map/ppermute | solution.py:420
  39.1 0.1 collective-permute-done.10.relay_ref
  39.2 2.1 %resample.1 = (bf16[4,131,2,128]{3,2,1,0:T(2,128)(2,1)}, bf16[4,131,2,128]{3,2,1,0:T(2,128)(2,1)}) custom-call(s32[8,4]{1,0:T(8,128)S(1)} %stack.3.counts_ref, bf16[1312,128]{1,0:T(8,128)(2,1)S(1)} %collective-permute-done.3.near_ref, bf16[1088,128]{1,0:T(8,128)(2,1)S(1)} %collective-permute-done.10.relay_ref, ...), custom_call_target="tpu_custom_call" | custom-call | bytes 7700000 | tf_op jit(solution)/shard_map/resample/pallas_call | solution.py:488
  41.3 0.0 collective-permute-done.11.refs_3_
  41.3 0.9 %collective-permute-done.12.refs_4_ = bf16[16,1536]{1,0:T(8,128)(2,1)S(1)} collective-permute-done((bf16[16,1536]{1,0:T(8,128)(2,1)S(1)}, bf16[16,1536]{1,0:T(8,128)(2,1)S(1)}, u32[]{:S(2)}, u32[]{:S(2)}) %collective-permute-start.12) | collective-permute-done | bytes 49184 | tf_op jit(solution)/shard_map/ppermute | solution.py:420
  42.2 0.0 collective-permute-done.13.refs_5_
  42.3 0.1 collective-permute-start.14
  42.3 1.2 %collective-permute-done.14.other_ref = bf16[16,1536]{1,0:T(8,128)(2,1)S(1)} collective-permute-done((bf16[16,1536]{1,0:T(8,128)(2,1)S(1)}, bf16[16,1536]{1,0:T(8,128)(2,1)S(1)}, u32[]{:S(2)}, u32[]{:S(2)}) %collective-permute-start.14) | collective-permute-done | bytes 49184 | tf_op jit(solution)/shard_map/ppermute | solution.py:423
  43.6 0.7 %unpack.1 = bf16[3,4,4096]{2,1,0:T(4,128)(2,1)} custom-call(bf16[16,1536]{1,0:T(8,128)(2,1)S(1)} %total.1.own_ref, bf16[16,1536]{1,0:T(8,128)(2,1)S(1)} %collective-permute-done.14.other_ref), custom_call_target="tpu_custom_call" | custom-call | bytes 1750000 | tf_op jit(solution)/shard_map/unpack/pallas_call | solution.py:496
  (14 shorter events, 0.2 us)
Async XLA Ops:
  1.9 12.7 %collective-permute-start.3 = (bf16[1312,128]{1,0:T(8,128)(2,1)S(1)}, bf16[1312,128]{1,0:T(8,128)(2,1)S(1)}, u32[]{:S(2)}, u32[]{:S(2)}) collective-permute-start(bf16[1312,128]{1,0:T(8,128)(2,1)S(1)} %get-tuple-element.54), channel_id=1, source_target_pairs={{0,2},{2,0},{4,6},{6,4},{8,10},{10,8},{12,14},{14,12},{1,3},{3,1},... | collective-permute-start | bytes 1007624 | tf_op jit(solution)/shard_map/ppermute | solution.py:420
  5.9 6.6 %collective-permute-start = (bf16[16,1664]{1,0:T(8,128)(2,1)S(1)}, bf16[16,1664]{1,0:T(8,128)(2,1)S(1)}, u32[]{:S(2)}, u32[]{:S(2)}) collective-permute-start(bf16[16,1664]{1,0:T(8,128)(2,1)S(1)} %get-tuple-element.53), channel_id=1, source_target_pairs={{0,12},{2,14},{4,8},{6,10},{8,4},{10,6},{12,0},{14,2},{1,13},{3,15... | collective-permute-start | bytes 159752 | tf_op jit(solution)/shard_map/ppermute | solution.py:420
  9.5 5.0 %collective-permute-start.1 = (bf16[16,1664]{1,0:T(8,128)(2,1)S(1)}, bf16[16,1664]{1,0:T(8,128)(2,1)S(1)}, u32[]{:S(2)}, u32[]{:S(2)}) collective-permute-start(bf16[16,1664]{1,0:T(8,128)(2,1)S(1)} %get-tuple-element.53), channel_id=1, source_target_pairs={{0,8},{2,10},{4,12},{6,14},{8,0},{10,2},{12,4},{14,6},{1,9},{3,11}... | collective-permute-start | bytes 159752 | tf_op jit(solution)/shard_map/ppermute | solution.py:420
  9.5 5.0 %collective-permute-start.2 = (bf16[16,1664]{1,0:T(8,128)(2,1)S(1)}, bf16[16,1664]{1,0:T(8,128)(2,1)S(1)}, u32[]{:S(2)}, u32[]{:S(2)}) collective-permute-start(bf16[16,1664]{1,0:T(8,128)(2,1)S(1)} %get-tuple-element.53), channel_id=1, source_target_pairs={{0,4},{2,6},{4,0},{6,2},{8,12},{10,14},{12,8},{14,10},{1,5},{3,7},... | collective-permute-start | bytes 159752 | tf_op jit(solution)/shard_map/ppermute | solution.py:420
  14.6 5.9 %collective-permute-start.4 = (bf16[64,1664]{1,0:T(8,128)(2,1)S(1)}, bf16[64,1664]{1,0:T(8,128)(2,1)S(1)}, u32[]{:S(2)}, u32[]{:S(2)}) collective-permute-start(bf16[64,1664]{1,0:T(8,128)(2,1)S(1)} %pad_maximum_fusion.after_ref.even_ref), channel_id=1, source_target_pairs={{0,2},{2,0},{4,6},{6,4},{8,10},{10,8},{12,14},{14,12},{1,3},{3,1},... | collective-permute-start | bytes 638984 | tf_op jit(solution)/shard_map/ppermute | solution.py:420
  15.2 7.2 %collective-permute-start.5 = (bf16[64,1664]{1,0:T(8,128)(2,1)S(1)}, bf16[64,1664]{1,0:T(8,128)(2,1)S(1)}, u32[]{:S(2)}, u32[]{:S(2)}) collective-permute-start(bf16[64,1664]{1,0:T(8,128)(2,1)S(1)} %pad_maximum_fusion.after_ref.even_ref), channel_id=1, source_target_pairs={{0,1},{1,0},{2,3},{3,2},{4,5},{5,4},{6,7},{7,6},{8,9},{9,8},{10,11... | collective-permute-start | bytes 638984 | tf_op jit(solution)/shard_map/ppermute | solution.py:423
  20.5 1.9 %collective-permute-start.6 = (bf16[64,1664]{1,0:T(8,128)(2,1)S(1)}, bf16[64,1664]{1,0:T(8,128)(2,1)S(1)}, u32[]{:S(2)}, u32[]{:S(2)}) collective-permute-start(bf16[64,1664]{1,0:T(8,128)(2,1)S(1)} %collective-permute-done.4.odd_ref), channel_id=1, source_target_pairs={{0,1},{1,0},{2,3},{3,2},{4,5},{5,4},{6,7},{7,6},{8,9},{9,8},{10,11... | collective-permute-start | bytes 638984 | tf_op jit(solution)/shard_map/ppermute | solution.py:423
  20.5 7.5 %collective-permute-start.8 = (bf16[800,128]{1,0:T(8,128)(2,1)S(1)}, bf16[800,128]{1,0:T(8,128)(2,1)S(1)}, u32[]{:S(2)}, u32[]{:S(2)}) collective-permute-start(bf16[800,128]{1,0:T(8,128)(2,1)S(1)} %get-tuple-element.68), channel_id=1, source_target_pairs={{0,2},{2,0},{4,6},{6,4},{8,10},{10,8},{12,14},{14,12},{1,3},{3,1},... | collective-permute-start | bytes 614408 | tf_op jit(solution)/shard_map/ppermute | solution.py:420
  21.1 4.2 %slice-start = ((s8[6291456]{0:T(1024)(128)(4,1)}), s8[4194304]{0:T(1024)(128)(4,1)S(1)}, s32[]{:S(2)}) async-start(s8[6291456]{0:T(1024)(128)(4,1)} %bitcast.21), calls=%async_computation | async-start | bytes 8388608
  22.4 2.9 %slice-start.1 = ((s8[6291456]{0:T(1024)(128)(4,1)}), s8[2097152]{0:T(1024)(128)(4,1)S(1)}, s32[]{:S(2)}) async-start(s8[6291456]{0:T(1024)(128)(4,1)} %bitcast.21), calls=%async_computation.1 | async-start | bytes 4194304
  23.7 1.5 %collective-permute-start.7 = (bf16[128,768]{1,0:T(8,128)(2,1)S(1)}, bf16[128,768]{1,0:T(8,128)(2,1)S(1)}, u32[]{:S(2)}, u32[]{:S(2)}) collective-permute-start(bf16[128,768]{1,0:T(8,128)(2,1)S(1)} %hidden.1.own_ref), channel_id=1, source_target_pairs={{0,1},{1,0},{2,3},{3,2},{4,5},{5,4},{6,7},{7,6},{8,9},{9,8},{10,11... | collective-permute-start | bytes 589832 | tf_op jit(solution)/shard_map/ppermute | solution.py:423
  28.0 6.5 %collective-permute-start.9 = (bf16[64,1536]{1,0:T(8,128)(2,1)S(1)}, bf16[64,1536]{1,0:T(8,128)(2,1)S(1)}, u32[]{:S(2)}, u32[]{:S(2)}) collective-permute-start(bf16[64,1536]{1,0:T(8,128)(2,1)S(1)} %get-tuple-element.69), channel_id=1, source_target_pairs={{0,2},{2,0},{4,6},{6,4},{8,10},{10,8},{12,14},{14,12},{1,3},{3,1},... | collective-permute-start | bytes 589832 | tf_op jit(solution)/shard_map/ppermute | solution.py:420
  29.0 10.2 %collective-permute-start.10 = (bf16[1088,128]{1,0:T(8,128)(2,1)S(1)}, bf16[1088,128]{1,0:T(8,128)(2,1)S(1)}, u32[]{:S(2)}, u32[]{:S(2)}) collective-permute-start(bf16[1088,128]{1,0:T(8,128)(2,1)S(1)} %join.1), channel_id=1, source_target_pairs={{0,4},{4,8},{6,2},{8,12},{10,6},{12,14},{14,10},{1,5},{5,9},{7,3},... | collective-permute-start | bytes 835592 | tf_op jit(solution)/shard_map/ppermute | solution.py:481
  34.6 6.7 %collective-permute-start.11 = (bf16[16,1536]{1,0:T(8,128)(2,1)S(1)}, bf16[16,1536]{1,0:T(8,128)(2,1)S(1)}, u32[]{:S(2)}, u32[]{:S(2)}) collective-permute-start(bf16[16,1536]{1,0:T(8,128)(2,1)S(1)} %get-tuple-element.81), channel_id=1, source_target_pairs={{0,12},{2,14},{4,8},{6,10},{8,4},{10,6},{12,0},{14,2},{1,13},{3,15... | collective-permute-start | bytes 147464 | tf_op jit(solution)/shard_map/ppermute | solution.py:420
  37.2 5.0 %collective-permute-start.12 = (bf16[16,1536]{1,0:T(8,128)(2,1)S(1)}, bf16[16,1536]{1,0:T(8,128)(2,1)S(1)}, u32[]{:S(2)}, u32[]{:S(2)}) collective-permute-start(bf16[16,1536]{1,0:T(8,128)(2,1)S(1)} %get-tuple-element.80), channel_id=1, source_target_pairs={{0,8},{2,10},{4,12},{6,14},{8,0},{10,2},{12,4},{14,6},{1,9},{3,11}... | collective-permute-start | bytes 147464 | tf_op jit(solution)/shard_map/ppermute | solution.py:420
  37.2 5.0 %collective-permute-start.13 = (bf16[16,1536]{1,0:T(8,128)(2,1)S(1)}, bf16[16,1536]{1,0:T(8,128)(2,1)S(1)}, u32[]{:S(2)}, u32[]{:S(2)}) collective-permute-start(bf16[16,1536]{1,0:T(8,128)(2,1)S(1)} %get-tuple-element.79), channel_id=1, source_target_pairs={{0,4},{2,6},{4,0},{6,2},{8,12},{10,14},{12,8},{14,10},{1,5},{3,7},... | collective-permute-start | bytes 147464 | tf_op jit(solution)/shard_map/ppermute | solution.py:420
  42.3 1.3 %collective-permute-start.14 = (bf16[16,1536]{1,0:T(8,128)(2,1)S(1)}, bf16[16,1536]{1,0:T(8,128)(2,1)S(1)}, u32[]{:S(2)}, u32[]{:S(2)}) collective-permute-start(bf16[16,1536]{1,0:T(8,128)(2,1)S(1)} %total.1.own_ref), channel_id=1, source_target_pairs={{0,1},{1,0},{2,3},{3,2},{4,5},{5,4},{6,7},{7,6},{8,9},{9,8},{10,11... | collective-permute-start | bytes 147464 | tf_op jit(solution)/shard_map/ppermute | solution.py:423

commit v8 on v6

--- a/solution.py
+++ b/solution.py
@@ -50,7 +50,7 @@
         copy.start()
     tokens, kv_heads, cached, width = ck_ref.shape
     chosen_ref[...] = packing(steps, tokens, q_ref.shape[2])
-    for copy in copies:
+    for copy in copies[:4]:
         copy.wait()
 
     odd = lax.rem(lax.axis_index("expert"), 2)
@@ -84,6 +84,9 @@
     @pl.when(odd == 1)
     def _():
         fill(0, tail)
+
+    for copy in copies[4:]:
+        copy.wait()
 
 
 def weight_kernel(after_ref, source, own_ref, other_ref, token_ref, sems):

time: 44.8 us -> 44.8 us (level)
  no operation moved by 1% of the time
where the time goes in v8:
time: 44.8 us; the launch traced here: 44.1 us
  starting transfers between devices  17.1 us (38%)
  Pallas kernels  14.5 us (32%)
  waiting for transfers between devices  11.2 us (25%)
  between operations  0.81 us (2%)
  local copies, waits for them, and re-layouts  0.5 us (1%)
    ppermute x10, starting transfers between devices, swap(): lax.ppermute(value, 'expert', [(i, i ^ offset) for i in range(count)])  13.6 us
    ppermute x10, waiting for transfers between devices, swap(): lax.ppermute(value, 'expert', [(i, i ^ offset) for i in range(count)])  8.63 us
    pallas_call x2, Pallas kernels, fetch(): pl.pallas_call(weight_kernel, out_shape=[half, half, pltpu.VMEM((8, LANES...  5.73 us
    ppermute x1, starting transfers between devices, fast_shards(): lax.ppermute(call(join_kernel, joined, [VMEM] * 2, 'join', 0.1)(near, rel...  3.13 us
    ppermute x4, waiting for transfers between devices, sibling(): return lax.ppermute(value, 'tensor', [(0, 1), (1, 0)])  2.44 us
    pallas_call x1, Pallas kernels, fast_shards(): call(functools.partial(resample_kernel, steps, early), (out, out), [SMEM]...  2.06 us
    pallas_call x1, Pallas kernels, fast_shards(): call(functools.partial(hidden_kernel, steps, tokens, experts), struct((co...  1.32 us
    pallas_call x1, Pallas kernels, fast_shards(): call(functools.partial(partial_kernel, steps, tokens), struct((2 * local,...  1.27 us
  transfers between devices with their start and end apart: 15, of which 8 were waited for; matrix products, arithmetic and copies ran while one was open for 1% of the time, Pallas kernels for 29%

profile of v8, /device:TPU:0, one launch (start us, length us, event | category | flops | bytes accessed | tf_op | source)
XLA Modules:
  0.0 44.1 jit_solution(7027008564247513269)
XLA Ops:
  0.6 1.2 %load.1 = (s32[3,4,8]{2,1,0:T(4,128)S(1)}, f32[3,4,8]{2,1,0:T(4,128)S(1)}, s32[4]{0:T(128)S(4)}, f32[1,4096]{1,0:T(1,128)S(1)}, bf16[3,4,4096]{2,1,0:T(4,128)(2,...) custom-call(s32[3,4,8]{2,1,0:T(4,128)} %ids_in.1, ...), custom_call_target="tpu_custom_call" | custom-call | tf_op jit(solution)/shard_map/load/pallas_call | solution.py:428
  1.8 3.0 %collective-permute-start.3 = (bf16[1312,128]{1,0:T(8,128)(2,1)S(1)}, bf16[1312,128]{1,0:T(8,128)(2,1)S(1)}, u32[]{:S(2)}, u32[]{:S(2)}) collective-permute-start(bf16[1312,128]{1,0:T(8,128)(2,1)S(1)} %get-tuple-element.54), channel_id=1, source_target_pairs={{0,2},{2,0},{4,6},{6,4},{8,10},{10,8},{12,14},{14,12},{1,3},{3,1},... | collective-permute-start | bytes 1007624 | tf_op jit(solution)/shard_map/ppermute | solution.py:421
  4.9 0.9 %attend.1 = (bf16[16,1664]{1,0:T(8,128)(2,1)S(1)}, f32[16,1536]{1,0:T(8,128)S(1)}) custom-call(s32[3,4,8]{2,1,0:T(4,128)S(1)} %get-tuple-element.41.ids_ref, f32[3,4,8]{2,1,0:T(4,128)S(1)} %get-tuple-element.42.weights_ref, s32[4]{0:T(128)S(4)} %get-tuple-element.43.counts_ref, f32[1,4096]{1,0:T(1,128)S(1)} %get-tuple-element.44.gain_ref, ...), custom_call_target="tpu_custom_call" | custom-call | bytes 8049999 | tf_op jit(solution)/shard_map/attend/pallas_call | solution.py:438
  5.8 3.7 %collective-permute-start = (bf16[16,1664]{1,0:T(8,128)(2,1)S(1)}, bf16[16,1664]{1,0:T(8,128)(2,1)S(1)}, u32[]{:S(2)}, u32[]{:S(2)}) collective-permute-start(bf16[16,1664]{1,0:T(8,128)(2,1)S(1)} %get-tuple-element.53), channel_id=1, source_target_pairs={{0,12},{2,14},{4,8},{6,10},{8,4},{10,6},{12,0},{14,2},{1,13},{3,15... | collective-permute-start | bytes 159752 | tf_op jit(solution)/shard_map/ppermute | solution.py:421
  9.4 0.0 collective-permute-start.1
  9.5 0.8 %collective-permute-start.2 = (bf16[16,1664]{1,0:T(8,128)(2,1)S(1)}, bf16[16,1664]{1,0:T(8,128)(2,1)S(1)}, u32[]{:S(2)}, u32[]{:S(2)}) collective-permute-start(bf16[16,1664]{1,0:T(8,128)(2,1)S(1)} %get-tuple-element.53), channel_id=1, source_target_pairs={{0,4},{2,6},{4,0},{6,2},{8,12},{10,14},{12,8},{14,10},{1,5},{3,7},... | collective-permute-start | bytes 159752 | tf_op jit(solution)/shard_map/ppermute | solution.py:421
  10.2 2.9 %gate.1 = (bf16[2,2048,384]{2,1,0:T(8,128)(2,1)S(1)}, bf16[2,2048,384]{2,1,0:T(8,128)(2,1)S(1)}, f32[8,128]{1,0:T(8,128)S(1)}) custom-call(f32[16,1536]{1,0:T(8,128)S(1)} %get-tuple-element.52.after_ref.refs_0_, bf16[2,4096,384]{2,1,0:T(8,128)(2,1)} %source.2), custom_call_target="tpu_custom_call" | custom-call | bytes 7000000 | tf_op jit(solution)/shard_map/gate/pallas_call | solution.py:447
  13.1 0.0 collective-permute-done
  13.1 1.4 %collective-permute-done.1 = bf16[16,1664]{1,0:T(8,128)(2,1)S(1)} collective-permute-done((bf16[16,1664]{1,0:T(8,128)(2,1)S(1)}, bf16[16,1664]{1,0:T(8,128)(2,1)S(1)}, u32[]{:S(2)}, u32[]{:S(2)}) %collective-permute-start.1) | collective-permute-done | bytes 53280 | tf_op jit(solution)/shard_map/ppermute | solution.py:421
  14.5 0.0 collective-permute-done.2
  14.5 0.0 collective-permute-done.3.near_ref
  14.5 0.6 %collective-permute-start.4 = (bf16[64,1664]{1,0:T(8,128)(2,1)S(1)}, bf16[64,1664]{1,0:T(8,128)(2,1)S(1)}, u32[]{:S(2)}, u32[]{:S(2)}) collective-permute-start(bf16[64,1664]{1,0:T(8,128)(2,1)S(1)} %pad_maximum_fusion.after_ref.even_ref), channel_id=1, source_target_pairs={{0,2},{2,0},{4,6},{6,4},{8,10},{10,8},{12,14},{14,12},{1,3},{3,1},... | collective-permute-start | bytes 638984 | tf_op jit(solution)/shard_map/ppermute | solution.py:421
  15.1 0.0 collective-permute-start.5
  15.1 2.9 %up.1 = (bf16[2,2048,384]{2,1,0:T(8,128)(2,1)S(1)}, bf16[2,2048,384]{2,1,0:T(8,128)(2,1)S(1)}, f32[8,128]{1,0:T(8,128)S(1)}) custom-call(bf16[64,1664]{1,0:T(8,128)(2,1)S(1)} %pad_maximum_fusion.after_ref.even_ref, bf16[2,4096,384]{2,1,0:T(8,128)(2,1)} %source.3), custom_call_target="tpu_custom_call" | custom-call | bytes 7000000 | tf_op jit(solution)/shard_map/up/pallas_call | solution.py:447
  18.0 2.4 %collective-permute-done.4.odd_ref = bf16[64,1664]{1,0:T(8,128)(2,1)S(1)} collective-permute-done((bf16[64,1664]{1,0:T(8,128)(2,1)S(1)}, bf16[64,1664]{1,0:T(8,128)(2,1)S(1)}, u32[]{:S(2)}, u32[]{:S(2)}) %collective-permute-start.4) | collective-permute-done | bytes 213024 | tf_op jit(solution)/shard_map/ppermute | solution.py:421
  20.4 0.0 collective-permute-start.6
  20.4 0.5 %collective-permute-start.8 = (bf16[800,128]{1,0:T(8,128)(2,1)S(1)}, bf16[800,128]{1,0:T(8,128)(2,1)S(1)}, u32[]{:S(2)}, u32[]{:S(2)}) collective-permute-start(bf16[800,128]{1,0:T(8,128)(2,1)S(1)} %get-tuple-element.68), channel_id=1, source_target_pairs={{0,2},{2,0},{4,6},{6,4},{8,10},{10,8},{12,14},{14,12},{1,3},{3,1},... | collective-permute-start | bytes 614408 | tf_op jit(solution)/shard_map/ppermute | solution.py:421
  21.0 0.0 slice-start
  21.0 1.3 %partial.1.partial_ref = f32[4,128,384]{2,1,0:T(8,128)S(1)} custom-call(f32[8,128]{1,0:T(8,128)S(1)} %get-tuple-element.56.after_ref, f32[8,128]{1,0:T(8,128)S(1)} %get-tuple-element.60.also_after_ref, bf16[64,1664]{1,0:T(8,128)(2,1)S(1)} %pad_maximum_fusion.after_ref.even_ref, bf16[64,1664]{1,0:T(8,128)(2,1)S(1)} %collective-permute-done.4.odd_ref, ...), custom_call_target="tpu_custom_call" | custom-call | bytes 35000 | tf_op jit(solution)/shard_map/partial/pallas_call | solution.py:463
  22.2 0.0 collective-permute-done.5.even_other_ref
  22.3 0.0 collective-permute-done.6.odd_other_ref
  22.3 0.0 slice-start.1
  22.3 1.3 %hidden.1.own_ref = bf16[128,768]{1,0:T(8,128)(2,1)S(1)} custom-call(f32[4,128,384]{2,1,0:T(8,128)S(1)} %partial.1.partial_ref, bf16[64,1664]{1,0:T(8,128)(2,1)S(1)} %pad_maximum_fusion.after_ref.even_ref, bf16[64,1664]{1,0:T(8,128)(2,1)S(1)} %collective-permute-done.4.odd_ref, bf16[64,1664]{1,0:T(8,128)(2,1)S(1)} %collective-permute-done.5.even_other_ref, ...), custom_call_target="tpu_custom_call" | custom-call | bytes 35000 | tf_op jit(solution)/shard_map/hidden/pallas_call | solution.py:466
  23.6 0.3 collective-permute-start.7
  23.9 1.2 %collective-permute-done.7.other_ref = bf16[128,768]{1,0:T(8,128)(2,1)S(1)} collective-permute-done((bf16[128,768]{1,0:T(8,128)(2,1)S(1)}, bf16[128,768]{1,0:T(8,128)(2,1)S(1)}, u32[]{:S(2)}, u32[]{:S(2)}) %collective-permute-start.7) | collective-permute-done | bytes 196640 | tf_op jit(solution)/shard_map/ppermute | solution.py:424
  25.1 0.0 slice-done
  25.1 0.0 slice-done.1
  25.1 1.3 %down.1 = (f32[64,1536]{1,0:T(8,128)S(1)}, bf16[64,1536]{1,0:T(8,128)(2,1)S(1)}) custom-call(bf16[128,768]{1,0:T(8,128)(2,1)S(1)} %hidden.1.own_ref, bf16[128,768]{1,0:T(8,128)(2,1)S(1)} %collective-permute-done.7.other_ref, bf16[2,768,2048]{2,1,0:T(8,128)(2,1)S(1)} %bitcast.22), custom_call_target="tpu_custom_call" | custom-call | bytes 35000 | tf_op jit(solution)/shard_map/down/pallas_call | solution.py:473
  26.4 1.5 %collective-permute-done.8.rest_ref = bf16[800,128]{1,0:T(8,128)(2,1)S(1)} collective-permute-done((bf16[800,128]{1,0:T(8,128)(2,1)S(1)}, bf16[800,128]{1,0:T(8,128)(2,1)S(1)}, u32[]{:S(2)}, u32[]{:S(2)}) %collective-permute-start.8) | collective-permute-done | bytes 204832 | tf_op jit(solution)/shard_map/ppermute | solution.py:421
  27.9 0.5 %collective-permute-start.9 = (bf16[64,1536]{1,0:T(8,128)(2,1)S(1)}, bf16[64,1536]{1,0:T(8,128)(2,1)S(1)}, u32[]{:S(2)}, u32[]{:S(2)}) collective-permute-start(bf16[64,1536]{1,0:T(8,128)(2,1)S(1)} %get-tuple-element.69), channel_id=1, source_target_pairs={{0,2},{2,0},{4,6},{6,4},{8,10},{10,8},{12,14},{14,12},{1,3},{3,1},... | collective-permute-start | bytes 589832 | tf_op jit(solution)/shard_map/ppermute | solution.py:421
  28.5 0.1 slice.101
  28.5 0.1 copy.18
  28.7 0.1 slice.103
  28.7 0.1 copy.19
  28.9 3.1 %collective-permute-start.10 = (bf16[1088,128]{1,0:T(8,128)(2,1)S(1)}, bf16[1088,128]{1,0:T(8,128)(2,1)S(1)}, u32[]{:S(2)}, u32[]{:S(2)}) collective-permute-start(bf16[1088,128]{1,0:T(8,128)(2,1)S(1)} %join.1), channel_id=1, source_target_pairs={{0,4},{4,8},{6,2},{8,12},{10,6},{14,10},{1,5},{5,9},{7,3},{9,13},{... | collective-permute-start | bytes 835592 | tf_op jit(solution)/shard_map/ppermute | solution.py:480
  32.1 2.4 %collective-permute-done.9 = bf16[64,1536]{1,0:T(8,128)(2,1)S(1)} collective-permute-done((bf16[64,1536]{1,0:T(8,128)(2,1)S(1)}, bf16[64,1536]{1,0:T(8,128)(2,1)S(1)}, u32[]{:S(2)}, u32[]{:S(2)}) %collective-permute-start.9) | collective-permute-done | bytes 196640 | tf_op jit(solution)/shard_map/ppermute | solution.py:421
  34.5 2.4 %collective-permute-start.11 = (bf16[16,1536]{1,0:T(8,128)(2,1)S(1)}, bf16[16,1536]{1,0:T(8,128)(2,1)S(1)}, u32[]{:S(2)}, u32[]{:S(2)}) collective-permute-start(bf16[16,1536]{1,0:T(8,128)(2,1)S(1)} %get-tuple-element.81), channel_id=1, source_target_pairs={{0,12},{2,14},{4,8},{6,10},{8,4},{10,6},{12,0},{14,2},{1,13},{3,15... | collective-permute-start | bytes 147464 | tf_op jit(solution)/shard_map/ppermute | solution.py:421
  36.9 0.0 collective-permute-start.12
  36.9 2.1 %collective-permute-start.13 = (bf16[16,1536]{1,0:T(8,128)(2,1)S(1)}, bf16[16,1536]{1,0:T(8,128)(2,1)S(1)}, u32[]{:S(2)}, u32[]{:S(2)}) collective-permute-start(bf16[16,1536]{1,0:T(8,128)(2,1)S(1)} %get-tuple-element.79), channel_id=1, source_target_pairs={{0,4},{2,6},{4,0},{6,2},{8,12},{10,14},{12,8},{14,10},{1,5},{3,7},... | collective-permute-start | bytes 147464 | tf_op jit(solution)/shard_map/ppermute | solution.py:421
  39.0 0.1 collective-permute-done.10.relay_ref
  39.2 2.1 %resample.1 = (bf16[4,131,2,128]{3,2,1,0:T(2,128)(2,1)}, bf16[4,131,2,128]{3,2,1,0:T(2,128)(2,1)}) custom-call(s32[8,4]{1,0:T(8,128)S(1)} %stack.3.counts_ref, bf16[1312,128]{1,0:T(8,128)(2,1)S(1)} %collective-permute-done.3.near_ref, bf16[1088,128]{1,0:T(8,128)(2,1)S(1)} %collective-permute-done.10.relay_ref, ...), custom_call_target="tpu_custom_call" | custom-call | bytes 7700000 | tf_op jit(solution)/shard_map/resample/pallas_call | solution.py:487
  41.2 0.0 collective-permute-done.11.refs_3_
  41.2 0.9 %collective-permute-done.12.refs_4_ = bf16[16,1536]{1,0:T(8,128)(2,1)S(1)} collective-permute-done((bf16[16,1536]{1,0:T(8,128)(2,1)S(1)}, bf16[16,1536]{1,0:T(8,128)(2,1)S(1)}, u32[]{:S(2)}, u32[]{:S(2)}) %collective-permute-start.12) | collective-permute-done | bytes 49184 | tf_op jit(solution)/shard_map/ppermute | solution.py:421
  42.1 0.0 collective-permute-done.13.refs_5_
  42.2 0.1 collective-permute-start.14
  42.3 1.2 %collective-permute-done.14.other_ref = bf16[16,1536]{1,0:T(8,128)(2,1)S(1)} collective-permute-done((bf16[16,1536]{1,0:T(8,128)(2,1)S(1)}, bf16[16,1536]{1,0:T(8,128)(2,1)S(1)}, u32[]{:S(2)}, u32[]{:S(2)}) %collective-permute-start.14) | collective-permute-done | bytes 49184 | tf_op jit(solution)/shard_map/ppermute | solution.py:424
  43.5 0.7 %unpack.1 = bf16[3,4,4096]{2,1,0:T(4,128)(2,1)} custom-call(bf16[16,1536]{1,0:T(8,128)(2,1)S(1)} %total.1.own_ref, bf16[16,1536]{1,0:T(8,128)(2,1)S(1)} %collective-permute-done.14.other_ref), custom_call_target="tpu_custom_call" | custom-call | bytes 1750000 | tf_op jit(solution)/shard_map/unpack/pallas_call | solution.py:495
  (14 shorter events, 0.2 us)
Async XLA Ops:
  1.8 12.7 %collective-permute-start.3 = (bf16[1312,128]{1,0:T(8,128)(2,1)S(1)}, bf16[1312,128]{1,0:T(8,128)(2,1)S(1)}, u32[]{:S(2)}, u32[]{:S(2)}) collective-permute-start(bf16[1312,128]{1,0:T(8,128)(2,1)S(1)} %get-tuple-element.54), channel_id=1, source_target_pairs={{0,2},{2,0},{4,6},{6,4},{8,10},{10,8},{12,14},{14,12},{1,3},{3,1},... | collective-permute-start | bytes 1007624 | tf_op jit(solution)/shard_map/ppermute | solution.py:421
  5.8 7.3 %collective-permute-start = (bf16[16,1664]{1,0:T(8,128)(2,1)S(1)}, bf16[16,1664]{1,0:T(8,128)(2,1)S(1)}, u32[]{:S(2)}, u32[]{:S(2)}) collective-permute-start(bf16[16,1664]{1,0:T(8,128)(2,1)S(1)} %get-tuple-element.53), channel_id=1, source_target_pairs={{0,12},{2,14},{4,8},{6,10},{8,4},{10,6},{12,0},{14,2},{1,13},{3,15... | collective-permute-start | bytes 159752 | tf_op jit(solution)/shard_map/ppermute | solution.py:421
  9.4 5.0 %collective-permute-start.1 = (bf16[16,1664]{1,0:T(8,128)(2,1)S(1)}, bf16[16,1664]{1,0:T(8,128)(2,1)S(1)}, u32[]{:S(2)}, u32[]{:S(2)}) collective-permute-start(bf16[16,1664]{1,0:T(8,128)(2,1)S(1)} %get-tuple-element.53), channel_id=1, source_target_pairs={{0,8},{2,10},{4,12},{6,14},{8,0},{10,2},{12,4},{14,6},{1,9},{3,11}... | collective-permute-start | bytes 159752 | tf_op jit(solution)/shard_map/ppermute | solution.py:421
  9.5 5.0 %collective-permute-start.2 = (bf16[16,1664]{1,0:T(8,128)(2,1)S(1)}, bf16[16,1664]{1,0:T(8,128)(2,1)S(1)}, u32[]{:S(2)}, u32[]{:S(2)}) collective-permute-start(bf16[16,1664]{1,0:T(8,128)(2,1)S(1)} %get-tuple-element.53), channel_id=1, source_target_pairs={{0,4},{2,6},{4,0},{6,2},{8,12},{10,14},{12,8},{14,10},{1,5},{3,7},... | collective-permute-start | bytes 159752 | tf_op jit(solution)/shard_map/ppermute | solution.py:421
  14.5 5.9 %collective-permute-start.4 = (bf16[64,1664]{1,0:T(8,128)(2,1)S(1)}, bf16[64,1664]{1,0:T(8,128)(2,1)S(1)}, u32[]{:S(2)}, u32[]{:S(2)}) collective-permute-start(bf16[64,1664]{1,0:T(8,128)(2,1)S(1)} %pad_maximum_fusion.after_ref.even_ref), channel_id=1, source_target_pairs={{0,2},{2,0},{4,6},{6,4},{8,10},{10,8},{12,14},{14,12},{1,3},{3,1},... | collective-permute-start | bytes 638984 | tf_op jit(solution)/shard_map/ppermute | solution.py:421
  15.1 7.1 %collective-permute-start.5 = (bf16[64,1664]{1,0:T(8,128)(2,1)S(1)}, bf16[64,1664]{1,0:T(8,128)(2,1)S(1)}, u32[]{:S(2)}, u32[]{:S(2)}) collective-permute-start(bf16[64,1664]{1,0:T(8,128)(2,1)S(1)} %pad_maximum_fusion.after_ref.even_ref), channel_id=1, source_target_pairs={{0,1},{1,0},{2,3},{3,2},{4,5},{5,4},{6,7},{7,6},{8,9},{9,8},{10,11... | collective-permute-start | bytes 638984 | tf_op jit(solution)/shard_map/ppermute | solution.py:424
  20.4 1.8 %collective-permute-start.6 = (bf16[64,1664]{1,0:T(8,128)(2,1)S(1)}, bf16[64,1664]{1,0:T(8,128)(2,1)S(1)}, u32[]{:S(2)}, u32[]{:S(2)}) collective-permute-start(bf16[64,1664]{1,0:T(8,128)(2,1)S(1)} %collective-permute-done.4.odd_ref), channel_id=1, source_target_pairs={{0,1},{1,0},{2,3},{3,2},{4,5},{5,4},{6,7},{7,6},{8,9},{9,8},{10,11... | collective-permute-start | bytes 638984 | tf_op jit(solution)/shard_map/ppermute | solution.py:424
  20.4 7.5 %collective-permute-start.8 = (bf16[800,128]{1,0:T(8,128)(2,1)S(1)}, bf16[800,128]{1,0:T(8,128)(2,1)S(1)}, u32[]{:S(2)}, u32[]{:S(2)}) collective-permute-start(bf16[800,128]{1,0:T(8,128)(2,1)S(1)} %get-tuple-element.68), channel_id=1, source_target_pairs={{0,2},{2,0},{4,6},{6,4},{8,10},{10,8},{12,14},{14,12},{1,3},{3,1},... | collective-permute-start | bytes 614408 | tf_op jit(solution)/shard_map/ppermute | solution.py:421
  21.0 4.2 %slice-start = ((s8[6291456]{0:T(1024)(128)(4,1)}), s8[4194304]{0:T(1024)(128)(4,1)S(1)}, s32[]{:S(2)}) async-start(s8[6291456]{0:T(1024)(128)(4,1)} %bitcast.21), calls=%async_computation | async-start | bytes 8388608
  22.3 2.9 %slice-start.1 = ((s8[6291456]{0:T(1024)(128)(4,1)}), s8[2097152]{0:T(1024)(128)(4,1)S(1)}, s32[]{:S(2)}) async-start(s8[6291456]{0:T(1024)(128)(4,1)} %bitcast.21), calls=%async_computation.1 | async-start | bytes 4194304
  23.6 1.5 %collective-permute-start.7 = (bf16[128,768]{1,0:T(8,128)(2,1)S(1)}, bf16[128,768]{1,0:T(8,128)(2,1)S(1)}, u32[]{:S(2)}, u32[]{:S(2)}) collective-permute-start(bf16[128,768]{1,0:T(8,128)(2,1)S(1)} %hidden.1.own_ref), channel_id=1, source_target_pairs={{0,1},{1,0},{2,3},{3,2},{4,5},{5,4},{6,7},{7,6},{8,9},{9,8},{10,11... | collective-permute-start | bytes 589832 | tf_op jit(solution)/shard_map/ppermute | solution.py:424
  27.9 6.5 %collective-permute-start.9 = (bf16[64,1536]{1,0:T(8,128)(2,1)S(1)}, bf16[64,1536]{1,0:T(8,128)(2,1)S(1)}, u32[]{:S(2)}, u32[]{:S(2)}) collective-permute-start(bf16[64,1536]{1,0:T(8,128)(2,1)S(1)} %get-tuple-element.69), channel_id=1, source_target_pairs={{0,2},{2,0},{4,6},{6,4},{8,10},{10,8},{12,14},{14,12},{1,3},{3,1},... | collective-permute-start | bytes 589832 | tf_op jit(solution)/shard_map/ppermute | solution.py:421
  28.9 10.2 %collective-permute-start.10 = (bf16[1088,128]{1,0:T(8,128)(2,1)S(1)}, bf16[1088,128]{1,0:T(8,128)(2,1)S(1)}, u32[]{:S(2)}, u32[]{:S(2)}) collective-permute-start(bf16[1088,128]{1,0:T(8,128)(2,1)S(1)} %join.1), channel_id=1, source_target_pairs={{0,4},{4,8},{6,2},{8,12},{10,6},{14,10},{1,5},{5,9},{7,3},{9,13},{... | collective-permute-start | bytes 835592 | tf_op jit(solution)/shard_map/ppermute | solution.py:480
  34.5 6.7 %collective-permute-start.11 = (bf16[16,1536]{1,0:T(8,128)(2,1)S(1)}, bf16[16,1536]{1,0:T(8,128)(2,1)S(1)}, u32[]{:S(2)}, u32[]{:S(2)}) collective-permute-start(bf16[16,1536]{1,0:T(8,128)(2,1)S(1)} %get-tuple-element.81), channel_id=1, source_target_pairs={{0,12},{2,14},{4,8},{6,10},{8,4},{10,6},{12,0},{14,2},{1,13},{3,15... | collective-permute-start | bytes 147464 | tf_op jit(solution)/shard_map/ppermute | solution.py:421
  36.9 5.3 %collective-permute-start.12 = (bf16[16,1536]{1,0:T(8,128)(2,1)S(1)}, bf16[16,1536]{1,0:T(8,128)(2,1)S(1)}, u32[]{:S(2)}, u32[]{:S(2)}) collective-permute-start(bf16[16,1536]{1,0:T(8,128)(2,1)S(1)} %get-tuple-element.80), channel_id=1, source_target_pairs={{0,8},{2,10},{4,12},{6,14},{8,0},{10,2},{12,4},{14,6},{1,9},{3,11}... | collective-permute-start | bytes 147464 | tf_op jit(solution)/shard_map/ppermute | solution.py:421
  36.9 5.3 %collective-permute-start.13 = (bf16[16,1536]{1,0:T(8,128)(2,1)S(1)}, bf16[16,1536]{1,0:T(8,128)(2,1)S(1)}, u32[]{:S(2)}, u32[]{:S(2)}) collective-permute-start(bf16[16,1536]{1,0:T(8,128)(2,1)S(1)} %get-tuple-element.79), channel_id=1, source_target_pairs={{0,4},{2,6},{4,0},{6,2},{8,12},{10,14},{12,8},{14,10},{1,5},{3,7},... | collective-permute-start | bytes 147464 | tf_op jit(solution)/shard_map/ppermute | solution.py:421
  42.2 1.3 %collective-permute-start.14 = (bf16[16,1536]{1,0:T(8,128)(2,1)S(1)}, bf16[16,1536]{1,0:T(8,128)(2,1)S(1)}, u32[]{:S(2)}, u32[]{:S(2)}) collective-permute-start(bf16[16,1536]{1,0:T(8,128)(2,1)S(1)} %total.1.own_ref), channel_id=1, source_target_pairs={{0,1},{1,0},{2,3},{3,2},{4,5},{5,4},{6,7},{7,6},{8,9},{9,8},{10,11... | collective-permute-start | bytes 147464 | tf_op jit(solution)/shard_map/ppermute | solution.py:424
